TPU v7x, 256 devices: a whole 4x4x8 slice. The times are simulated.
256 devices in a mesh: shard: 16 (over x_lo, z), dp: 8 (over y, x_hi), buffer: 2 (over core).
Axes of the slice: x: 4 (x_hi: 2, x_lo: 2; x = x_hi * 2 + x_lo), y: 4, z: 8, core: 2. Of those that a mesh axis runs over, the one named last changes fastest.
Arguments:
- query_grad: bfloat16 [4, 128, 14336], P(None, None, 'dp'), may hold values from -6 to 6
- query_act: bfloat16 [4, 128, 8192], P(None, 'dp', 'shard'), may hold values from -6 to 6
- buffer_grad: bfloat16 [8, 128, 14336], P('buffer', None, 'dp'), may hold values from -6 to 6
- buffer_act: bfloat16 [8, 128, 8192], P('buffer', 'dp', 'shard'), may hold values from -6 to 6
- grad_basis: bfloat16 [14336, 14336], P('shard', 'dp'), may hold values from -0.046875 to 0.046875
- act_basis: bfloat16 [8192, 8192], P('dp', 'shard'), may hold values from -0.0625 to 0.0625
- eigenvalues: float32 [14336, 8192], P('shard', 'dp'), may hold values from 0.01 to 10
Outputs:
- scores: float32 [4, 8], P(None, 'buffer')
All inputs are finite; a program needn't handle non-finite values.
Results may differ from a plain program's by a relative error of at most 0.033.
Values may be sent and summed in bfloat16 or wider, within the bound.
No kernel may reach another device: no remote copies, remote signals or barrier semaphores. Data moves between devices by JAX's collectives and lax.ppermute only.
A program may use at most 128 MiB of HBM per device.

v0:
```python
import jax
import jax.numpy as jnp
from jax import lax
from jax.sharding import PartitionSpec as P

PH = 14336
Q = 8192
T_SIZE = 128


DAMPING = 0.1


def local(query_grad, query_act, buffer_grad, buffer_act, grad_basis, act_basis, eigenvalues):
    count_q = query_grad.shape[0]
    count_b = buffer_grad.shape[0]
    seq = query_grad.shape[1]
    examples = count_q + count_b
    total_rows = examples * seq
    grads = jnp.concatenate([query_grad, buffer_grad], 0).reshape(total_rows, query_grad.shape[2])
    grad_part = lax.dot_general(
        grads, grad_basis, (((1,), (1,)), ((), ())), preferred_element_type=jnp.float32
    )
    rotated_grad = lax.psum(grad_part.astype(jnp.bfloat16), "dp")
    query_full, buffer_full = (
        lax.all_gather(query_act, "dp", axis=1, tiled=True),
        lax.all_gather(buffer_act, "dp", axis=1, tiled=True),
    )
    acts = jnp.concatenate([query_full, buffer_full], 0).reshape(total_rows, query_act.shape[2])
    act_part = lax.dot_general(
        acts, act_basis, (((1,), (1,)), ((), ())), preferred_element_type=jnp.float32
    )
    rotated_act = lax.psum(act_part.astype(jnp.bfloat16), "shard")
    all_examples = count_q + count_b
    grad_rows = rotated_grad.reshape(all_examples, seq, rotated_grad.shape[1])
    act_rows = rotated_act.reshape(all_examples, seq, rotated_act.shape[1])
    tiles = jnp.einsum("nte,ntq->neq", grad_rows, act_rows, preferred_element_type=jnp.float32)
    scaled = tiles[:count_q] / (eigenvalues + DAMPING)
    buffer_tiles = tiles[count_q:].reshape(count_b, -1)
    local_scores = jnp.dot(
        scaled.reshape(count_q, -1), buffer_tiles.T, precision=lax.Precision.HIGHEST
    )
    norm = 1.0 / (T_SIZE * (float(PH) * float(Q)) ** 0.5)
    return lax.psum(local_scores * norm, ("shard", "dp"))


def solution(mesh):
    in_specs = (
        P(None, None, "dp"),
        P(None, "dp", "shard"),
        P("buffer", None, "dp"),
        P("buffer", "dp", "shard"),
        P("shard", "dp"),
        P("dp", "shard"),
        P("shard", "dp"),
    )
    out_specs = P(None, "buffer")
    return jax.shard_map(local, mesh=mesh, in_specs=in_specs, out_specs=out_specs, check_vma=False)
```

profile of v0, /device:TPU:128, one launch (start us, length us, event | category | flops | bytes accessed | tf_op | source)
XLA Modules:
  0.0 746.3 jit_solution(8024703425757017184)
XLA Ops:
  6.5 0.0 copy-start
  6.5 0.0 all-reduce.3.cloned.1.call-start
  6.5 2.5 pad_maximum_fusion
  9.1 0.5 copy-done
  9.5 5.1 convolution_convert_fusion.1
  14.7 0.0 copy-start.3
  14.7 0.0 copy-start.4
  14.7 0.0 copy-start.5
  14.7 3.8 copy.8
  18.5 0.0 all-reduce.3.cloned.1.call-update
  18.6 0.0 all-reduce.5.cloned.1.call-start
  18.6 0.0 copy-done.3
  18.6 38.6 %all_gather.6 = bf16[4,128,512]{2,1,0:T(8,128)(2,1)S(1)} all-gather(bf16[4,16,512]{2,1,0:T(8,128)(2,1)S(1)} %copy-done.3), channel_id=1, replica_groups=mesh['shard'=16,'dp'=8,'buffer'=2] {'dp'}, dimensions={1}, use_global_device_ids=true | all-gather | bytes 589824 | tf_op jit(solution)/shard_map/all_gather | solution.py:26
  57.2 0.0 copy-done.4
  57.2 38.7 %all_gather.7 = bf16[4,128,512]{2,1,0:T(8,128)(2,1)S(1)} all-gather(bf16[4,16,512]{2,1,0:T(8,128)(2,1)S(1)} %copy-done.4), channel_id=1, replica_groups=mesh['shard'=16,'dp'=8,'buffer'=2] {'dp'}, dimensions={1}, use_global_device_ids=true | all-gather | bytes 589824 | tf_op jit(solution)/shard_map/all_gather | solution.py:27
  95.9 0.1 pad_maximum_fusion.1
  96.0 0.0 copy-done.5
  96.0 2.6 convolution_convert_fusion
  98.6 0.0 all-reduce.5.cloned.1.call-update
  98.6 4.6 broadcast_add_fusion
  103.3 33.8 %all-reduce.3.cloned.1.call-done = bf16[8,128,896]{1,2,0:T(8,128)(2,1)} async-done(((bf16[8,128,896]{1,2,0:T(8,128)(2,1)}), bf16[8,128,896]{1,2,0:T(8,128)(2,1)}) %all-reduce.3.cloned.1.call-update) | async-done | bytes 1835024 | tf_op jit(solution)/shard_map/psum | solution.py:24
  137.1 139.0 %all-reduce.5.cloned.1.call-done = bf16[8,128,1024]{2,1,0:T(8,128)(2,1)} async-done(((bf16[8,128,1024]{2,1,0:T(8,128)(2,1)}), bf16[8,128,1024]{2,1,0:T(8,128)(2,1)}) %all-reduce.5.cloned.1.call-update) | async-done | bytes 2097168 | tf_op jit(solution)/shard_map/psum | solution.py:33
  276.1 0.0 copy-start.2
  276.1 15.9 %fusion.13 = f32[8,896,1024]{2,1,0:T(8,128)} fusion(bf16[8,128,896]{1,2,0:T(8,128)(2,1)} %all-reduce.3.cloned.1.call-done, bf16[8,128,1024]{2,1,0:T(8,128)(2,1)} %all-reduce.5.cloned.1.call-done), kind=kOutput, calls=%fused_computation.11 | convolution fusion | flops 1879048192 | bytes 33292288 | tf_op jit(solution)/shard_map/nte,ntq->neq/dot_general | solution.py:37
  292.0 0.0 copy-done.2
  292.0 15.3 %slice_divide_fusion = (f32[4,896,1024]{2,1,0:T(8,128)S(1)}, f32[4,896,1024]{2,1,0:T(8,128)}) fusion(f32[8,896,1024]{2,1,0:T(8,128)} %fusion.13, f32[896,1024]{1,0:T(8,128)S(1)} %copy-done.2), kind=kLoop, calls=%fused_computation | loop fusion | flops 3670016 | bytes 62390272 | tf_op jit(solution)/shard_map/div | solution.py:38
  307.3 0.0 copy-start.1
  307.3 74.0 %fusion.8 = f32[4,4]{1,0:T(4,128)S(1)} fusion(f32[4,896,1024]{2,1,0:T(8,128)} %get-tuple-element.6, f32[4,896,1024]{2,1,0:T(8,128)S(1)} %get-tuple-element.5), kind=kOutput, calls=%fused_computation.9 | convolution fusion | flops 176160784 | bytes 29360192 | tf_op jit(solution)/shard_map/dot_general | solution.py:40
  381.3 358.1 %psum.23 = f32[4,4]{1,0:T(4,128)} all-reduce(f32[4,4]{1,0:T(4,128)S(1)} %fusion.8), channel_id=1, replica_groups=mesh['shard'=16,'dp'=8,'buffer'=2] {'shard','dp'}, use_global_device_ids=true, to_apply=%region_2.0 | all-reduce | flops 16 | bytes 128 | tf_op jit(solution)/shard_map/psum | solution.py:44
  739.5 0.0 copy-done.1
Async XLA Ops:
  6.5 3.0 copy-start
  6.5 130.5 %all-reduce.3.cloned.1.call-start = ((), (), s32[]{:S(2)}) async-start(), calls=%async_computation | async-start | bytes 3670016 | tf_op jit(solution)/shard_map/psum | solution.py:24
  14.7 3.9 copy-start.3
  14.7 42.5 %copy-start.4 = (bf16[4,16,512]{2,1,0:T(8,128)(2,1)S(1)}, bf16[4,16,512]{2,1,0:T(8,128)(2,1)}, u32[]{:S(2)}) copy-start(bf16[4,16,512]{2,1,0:T(8,128)(2,1)} %param.10) | copy-start | bytes 196612
  14.7 81.3 %copy-start.5 = (bf16[1024,512]{1,0:T(8,128)(2,1)S(1)}, bf16[1024,512]{1,0:T(8,128)(2,1)}, u32[]{:S(2)}) copy-start(bf16[1024,512]{1,0:T(8,128)(2,1)} %param.12) | copy-start | bytes 3145732
  18.6 257.5 %all-reduce.5.cloned.1.call-start = ((), (), s32[]{:S(2)}) async-start(), calls=%async_computation.1 | async-start | bytes 4194304 | tf_op jit(solution)/shard_map/psum | solution.py:33
  276.1 16.0 %copy-start.2 = (f32[896,1024]{1,0:T(8,128)S(1)}, f32[896,1024]{1,0:T(8,128)}, u32[]{:S(2)}) copy-start(f32[896,1024]{1,0:T(8,128)} %broadcast_add_fusion) | copy-start | bytes 11010052
  307.3 432.1 %copy-start.1 = (bf16[896,1792]{1,0:T(8,128)(2,1)S(1)}, bf16[896,1792]{1,0:T(8,128)(2,1)}, u32[]{:S(2)}) copy-start(bf16[896,1792]{1,0:T(8,128)(2,1)} %param.11) | copy-start | bytes 9633796
Sparse Core Ops, SparseCore 0:
  18.7 118.3 all-reduce.2
  139.7 136.3 all-reduce.4
where the time goes:
time: 747 us; the launch traced here: 746 us
  blocking collectives  435 us (58%)
  waiting for transfers between devices  173 us (23%)
  matrix products  97.7 us (13%)
  other arithmetic  22.5 us (3%)
  between operations  13.4 us (2%)
    psum x1, blocking collectives, local(): return lax.psum(local_scores * norm, ('shard', 'dp'))  358 us
    psum x1, waiting for transfers between devices, local(): rotated_act = lax.psum(act_part.astype(jnp.bfloat16), 'shard')  139 us
    dot_general x1, matrix products, local(): jnp.dot(scaled.reshape(count_q, -1), buffer_tiles.T, precision=lax.Precis...  74 us
    all_gather x1, blocking collectives, local(): lax.all_gather(buffer_act, 'dp', axis=1, tiled=True)  38.7 us
    all_gather x1, blocking collectives, local(): lax.all_gather(query_act, 'dp', axis=1, tiled=True)  38.6 us
    psum x1, waiting for transfers between devices, local(): rotated_grad = lax.psum(grad_part.astype(jnp.bfloat16), 'dp')  33.8 us
    dot_general x1, matrix products, local(): jnp.einsum('nte,ntq->neq', grad_rows, act_rows, preferred_element_type=jn...  15.9 us
    div x1, other arithmetic, local(): scaled = tiles[:count_q] / (eigenvalues + DAMPING)  15.3 us
  transfers between devices with their start and end apart: 2, of which 2 were waited for; matrix products, arithmetic and copies ran while one was open for 1% of the time, Pallas kernels for 0%

commit v1 on v0

v1 whole, which is shorter than its diff:
```python
import jax
import jax.numpy as jnp
from jax import lax
from jax.experimental import pallas as pl
from jax.experimental.pallas import tpu as pltpu
from jax.sharding import PartitionSpec as P

PH = 14336
Q = 8192
T_SIZE = 128
DAMPING = 0.1
NORM = 1.0 / (T_SIZE * (float(PH) * float(Q)) ** 0.5)

F32 = jnp.float32
BF16 = jnp.bfloat16
NT = (((1,), (1,)), ((), ()))


def params(mib):
    return pltpu.CompilerParams(vmem_limit_bytes=mib * 1024 * 1024)


def rotate_grad_kernel(core_ref, qg_ref, bg_ref, basis_ref, qa_ref, ba_ref, out_ref):
    step = pl.program_id(0)
    n_dp, rows, _ = out_ref.shape
    half_rows = (rows - basis_ref.shape[0] // n_dp) // 2
    eigen = basis_ref.shape[0] // n_dp

    def emit(grads):
        part = lax.dot_general(basis_ref[...], grads, NT, preferred_element_type=F32).astype(BF16)
        for d in range(n_dp):
            out_ref[d, :eigen, :] = part[d * eigen:(d + 1) * eigen, :]

    def pack(top, bottom):
        for d in range(n_dp):
            out_ref[d, eigen:eigen + half_rows, :] = top
            out_ref[d, eigen + half_rows:, :] = bottom

    width = out_ref.shape[2]

    @pl.when(step == 0)
    def _():
        emit(qg_ref[...].reshape(width, qg_ref.shape[2]))
        pack(qa_ref[:, :, :width].reshape(half_rows, width), ba_ref[:2, :, :width].reshape(half_rows, width))

    @pl.when(step > 0)
    def _():
        emit(bg_ref[...].reshape(width, bg_ref.shape[2]))

    @pl.when(step == 1)
    def _():
        pack(qa_ref[:, :, width:].reshape(half_rows, width), ba_ref[:2, :, width:].reshape(half_rows, width))

    @pl.when(step == 2)
    def _():
        pack(ba_ref[2:, :, :width].reshape(half_rows, width), ba_ref[2:, :, width:].reshape(half_rows, width))


def rotate_grad(core, query_grad, buffer_grad, basis, query_act, buffer_act, n_dp):
    inner = basis.shape[1]
    outer = basis.shape[0]
    rows = outer // n_dp + 64
    q_in = query_act.shape[2]
    grid_spec = pltpu.PrefetchScalarGridSpec(
        num_scalar_prefetch=1,
        grid=(3,),
        in_specs=[
            pl.BlockSpec((2, T_SIZE, inner), lambda i, c: (c[0], 0, 0)),
            pl.BlockSpec((2, T_SIZE, inner), lambda i, c: (jnp.maximum(i - 1, 0), 0, 0)),
            pl.BlockSpec((outer, inner), lambda i, c: (0, 0)),
            pl.BlockSpec((2, 16, q_in), lambda i, c: (c[0], 0, 0)),
            pl.BlockSpec((4, 16, q_in), lambda i, c: (0, 0, 0)),
        ],
        out_specs=pl.BlockSpec((n_dp, rows, 256), lambda i, c: (0, 0, i)),
    )
    return pl.pallas_call(
        rotate_grad_kernel,
        grid_spec=grid_spec,
        out_shape=jax.ShapeDtypeStruct((n_dp, rows, 768), BF16),
        compiler_params=params(60),
        cost_estimate=pl.CostEstimate(flops=2 * 768 * outer * inner, bytes_accessed=8 * 1024 * 1024, transcendentals=0),
        name="rotate_grad",
    )(core, query_grad, buffer_grad, basis, query_act, buffer_act)


def rotate_act_kernel(recv_ref, basis_ref, grad_ref, out_ref, acts):
    n_dp, rows, _ = recv_ref.shape
    eigen = grad_ref.shape[0]

    @pl.when(pl.program_id(0) == 0)
    def _():
        total = recv_ref[0, :eigen, :].astype(F32)
        for d in range(1, n_dp):
            total = total + recv_ref[d, :eigen, :].astype(F32)
        grad_ref[...] = total.astype(BF16)
        for d in range(n_dp):
            for n in range(6):
                to = n * T_SIZE + d * 16
                if n < 4:
                    start = eigen + n * 16
                    acts[to:to + 16, :] = recv_ref[d, start:start + 16, :512]
                else:
                    start = eigen + (n - 4) * 16
                    acts[to:to + 16, :256] = recv_ref[d, start:start + 16, 512:]
                    acts[to:to + 16, 256:] = recv_ref[d, start + 32:start + 48, 512:]

    out_ref[...] = lax.dot_general(acts[...], basis_ref[...], NT, preferred_element_type=F32).astype(BF16)


def rotate_act(received, basis):
    n_dp, rows, width = received.shape
    outer, inner = basis.shape
    return pl.pallas_call(
        rotate_act_kernel,
        grid=(outer // 256,),
        in_specs=[
            pl.BlockSpec((n_dp, rows, width), lambda i: (0, 0, 0)),
            pl.BlockSpec((256, inner), lambda i: (i, 0)),
        ],
        out_specs=[
            pl.BlockSpec((rows - 64, width), lambda i: (0, 0)),
            pl.BlockSpec((width, 256), lambda i: (0, i)),
        ],
        out_shape=[
            jax.ShapeDtypeStruct((rows - 64, width), BF16),
            jax.ShapeDtypeStruct((width, outer), BF16),
        ],
        scratch_shapes=[pltpu.VMEM((width, inner), BF16)],
        compiler_params=params(40),
        cost_estimate=pl.CostEstimate(flops=2 * width * outer * inner, bytes_accessed=6 * 1024 * 1024, transcendentals=0),
        name="rotate_act",
    )(received, basis)


def add_parts_kernel(parts_ref, out_ref):
    count = parts_ref.shape[0]
    total = parts_ref[0].astype(F32)
    for s in range(1, count):
        total = total + parts_ref[s].astype(F32)
    total = total.astype(BF16)
    for s in range(count):
        out_ref[s] = total


def add_parts(parts):
    count, rows, width = parts.shape
    return pl.pallas_call(
        add_parts_kernel,
        grid=(2,),
        in_specs=[pl.BlockSpec((count, rows, width // 2), lambda i: (0, 0, i))],
        out_specs=pl.BlockSpec((count, rows, width // 2), lambda i: (0, 0, i)),
        out_shape=jax.ShapeDtypeStruct(parts.shape, BF16),
        compiler_params=params(40),
        cost_estimate=pl.CostEstimate(flops=parts.size, bytes_accessed=4 * parts.size, transcendentals=0),
        name="add_parts",
    )(parts)


def pack_grads_kernel(core_ref, own_ref, other_ref, out_ref):
    half = other_ref.shape[1]
    own = own_ref[:, :half]
    other = other_ref[...]
    first = core_ref[0] == 0
    out_ref[:, :half] = jnp.where(first, own, other)
    out_ref[:, half:2 * half] = jnp.where(first, other, own)
    out_ref[:, 2 * half:] = own_ref[:, half:]


def pack_grads(core, own, other):
    rows, width = own.shape
    half = other.shape[1]
    grid_spec = pltpu.PrefetchScalarGridSpec(
        num_scalar_prefetch=1,
        grid=(4,),
        in_specs=[
            pl.BlockSpec((rows // 4, width), lambda i, c: (i, 0)),
            pl.BlockSpec((rows // 4, half), lambda i, c: (i, 0)),
        ],
        out_specs=pl.BlockSpec((rows // 4, width + half), lambda i, c: (i, 0)),
    )
    return pl.pallas_call(
        pack_grads_kernel,
        grid_spec=grid_spec,
        out_shape=jax.ShapeDtypeStruct((rows, width + half), BF16),
        compiler_params=params(40),
        cost_estimate=pl.CostEstimate(flops=4 * 10**9, bytes_accessed=10 * 10**6, transcendentals=0),
        name="pack_grads",
    )(core, own, other)


def query_columns(grads, after):
    rows, width = grads.shape[0], 256
    return pl.pallas_call(
        query_rows_kernel,
        grid=(2,),
        in_specs=[pl.BlockSpec((rows // 2, width), lambda i: (i, 0)), pl.BlockSpec(memory_space=pl.ANY)],
        out_specs=pl.BlockSpec((rows // 2, width), lambda i: (i, 0)),
        out_shape=jax.ShapeDtypeStruct((rows, width), BF16),
        compiler_params=params(40),
        cost_estimate=pl.CostEstimate(flops=0, bytes_accessed=4 * rows * width, transcendentals=0),
        name="query_columns",
    )(grads, after)


def query_rows_kernel(acts_ref, after_ref, out_ref):
    out_ref[...] = acts_ref[...]


def query_rows(acts, after):
    rows, width = 256, acts.shape[1]
    return pl.pallas_call(
        query_rows_kernel,
        grid=(2,),
        in_specs=[pl.BlockSpec((rows // 2, width), lambda i: (i, 0)), pl.BlockSpec(memory_space=pl.ANY)],
        out_specs=pl.BlockSpec((rows // 2, width), lambda i: (i, 0)),
        out_shape=jax.ShapeDtypeStruct((rows, width), BF16),
        compiler_params=params(40),
        cost_estimate=pl.CostEstimate(flops=0, bytes_accessed=4 * rows * width, transcendentals=0),
        name="query_rows",
    )(acts, after)


PIECE = 64


def scores_kernel(core_ref, g_ref, a_ref, ao_ref, eig_ref, out_ref, inverse, left, right, total):
    step = pl.program_id(0)
    eigen = g_ref.shape[0]
    width = a_ref.shape[1]
    inverse[...] = 1.0 / (eig_ref[...] + DAMPING)

    def tile(n, acts):
        return jnp.dot(g_ref[:, n * T_SIZE:(n + 1) * T_SIZE], acts, preferred_element_type=F32)

    def keep(ref, slot, block):
        for c in range(eigen // PIECE):
            ref[slot * PIECE:(slot + 1) * PIECE, c * width:(c + 1) * width] = block[c * PIECE:(c + 1) * PIECE, :]

    first = core_ref[0] == 0
    for i in range(4):
        part = slice((i % 2) * T_SIZE, (i % 2 + 1) * T_SIZE)
        acts = jnp.where(first == (i < 2), a_ref[part, :], ao_ref[part, :])
        keep(left, i, (tile(i, acts) * inverse[...]).astype(BF16))
    for j in range(4):
        keep(right, j, tile(4 + j, a_ref[(2 + j) * T_SIZE:(3 + j) * T_SIZE, :]).astype(BF16))
    product = lax.dot_general(left[...], right[...], NT, preferred_element_type=F32)

    @pl.when(step == 0)
    def _():
        total[...] = product

    @pl.when(step > 0)
    def _():
        total[...] += product

    @pl.when(step == pl.num_programs(0) - 1)
    def _():
        size = total.shape[0]
        row = lax.broadcasted_iota(jnp.int32, (size, size), 0)
        column = lax.broadcasted_iota(jnp.int32, (size, size), 1)
        own = jnp.where(row % PIECE == column % PIECE, total[...], 0.0)
        lane = lax.broadcasted_iota(jnp.int32, (1, size), 1)
        place = lax.broadcasted_iota(jnp.int32, (8, 128), 1)
        result = jnp.zeros((8, 128), F32)
        for i in range(4):
            line = jnp.sum(own[i * PIECE:(i + 1) * PIECE, :], axis=0, keepdims=True)
            for j in range(4):
                value = jnp.sum(jnp.where(lane // PIECE == j, line, 0.0), axis=1, keepdims=True) * NORM
                result = result + jnp.where(place == i * 4 + j, value, 0.0)
        out_ref[...] = result


def tile_scores(core, grads, acts, acts_other, eigenvalues):
    eigen = grads.shape[0]
    rows = acts.shape[0]
    width = eigenvalues.shape[1]
    block = 256
    pieces = eigen // PIECE
    grid_spec = pltpu.PrefetchScalarGridSpec(
        num_scalar_prefetch=1,
        grid=(width // block,),
        in_specs=[
            pl.BlockSpec(grads.shape, lambda i, c: (0, 0)),
            pl.BlockSpec((rows, block), lambda i, c: (0, i)),
            pl.BlockSpec((256, block), lambda i, c: (0, i)),
            pl.BlockSpec((eigen, block), lambda i, c: (0, i)),
        ],
        out_specs=pl.BlockSpec((8, 128), lambda i, c: (0, 0)),
        scratch_shapes=[
            pltpu.VMEM((eigen, block), F32),
            pltpu.VMEM((4 * PIECE, pieces * block), BF16),
            pltpu.VMEM((4 * PIECE, pieces * block), BF16),
            pltpu.VMEM((4 * PIECE, 4 * PIECE), F32),
        ],
    )
    return pl.pallas_call(
        scores_kernel,
        grid_spec=grid_spec,
        out_shape=jax.ShapeDtypeStruct((8, 128), F32),
        compiler_params=params(40),
        cost_estimate=pl.CostEstimate(flops=4 * 8 * T_SIZE * eigen * width, bytes_accessed=8 * 1024 * 1024, transcendentals=0),
        name="tile_scores",
    )(core, grads, acts, acts_other, eigenvalues)


def local(query_grad, query_act, buffer_grad, buffer_act, grad_basis, act_basis, eigenvalues):
    n_dp, n_shard = lax.axis_size("dp"), lax.axis_size("shard")
    core = lax.axis_index("buffer").astype(jnp.int32).reshape(1)
    swap = [(0, 1), (1, 0)]
    sent = rotate_grad(core, query_grad, buffer_grad, grad_basis, query_act, buffer_act, n_dp)
    received = lax.all_to_all(sent, "dp", 0, 0, tiled=True)
    grad_piece, act_part = rotate_act(received, act_basis)
    grads = lax.all_gather(grad_piece, "dp", axis=0, tiled=True)
    parts = lax.all_to_all(act_part.reshape(n_shard, -1, act_part.shape[1]), "shard", 0, 0, tiled=True)
    sums = add_parts(parts)
    grads_other = lax.ppermute(query_columns(grads, sums), "buffer", swap)
    packed = pack_grads(core, grads, grads_other)
    acts = lax.all_to_all(sums, "shard", 0, 0, tiled=True).reshape(act_part.shape)
    acts_other = lax.ppermute(query_rows(acts, packed), "buffer", swap)
    mine = tile_scores(core, packed, acts, acts_other, eigenvalues)
    count = n_dp * n_shard
    every = lax.all_to_all(jnp.broadcast_to(mine[None, :1], (count, 1, 128)), ("shard", "dp"), 0, 0, tiled=True)
    return jnp.sum(every, axis=(0, 1))[:16].reshape(4, 4)


def solution(mesh):
    in_specs = (
        P(None, None, "dp"),
        P(None, "dp", "shard"),
        P("buffer", None, "dp"),
        P("buffer", "dp", "shard"),
        P("shard", "dp"),
        P("dp", "shard"),
        P("shard", "dp"),
    )
    out_specs = P(None, "buffer")
    return jax.shard_map(local, mesh=mesh, in_specs=in_specs, out_specs=out_specs, check_vma=False)
```

time: 747 us -> 182 us (0.24)
  the two profiles are of different devices: /device:TPU:128 before, /device:TPU:1 now
where the time goes in v1:
time: 182 us
  waiting for transfers between devices  70.7 us (39%)
  blocking collectives  54.5 us (30%)
  Pallas kernels  22.5 us (12%)
  starting transfers between devices  18.8 us (10%)
  between operations  13.5 us (7%)
  local copies, waits for them, and re-layouts  2.05 us (1%)
    all_to_all x1, blocking collectives, local(): received = lax.all_to_all(sent, 'dp', 0, 0, tiled=True)  35.5 us
    all_to_all x1, waiting for transfers between devices, local(): lax.all_to_all(act_part.reshape(n_shard, -1, act_part.shape[1]), 'shard',...  35.4 us
    all_gather x1, waiting for transfers between devices, local(): grads = lax.all_gather(grad_piece, 'dp', axis=0, tiled=True)  22.8 us
    all_to_all x1, blocking collectives, local(): lax.all_to_all(jnp.broadcast_to(mine[None, :1], (count, 1, 128)), ('shard...  18.9 us
    pallas_call x1, Pallas kernels, tile_scores(): pl.pallas_call(scores_kernel, grid_spec=grid_spec, out_shape=jax.ShapeDty...  10.7 us
    all_to_all x1, waiting for transfers between devices, local(): lax.all_to_all(sums, 'shard', 0, 0, tiled=True).reshape(act_part.shape)  8.87 us
    all_to_all x1, starting transfers between devices, local(): lax.all_to_all(act_part.reshape(n_shard, -1, act_part.shape[1]), 'shard',...  8.58 us
    pallas_call x1, Pallas kernels, rotate_grad(): pl.pallas_call(rotate_grad_kernel, grid_spec=grid_spec, out_shape=jax.Sha...  6.96 us
  transfers between devices with their start and end apart: 5, of which 5 were waited for; matrix products, arithmetic and copies ran while one was open for 0% of the time, Pallas kernels for 1%

profile of v1, /device:TPU:1, one launch (start us, length us, event | category | flops | bytes accessed | tf_op | source)
XLA Modules:
  0.0 181.9 jit_solution(1775270045577749591)
XLA Ops:
  6.5 7.0 %rotate_grad.1 = bf16[8,176,768]{2,1,0:T(8,128)(2,1)} custom-call(s32[1]{0:T(128)} %bitcast.core_ref, bf16[4,128,1792]{2,1,0:T(8,128)(2,1)} %qg_ref.1, bf16[4,128,1792]{2,1,0:T(8,128)(2,1)} %bg_ref.1, bf16[896,1792]{1,0:T(8,128)(2,1)} %basis_ref.2, bf16[4,16,512]{2,1,0:T(8,128)(2,1)} %qa_ref.1, bf16[4,16,512]{2,1,0:T(8,128)(2,1)} %ba_ref.1), custom_call_target="tpu_custom_call" | custom-call | flops 2466250752 | bytes 8388608 | tf_op jit(solution)/shard_map/rotate_grad/pallas_call | solution.py:76
  13.5 0.0 copy-start.2
  13.5 35.5 %all_to_all.20.recv_ref = bf16[8,176,768]{2,1,0:T(8,128)(2,1)S(1)} all-to-all(bf16[8,176,768]{2,1,0:T(8,128)(2,1)} %rotate_grad.1), channel_id=1, replica_groups=mesh['shard'=16,'dp'=8,'buffer'=2] {'dp'}, dimensions={0} | all-to-all | bytes 4325376 | tf_op jit(solution)/shard_map/all_to_all | solution.py:311
  49.0 0.0 copy-done.2
  49.0 3.0 %rotate_act.1 = (bf16[112,768]{1,0:T(8,128)(2,1)}, bf16[768,1024]{1,0:T(8,128)(2,1)}) custom-call(bf16[8,176,768]{2,1,0:T(8,128)(2,1)S(1)} %all_to_all.20.recv_ref, bf16[1024,512]{1,0:T(8,128)(2,1)S(1)} %copy-done.2), custom_call_target="tpu_custom_call" | custom-call | flops 805306368 | bytes 6291456 | tf_op jit(solution)/shard_map/rotate_act/pallas_call | solution.py:113
  52.0 8.6 %all-to-all-start.1 = ((bf16[16,48,1024]{2,1,0:T(8,128)(2,1)}), bf16[16,48,1024]{2,1,0:T(8,128)(2,1)S(1)}, u32[]{:S(2)}, u32[]{:S(2)}) async-start(bf16[16,48,1024]{2,1,0:T(8,128)(2,1)} %bitcast.1), calls=%async_computation.1 | async-start | bytes 3145728 | tf_op jit(solution)/shard_map/all_to_all | solution.py:314
  60.6 0.0 all-gather.2.cloned.1.call-start
  60.6 0.7 all-gather.2.cloned.1.call-update
  61.3 35.4 %all-to-all-done.1.parts_ref = bf16[16,48,1024]{2,1,0:T(8,128)(2,1)S(1)} async-done(((bf16[16,48,1024]{2,1,0:T(8,128)(2,1)}), bf16[16,48,1024]{2,1,0:T(8,128)(2,1)S(1)}, u32[]{:S(2)}, u32[]{:S(2)}) %all-to-all-start.1) | async-done | bytes 1572896 | tf_op jit(solution)/shard_map/all_to_all | solution.py:314
  96.7 1.5 add_parts.1.after_ref
  98.2 6.1 %all-to-all-start.2 = ((bf16[16,48,1024]{2,1,0:T(8,128)(2,1)}), bf16[16,48,1024]{2,1,0:T(8,128)(2,1)S(1)}, u32[]{:S(2)}, u32[]{:S(2)}) async-start(bf16[16,48,1024]{2,1,0:T(8,128)(2,1)} %add_parts.1.after_ref), calls=%async_computation.2 | async-start | bytes 3145728 | tf_op jit(solution)/shard_map/all_to_all | solution.py:318
  104.3 22.8 %all-gather.2.cloned.1.call-done.acts_ref.own_ref = bf16[896,768]{1,0:T(8,128)(2,1)} async-done(((bf16[112,768]{1,0:T(8,128)(2,1)}), bf16[896,768]{1,0:T(8,128)(2,1)}) %all-gather.2.cloned.1.call-update) | async-done | bytes 1376272 | tf_op jit(solution)/shard_map/all_gather | solution.py:313
  127.1 0.0 copy-start
  127.1 1.3 copy-done
  128.4 0.0 copy-start.1
  128.4 0.1 query_columns.1
  128.5 1.4 collective-permute-start
  129.9 1.4 collective-permute-done.other_ref
  131.4 0.0 copy-done.1
  131.4 0.2 pack_grads.1.after_ref.g_ref
  131.6 8.9 %all-to-all-done.2 = bf16[16,48,1024]{2,1,0:T(8,128)(2,1)S(1)} async-done(((bf16[16,48,1024]{2,1,0:T(8,128)(2,1)}), bf16[16,48,1024]{2,1,0:T(8,128)(2,1)S(1)}, u32[]{:S(2)}, u32[]{:S(2)}) %all-to-all-start.2) | async-done | bytes 1572896 | tf_op jit(solution)/shard_map/all_to_all | solution.py:318
  140.4 0.0 copy-start.3
  140.4 0.1 query_rows.1
  140.5 2.6 %collective-permute-start.1 = (bf16[256,1024]{1,0:T(8,128)(2,1)S(1)}, bf16[256,1024]{1,0:T(8,128)(2,1)S(1)}, u32[]{:S(2)}, u32[]{:S(2)}) collective-permute-start(bf16[256,1024]{1,0:T(8,128)(2,1)S(1)} %query_rows.1), channel_id=1, source_target_pairs={{0,1},{1,0},{2,3},{3,2},{4,5},{5,4},{6,7},{7,6},{8,9},{9,8},{10,11... | collective-permute-start | bytes 1572872 | tf_op jit(solution)/shard_map/ppermute | solution.py:319
  143.2 1.5 collective-permute-done.1.ao_ref
  144.7 0.0 copy-done.3
  144.7 10.7 %tile_scores.1 = f32[8,128]{1,0:T(8,128)S(1)} custom-call(s32[1]{0:T(128)} %bitcast.core_ref, bf16[896,1024]{1,0:T(8,128)(2,1)S(1)} %pack_grads.1.after_ref.g_ref, bf16[768,1024]{1,0:T(8,128)(2,1)S(1)} %bitcast.8, bf16[256,1024]{1,0:T(8,128)(2,1)S(1)} %collective-permute-done.1.ao_ref, f32[896,1024]{1,0:T(8,128)S(1)} %copy-done.3), custom_call_target="tpu_custom_call" | custom-call | flops 3758096384 | bytes 8388608 | tf_op jit(solution)/shard_map/tile_scores/pallas_call | solution.py:296
  155.5 18.9 %all_to_all.21 = f32[128,1,128]{2,1,0:T(1,128)S(1)} all-to-all(f32[128,1,128]{2,1,0:T(1,128)S(1)} %broadcast_in_dim.9), channel_id=1, replica_groups=mesh['shard'=16,'dp'=8,'buffer'=2] {'shard','dp'}, dimensions={0} | all-to-all | bytes 131072 | tf_op jit(solution)/shard_map/all_to_all | solution.py:322
  174.4 0.7 reshape.26
  (3 shorter events, 0.1 us)
Async XLA Ops:
  13.5 35.5 %copy-start.2 = (bf16[1024,512]{1,0:T(8,128)(2,1)S(1)}, bf16[1024,512]{1,0:T(8,128)(2,1)}, u32[]{:S(2)}) copy-start(bf16[1024,512]{1,0:T(8,128)(2,1)} %basis_ref.3) | copy-start | bytes 3145732
  52.0 44.7 %all-to-all-start.1 = ((bf16[16,48,1024]{2,1,0:T(8,128)(2,1)}), bf16[16,48,1024]{2,1,0:T(8,128)(2,1)S(1)}, u32[]{:S(2)}, u32[]{:S(2)}) async-start(bf16[16,48,1024]{2,1,0:T(8,128)(2,1)} %bitcast.1), calls=%async_computation.1 | async-start | bytes 3145728 | tf_op jit(solution)/shard_map/all_to_all | solution.py:314
  60.6 66.5 %all-gather.2.cloned.1.call-start = ((), (), s32[]{:S(2)}) async-start(), calls=%async_computation.4 | async-start | bytes 1548288 | tf_op jit(solution)/shard_map/all_gather | solution.py:313
  98.2 42.3 %all-to-all-start.2 = ((bf16[16,48,1024]{2,1,0:T(8,128)(2,1)}), bf16[16,48,1024]{2,1,0:T(8,128)(2,1)S(1)}, u32[]{:S(2)}, u32[]{:S(2)}) async-start(bf16[16,48,1024]{2,1,0:T(8,128)(2,1)} %add_parts.1.after_ref), calls=%async_computation.2 | async-start | bytes 3145728 | tf_op jit(solution)/shard_map/all_to_all | solution.py:318
  127.1 1.3 copy-start
  128.4 3.0 %copy-start.1 = (bf16[896,768]{1,0:T(8,128)(2,1)S(1)}, bf16[896,768]{1,0:T(8,128)(2,1)}, u32[]{:S(2)}) copy-start(bf16[896,768]{1,0:T(8,128)(2,1)} %all-gather.2.cloned.1.call-done.acts_ref.own_ref) | copy-start | bytes 4128772
  128.5 2.8 %collective-permute-start = (bf16[896,256]{1,0:T(8,128)(2,1)S(1)}, bf16[896,256]{1,0:T(8,128)(2,1)S(1)}, u32[]{:S(2)}, u32[]{:S(2)}) collective-permute-start(bf16[896,256]{1,0:T(8,128)(2,1)S(1)} %query_columns.1), channel_id=1, source_target_pairs={{0,1},{1,0},{2,3},{3,2},{4,5},{5,4},{6,7},{7,6},{8,9},{9,8},{10,11... | collective-permute-start | bytes 1376264 | tf_op jit(solution)/shard_map/ppermute | solution.py:316
  140.4 4.3 %copy-start.3 = (f32[896,1024]{1,0:T(8,128)S(1)}, f32[896,1024]{1,0:T(8,128)}, u32[]{:S(2)}) copy-start(f32[896,1024]{1,0:T(8,128)} %eig_ref.1) | copy-start | bytes 11010052
  140.5 4.2 %collective-permute-start.1 = (bf16[256,1024]{1,0:T(8,128)(2,1)S(1)}, bf16[256,1024]{1,0:T(8,128)(2,1)S(1)}, u32[]{:S(2)}, u32[]{:S(2)}) collective-permute-start(bf16[256,1024]{1,0:T(8,128)(2,1)S(1)} %query_rows.1), channel_id=1, source_target_pairs={{0,1},{1,0},{2,3},{3,2},{4,5},{5,4},{6,7},{7,6},{8,9},{9,8},{10,11... | collective-permute-start | bytes 1572872 | tf_op jit(solution)/shard_map/ppermute | solution.py:319
Sparse Core Ops, SparseCore 0:
  64.0 63.0 all-gather.1

commit v2 on v1

v2 whole, which is shorter than its diff:
```python
import jax
import jax.numpy as jnp
from jax import lax
from jax.experimental import pallas as pl
from jax.experimental.pallas import tpu as pltpu
from jax.sharding import PartitionSpec as P

PH = 14336
Q = 8192
T_SIZE = 128
DAMPING = 0.1
NORM = 1.0 / (T_SIZE * (float(PH) * float(Q)) ** 0.5)

F32 = jnp.float32
BF16 = jnp.bfloat16
NT = (((1,), (1,)), ((), ()))


def params(mib):
    return pltpu.CompilerParams(vmem_limit_bytes=mib * 1024 * 1024)


def pack_acts_kernel(core_ref, qa_ref, ba_ref, out_ref):
    half = qa_ref.shape[0] * qa_ref.shape[1]
    width = qa_ref.shape[2]
    for d in range(out_ref.shape[0]):
        out_ref[d, :half, :] = qa_ref[...].reshape(half, width)
        out_ref[d, half:, :] = ba_ref[...].reshape(2 * half, width)


def pack_acts(core, query_act, buffer_act, copies):
    _, tokens, width = query_act.shape
    grid_spec = pltpu.PrefetchScalarGridSpec(
        num_scalar_prefetch=1,
        grid=(1,),
        in_specs=[
            pl.BlockSpec((2, tokens, width), lambda i, c: (c[0], 0, 0)),
            pl.BlockSpec((4, tokens, width), lambda i, c: (0, 0, 0)),
        ],
        out_specs=pl.BlockSpec((copies, 6 * tokens, width), lambda i, c: (0, 0, 0)),
    )
    return pl.pallas_call(
        pack_acts_kernel,
        grid_spec=grid_spec,
        out_shape=jax.ShapeDtypeStruct((copies, 6 * tokens, width), BF16),
        compiler_params=params(60),
        cost_estimate=pl.CostEstimate(flops=0, bytes_accessed=2 * 1024 * 1024, transcendentals=0),
        name="pack_acts",
    )(core, query_act, buffer_act)


def rotate_grad_kernel(where_ref, qg_ref, bg_ref, basis_ref, *refs):
    outs, part = refs[:-1], refs[-1]
    width = part.shape[1]
    rows = outs[0].shape[0]

    def emit(grads):
        block = grads[...].reshape(width, grads.shape[2])
        part[...] = lax.dot_general(basis_ref[...], block, NT, preferred_element_type=F32).astype(BF16)

    @pl.when(pl.program_id(0) == 0)
    def _():
        emit(qg_ref)

    @pl.when(pl.program_id(0) > 0)
    def _():
        emit(bg_ref)

    for k, out_ref in enumerate(outs):
        start = pl.multiple_of(lax.rem(where_ref[1] + k, len(outs)) * rows, 16)
        out_ref[...] = part[pl.ds(start, rows), :]


def rotate_grad(where, query_grad, buffer_grad, basis, n_y):
    outer, inner = basis.shape
    rows = outer // n_y
    grid_spec = pltpu.PrefetchScalarGridSpec(
        num_scalar_prefetch=1,
        grid=(3,),
        in_specs=[
            pl.BlockSpec((2, T_SIZE, inner), lambda i, c: (c[0], 0, 0)),
            pl.BlockSpec((2, T_SIZE, inner), lambda i, c: (jnp.maximum(i - 1, 0), 0, 0)),
            pl.BlockSpec((outer, inner), lambda i, c: (0, 0)),
        ],
        out_specs=[pl.BlockSpec((rows, 256), lambda i, c: (0, i))] * n_y,
        scratch_shapes=[pltpu.VMEM((outer, 256), BF16)],
    )
    return pl.pallas_call(
        rotate_grad_kernel,
        grid_spec=grid_spec,
        out_shape=[jax.ShapeDtypeStruct((rows, 768), BF16)] * n_y,
        compiler_params=params(60),
        cost_estimate=pl.CostEstimate(flops=2 * 768 * outer * inner, bytes_accessed=8 * 1024 * 1024, transcendentals=0),
        name="rotate_grad",
    )(where, query_grad, buffer_grad, basis)


def add_grads_kernel(where_ref, *refs):
    parts, keep_ref, send_ref = refs[:-3], refs[-3], refs[-2]
    total = refs[-1]
    value = parts[0][...].astype(F32)
    for part in parts[1:]:
        value = value + part[...].astype(F32)
    total[...] = value.astype(BF16)
    rows = keep_ref.shape[0]
    keep_ref[...] = total[pl.ds(pl.multiple_of(where_ref[2] * rows, 16), rows), :]
    send_ref[...] = total[pl.ds(pl.multiple_of((1 - where_ref[2]) * rows, 16), rows), :]


def add_grads(where, parts):
    rows, width = parts[0].shape
    half = jax.ShapeDtypeStruct((rows // 2, width), BF16)
    grid_spec = pltpu.PrefetchScalarGridSpec(
        num_scalar_prefetch=1,
        grid=(1,),
        in_specs=[pl.BlockSpec((rows, width), lambda i, c: (0, 0))] * len(parts),
        out_specs=[pl.BlockSpec((rows // 2, width), lambda i, c: (0, 0))] * 2,
        scratch_shapes=[pltpu.VMEM((rows, width), BF16)],
    )
    return pl.pallas_call(
        add_grads_kernel,
        grid_spec=grid_spec,
        out_shape=[half, half],
        compiler_params=params(40),
        cost_estimate=pl.CostEstimate(flops=4 * rows * width, bytes_accessed=12 * rows * width, transcendentals=0),
        name="add_grads",
    )(where, *parts)


def pair_grads_kernel(where_ref, own_ref, other_ref, out_ref):
    rows = own_ref.shape[0]
    first = where_ref[2] == 0
    out_ref[:rows, :] = jnp.where(first, own_ref[...], other_ref[...])
    out_ref[rows:, :] = jnp.where(first, other_ref[...], own_ref[...])


def pair_grads(where, own, other):
    rows, width = own.shape
    grid_spec = pltpu.PrefetchScalarGridSpec(
        num_scalar_prefetch=1,
        grid=(1,),
        in_specs=[pl.BlockSpec((rows, width), lambda i, c: (0, 0))] * 2,
        out_specs=pl.BlockSpec((2 * rows, width), lambda i, c: (0, 0)),
    )
    return pl.pallas_call(
        pair_grads_kernel,
        grid_spec=grid_spec,
        out_shape=jax.ShapeDtypeStruct((2 * rows, width), BF16),
        compiler_params=params(40),
        cost_estimate=pl.CostEstimate(flops=0, bytes_accessed=8 * rows * width, transcendentals=0),
        name="pair_grads",
    )(where, own, other)


def join_grads_kernel(where_ref, *refs):
    parts, out_ref, query_ref = refs[:-2], refs[-2], refs[-1]
    rows = parts[0].shape[0]
    half = query_ref.shape[1]
    count = len(parts)
    for k, part in enumerate(parts):
        start = pl.multiple_of(lax.rem(where_ref[1] + count - k, count) * rows, 16)
        out_ref[pl.ds(start, rows), :] = part[...]
        query_ref[pl.ds(start, rows), :] = part[:, :half]


def join_grads(where, parts):
    rows, width = parts[0].shape
    full = rows * len(parts)
    grid_spec = pltpu.PrefetchScalarGridSpec(
        num_scalar_prefetch=1,
        grid=(1,),
        in_specs=[pl.BlockSpec((rows, width), lambda i, c: (0, 0))] * len(parts),
        out_specs=[pl.BlockSpec((full, width), lambda i, c: (0, 0)), pl.BlockSpec((full, 256), lambda i, c: (0, 0))],
    )
    return pl.pallas_call(
        join_grads_kernel,
        grid_spec=grid_spec,
        out_shape=[jax.ShapeDtypeStruct((full, width), BF16), jax.ShapeDtypeStruct((full, 256), BF16)],
        compiler_params=params(40),
        cost_estimate=pl.CostEstimate(flops=0, bytes_accessed=5 * full * width, transcendentals=0),
        name="join_grads",
    )(where, *parts)


def rotate_act_kernel(recv_ref, basis_ref, after_ref, out_ref, acts):
    @pl.when(pl.program_id(0) == 0)
    def _():
        for d in range(recv_ref.shape[0]):
            for n in range(6):
                to = n * T_SIZE + d * 16
                acts[to:to + 16, :] = recv_ref[d, n * 16:(n + 1) * 16, :]

    out_ref[...] = lax.dot_general(acts[...], basis_ref[...], NT, preferred_element_type=F32).astype(BF16)


def rotate_act(received, basis, after):
    n_dp, rows, inner = received.shape
    outer = basis.shape[0]
    return pl.pallas_call(
        rotate_act_kernel,
        grid=(outer // 256,),
        in_specs=[
            pl.BlockSpec((n_dp, rows, inner), lambda i: (0, 0, 0)),
            pl.BlockSpec((256, inner), lambda i: (i, 0)),
            pl.BlockSpec(memory_space=pl.ANY),
        ],
        out_specs=pl.BlockSpec((768, 256), lambda i: (0, i)),
        out_shape=jax.ShapeDtypeStruct((768, outer), BF16),
        scratch_shapes=[pltpu.VMEM((768, inner), BF16)],
        compiler_params=params(40),
        cost_estimate=pl.CostEstimate(flops=2 * 768 * outer * inner, bytes_accessed=6 * 1024 * 1024, transcendentals=0),
        name="rotate_act",
    )(received, basis, after)


def add_parts_kernel(parts_ref, keep_ref, came_ref, out_ref, piece_ref):
    count = parts_ref.shape[0]
    total = parts_ref[0].astype(F32)
    for s in range(1, count):
        total = total + parts_ref[s].astype(F32)
    total = total.astype(BF16)
    for s in range(count):
        out_ref[s] = total
    piece_ref[...] = (keep_ref[...].astype(F32) + came_ref[...].astype(F32)).astype(BF16)


def add_parts(parts, keep, came):
    count, rows, width = parts.shape
    high, wide = keep.shape
    return pl.pallas_call(
        add_parts_kernel,
        grid=(2,),
        in_specs=[
            pl.BlockSpec((count, rows, width // 2), lambda i: (0, 0, i)),
            pl.BlockSpec((high, wide // 2), lambda i: (0, i)),
            pl.BlockSpec((high, wide // 2), lambda i: (0, i)),
        ],
        out_specs=[
            pl.BlockSpec((count, rows, width // 2), lambda i: (0, 0, i)),
            pl.BlockSpec((high, wide // 2), lambda i: (0, i)),
        ],
        out_shape=[jax.ShapeDtypeStruct(parts.shape, BF16), jax.ShapeDtypeStruct(keep.shape, BF16)],
        compiler_params=params(40),
        cost_estimate=pl.CostEstimate(flops=parts.size, bytes_accessed=4 * parts.size, transcendentals=0),
        name="add_parts",
    )(parts, keep, came)


def query_rows_kernel(acts_ref, after_ref, out_ref):
    out_ref[...] = acts_ref[...]


def query_rows(acts, after):
    rows, width = 256, acts.shape[1]
    return pl.pallas_call(
        query_rows_kernel,
        grid=(2,),
        in_specs=[pl.BlockSpec((rows // 2, width), lambda i: (i, 0)), pl.BlockSpec(memory_space=pl.ANY)],
        out_specs=pl.BlockSpec((rows // 2, width), lambda i: (i, 0)),
        out_shape=jax.ShapeDtypeStruct((rows, width), BF16),
        compiler_params=params(40),
        cost_estimate=pl.CostEstimate(flops=0, bytes_accessed=4 * rows * width, transcendentals=0),
        name="query_rows",
    )(acts, after)


PIECE = 64


def scores_kernel(core_ref, g_ref, go_ref, a_ref, ao_ref, eig_ref, out_ref, inverse, left, right, total):
    step = pl.program_id(0)
    eigen = g_ref.shape[0]
    width = a_ref.shape[1]
    inverse[...] = 1.0 / (eig_ref[...] + DAMPING)

    def tile(grads, acts, n):
        part = slice(n * T_SIZE, (n + 1) * T_SIZE)
        return jnp.dot(grads[:, part], acts[part, :], preferred_element_type=F32)

    def keep(ref, slot, block):
        for c in range(eigen // PIECE):
            ref[slot * PIECE:(slot + 1) * PIECE, c * width:(c + 1) * width] = block[c * PIECE:(c + 1) * PIECE, :]

    for i in range(2):
        keep(left, i, (tile(g_ref, a_ref, i) * inverse[...]).astype(BF16))
    for j in range(4):
        keep(right, j, tile(g_ref, a_ref, 2 + j).astype(BF16))
    for i in range(2):
        keep(left, 2 + i, (tile(go_ref, ao_ref, i) * inverse[...]).astype(BF16))
    product = lax.dot_general(left[...], right[...], NT, preferred_element_type=F32)

    @pl.when(step == 0)
    def _():
        total[...] = product

    @pl.when(step > 0)
    def _():
        total[...] += product

    @pl.when(step == pl.num_programs(0) - 1)
    def _():
        size = total.shape[0]
        row = lax.broadcasted_iota(jnp.int32, (size, size), 0)
        column = lax.broadcasted_iota(jnp.int32, (size, size), 1)
        own = jnp.where(row % PIECE == column % PIECE, total[...], 0.0)
        lane = lax.broadcasted_iota(jnp.int32, (1, size), 1)
        place = lax.broadcasted_iota(jnp.int32, (8, 128), 1)
        result = jnp.zeros((8, 128), F32)
        for i in range(4):
            line = jnp.sum(own[i * PIECE:(i + 1) * PIECE, :], axis=0, keepdims=True)
            query = (i + 2 * core_ref[0]) % 4
            for j in range(4):
                value = jnp.sum(jnp.where(lane // PIECE == j, line, 0.0), axis=1, keepdims=True) * NORM
                result = result + jnp.where(place == query * 4 + j, value, 0.0)
        out_ref[...] = result


def tile_scores(core, grads, grads_other, acts, acts_other, eigenvalues):
    eigen = grads.shape[0]
    rows = acts.shape[0]
    width = eigenvalues.shape[1]
    block = 256
    pieces = eigen // PIECE
    grid_spec = pltpu.PrefetchScalarGridSpec(
        num_scalar_prefetch=1,
        grid=(width // block,),
        in_specs=[
            pl.BlockSpec(grads.shape, lambda i, c: (0, 0)),
            pl.BlockSpec(grads_other.shape, lambda i, c: (0, 0)),
            pl.BlockSpec((rows, block), lambda i, c: (0, i)),
            pl.BlockSpec((256, block), lambda i, c: (0, i)),
            pl.BlockSpec((eigen, block), lambda i, c: (0, i)),
        ],
        out_specs=pl.BlockSpec((8, 128), lambda i, c: (0, 0)),
        scratch_shapes=[
            pltpu.VMEM((eigen, block), F32),
            pltpu.VMEM((4 * PIECE, pieces * block), BF16),
            pltpu.VMEM((4 * PIECE, pieces * block), BF16),
            pltpu.VMEM((4 * PIECE, 4 * PIECE), F32),
        ],
    )
    return pl.pallas_call(
        scores_kernel,
        grid_spec=grid_spec,
        out_shape=jax.ShapeDtypeStruct((8, 128), F32),
        compiler_params=params(40),
        cost_estimate=pl.CostEstimate(flops=4 * 8 * T_SIZE * eigen * width, bytes_accessed=8 * 1024 * 1024, transcendentals=0),
        name="tile_scores",
    )(core, grads, grads_other, acts, acts_other, eigenvalues)


def local(query_grad, query_act, buffer_grad, buffer_act, grad_basis, act_basis, eigenvalues):
    n_dp, n_shard = lax.axis_size("dp"), lax.axis_size("shard")
    n_y = n_dp // 2
    core = lax.axis_index("buffer").astype(jnp.int32)
    place = lax.axis_index("dp").astype(jnp.int32)
    where = jnp.stack([core, place // 2, place % 2])
    swap = [(0, 1), (1, 0)]
    partner = [(d, d ^ 1) for d in range(n_dp)]

    def along_y(piece, k):
        return lax.ppermute(piece, "dp", [(d, (d + 2 * k) % n_dp) for d in range(n_dp)])

    received = lax.all_to_all(pack_acts(where, query_act, buffer_act, n_dp), "dp", 0, 0, tiled=True)
    blocks = rotate_grad(where, query_grad, buffer_grad, grad_basis, n_y)
    act_part = rotate_act(received, act_basis, blocks[0])
    parts = lax.all_to_all(act_part.reshape(n_shard, -1, act_part.shape[1]), "shard", 0, 0, tiled=True)
    keep, send = add_grads(where, [blocks[0]] + [along_y(blocks[k], k) for k in range(1, n_y)])
    sums, piece = add_parts(parts, keep, lax.ppermute(send, "dp", partner))
    acts = lax.all_to_all(sums, "shard", 0, 0, tiled=True).reshape(act_part.shape)
    pair = pair_grads(where, piece, lax.ppermute(piece, "dp", partner))
    grads, grads_query = join_grads(where, [pair] + [along_y(pair, k) for k in range(1, n_y)])
    grads_other = lax.ppermute(grads_query, "buffer", swap)
    acts_other = lax.ppermute(query_rows(acts, grads_other), "buffer", swap)
    mine = tile_scores(where, grads, grads_other, acts, acts_other, eigenvalues)
    count = n_dp * n_shard
    every = lax.all_to_all(jnp.broadcast_to(mine[None, :1], (count, 1, 128)), ("shard", "dp"), 0, 0, tiled=True)
    return jnp.sum(every, axis=(0, 1))[:16].reshape(4, 4)


def solution(mesh):
    in_specs = (
        P(None, None, "dp"),
        P(None, "dp", "shard"),
        P("buffer", None, "dp"),
        P("buffer", "dp", "shard"),
        P("shard", "dp"),
        P("dp", "shard"),
        P("shard", "dp"),
    )
    out_specs = P(None, "buffer")
    return jax.shard_map(local, mesh=mesh, in_specs=in_specs, out_specs=out_specs, check_vma=False)
```

time: 182 us -> 155 us (0.85)
  blocking collectives: 54.5 us -> 20.6 us
  starting transfers between devices: 18.8 us -> 33.7 us
  between operations: 13.5 us -> 0.13 us
  Pallas kernels: 22.5 us -> 27.4 us
  waiting for transfers between devices: 70.7 us -> 68.2 us
    ppermute x2 -> x10, waiting for transfers between devices: 2.98 us -> 55.4 us  [the longest x6 31.9 us: along_y(): lax.ppermute(piece, 'dp', [(d, (d + 2 * k) % n_dp) for d in range(n_dp)])]
    all_to_all x1 -> x0, blocking collectives: 35.5 us -> none  [local(): received = lax.all_to_all(sent, 'dp', 0, 0, tiled=True)]
    all_to_all x1, waiting for transfers between devices: 35.4 us -> 6.04 us  [local(): lax.all_to_all(act_part.reshape(n_shard, -1, act_part.shape[1]), 'shard',...]
    all_gather x1 -> x0, waiting for transfers between devices: 22.8 us -> none  [local(): grads = lax.all_gather(grad_piece, 'dp', axis=0, tiled=True)]
    all_to_all x1, waiting for transfers between devices: 8.87 us -> 1.22 us  [local(): lax.all_to_all(sums, 'shard', 0, 0, tiled=True).reshape(act_part.shape)]
    ppermute x2 -> x10, starting transfers between devices: 4.03 us -> 11.7 us  [the longest x6 5.35 us: along_y(): lax.ppermute(piece, 'dp', [(d, (d + 2 * k) % n_dp) for d in range(n_dp)])]
    all_to_all x0 -> x1, starting transfers between devices: none -> 7.48 us  [local(): lax.all_to_all(pack_acts(where, query_act, buffer_act, n_dp), 'dp', 0, 0,...]
    all_to_all x0 -> x1, waiting for transfers between devices: none -> 5.59 us  [local(): lax.all_to_all(pack_acts(where, query_act, buffer_act, n_dp), 'dp', 0, 0,...]
  transfers between devices with their start and end apart: 5 -> 13, of which waited for: 5 -> 13; matrix products, arithmetic and copies ran while one was open for 0% -> 0% of each run, Pallas kernels for 1% -> 6%
where the time goes in v2:
time: 155 us; the launch traced here: 154 us
  waiting for transfers between devices  68.2 us (44%)
  starting transfers between devices  33.7 us (22%)
  Pallas kernels  27.4 us (18%)
  blocking collectives  20.6 us (13%)
  local copies, waits for them, and re-layouts  3.74 us (2%)
    ppermute x6, waiting for transfers between devices, along_y(): lax.ppermute(piece, 'dp', [(d, (d + 2 * k) % n_dp) for d in range(n_dp)])  31.9 us
    all_to_all x1, blocking collectives, local(): lax.all_to_all(jnp.broadcast_to(mine[None, :1], (count, 1, 128)), ('shard...  20.6 us
    pallas_call x1, Pallas kernels, tile_scores(): pl.pallas_call(scores_kernel, grid_spec=grid_spec, out_shape=jax.ShapeDty...  10.9 us
    ppermute x1, waiting for transfers between devices, local(): pair = pair_grads(where, piece, lax.ppermute(piece, 'dp', partner))  10.8 us
    ppermute x1, waiting for transfers between devices, local(): sums, piece = add_parts(parts, keep, lax.ppermute(send, 'dp', partner))  9.71 us
    all_to_all x1, starting transfers between devices, local(): lax.all_to_all(act_part.reshape(n_shard, -1, act_part.shape[1]), 'shard',...  8.46 us
    pallas_call x1, Pallas kernels, rotate_grad(): pl.pallas_call(rotate_grad_kernel, grid_spec=grid_spec, out_shape=[jax.Sh...  7.59 us
    all_to_all x1, starting transfers between devices, local(): lax.all_to_all(pack_acts(where, query_act, buffer_act, n_dp), 'dp', 0, 0,...  7.48 us
  transfers between devices with their start and end apart: 13, of which 13 were waited for; matrix products, arithmetic and copies ran while one was open for 0% of the time, Pallas kernels for 6%

profile of v2, /device:TPU:1, one launch (start us, length us, event | category | flops | bytes accessed | tf_op | source)
XLA Modules:
  0.0 154.4 jit_solution(2944986101549483574)
XLA Ops:
  0.0 0.6 pad_add_fusion.core_ref.where_ref
  0.6 2.4 %pack_acts.1 = bf16[8,96,512]{2,1,0:T(8,128)(2,1)} custom-call(s32[3]{0:T(128)} %pad_add_fusion.core_ref.where_ref, bf16[4,16,512]{2,1,0:T(8,128)(2,1)} %qa_ref.1, bf16[4,16,512]{2,1,0:T(8,128)(2,1)} %ba_ref.1), custom_call_target="tpu_custom_call" | custom-call | bytes 2097152 | tf_op jit(solution)/shard_map/pack_acts/pallas_call | solution.py:42
  3.0 7.5 %all-to-all-start = ((bf16[8,96,512]{2,1,0:T(8,128)(2,1)}), bf16[8,96,512]{2,1,0:T(8,128)(2,1)S(1)}, u32[]{:S(2)}, u32[]{:S(2)}) async-start(bf16[8,96,512]{2,1,0:T(8,128)(2,1)} %pack_acts.1), calls=%async_computation | async-start | bytes 1572864 | tf_op jit(solution)/shard_map/all_to_all | solution.py:364
  10.5 0.0 copy-start.2
  10.5 7.6 %rotate_grad.1 = (bf16[224,768]{1,0:T(8,128)(2,1)}, bf16[224,768]{1,0:T(8,128)(2,1)}, bf16[224,768]{1,0:T(8,128)(2,1)}, bf16[224,768]{1,0:T(8,128)(2,1)}) custom-call(s32[3]{0:T(128)} %pad_add_fusion.core_ref.where_ref, bf16[4,128,1792]{2,1,0:T(8,128)(2,1)} %qg_ref.1, bf16[4,128,1792]{2,1,0:T(8,128)(2,1)} %bg_ref.1, bf16[896,1792]{1,0:T(8,128)(2,1)} %basis_ref.2), custom_call_target="tpu_custom_call" | custom-call | flops 2466250752 | bytes 8388608 | tf_op jit(solution)/shard_map/rotate_grad/pallas_call | solution.py:88
  18.1 5.6 %all-to-all-done.recv_ref = bf16[8,96,512]{2,1,0:T(8,128)(2,1)S(1)} async-done(((bf16[8,96,512]{2,1,0:T(8,128)(2,1)}), bf16[8,96,512]{2,1,0:T(8,128)(2,1)S(1)}, u32[]{:S(2)}, u32[]{:S(2)}) %all-to-all-start) | async-done | bytes 786464 | tf_op jit(solution)/shard_map/all_to_all | solution.py:364
  23.7 0.0 copy-done.2
  23.7 0.0 copy-start
  23.7 1.0 copy-done
  24.7 2.8 %rotate_act.1 = bf16[768,1024]{1,0:T(8,128)(2,1)} custom-call(bf16[8,96,512]{2,1,0:T(8,128)(2,1)S(1)} %all-to-all-done.recv_ref, bf16[1024,512]{1,0:T(8,128)(2,1)S(1)} %copy-done.2, bf16[224,768]{1,0:T(8,128)(2,1)S(1)} %copy-done), custom_call_target="tpu_custom_call" | custom-call | flops 805306368 | bytes 6291456 | tf_op jit(solution)/shard_map/rotate_act/pallas_call | solution.py:199
  27.5 0.0 copy-start.7
  27.5 0.0 copy-start.6
  27.5 0.0 copy-start.5
  27.5 0.0 copy-start.1
  27.5 0.0 copy-start.3
  27.5 8.5 %all-to-all-start.1 = ((bf16[16,48,1024]{2,1,0:T(8,128)(2,1)}), bf16[16,48,1024]{2,1,0:T(8,128)(2,1)S(1)}, u32[]{:S(2)}, u32[]{:S(2)}) async-start(bf16[16,48,1024]{2,1,0:T(8,128)(2,1)} %bitcast.3), calls=%async_computation.1 | async-start | bytes 3145728 | tf_op jit(solution)/shard_map/all_to_all | solution.py:367
  36.0 0.0 copy-done.7
  36.0 0.1 collective-permute-start
  36.1 0.0 copy-done.6
  36.1 2.0 %collective-permute-start.1 = (bf16[224,768]{1,0:T(8,128)(2,1)S(1)}, bf16[224,768]{1,0:T(8,128)(2,1)S(1)}, u32[]{:S(2)}, u32[]{:S(2)}) collective-permute-start(bf16[224,768]{1,0:T(8,128)(2,1)S(1)} %copy-done.6), channel_id=1, source_target_pairs={{0,8},{2,10},{4,12},{6,14},{8,0},{10,2},{12,4},{14,6},{1,9},{3,11}... | collective-permute-start | bytes 1032200 | tf_op jit(solution)/shard_map/ppermute | solution.py:362
  38.1 0.0 copy-done.5
  38.1 0.9 collective-permute-start.2
  39.0 5.6 %collective-permute-done.refs_1_ = bf16[224,768]{1,0:T(8,128)(2,1)S(1)} collective-permute-done((bf16[224,768]{1,0:T(8,128)(2,1)S(1)}, bf16[224,768]{1,0:T(8,128)(2,1)S(1)}, u32[]{:S(2)}, u32[]{:S(2)}) %collective-permute-start) | collective-permute-done | bytes 344096 | tf_op jit(solution)/shard_map/ppermute | solution.py:362
  44.6 6.9 %collective-permute-done.1.refs_2_ = bf16[224,768]{1,0:T(8,128)(2,1)S(1)} collective-permute-done((bf16[224,768]{1,0:T(8,128)(2,1)S(1)}, bf16[224,768]{1,0:T(8,128)(2,1)S(1)}, u32[]{:S(2)}, u32[]{:S(2)}) %collective-permute-start.1) | collective-permute-done | bytes 344096 | tf_op jit(solution)/shard_map/ppermute | solution.py:362
  51.5 2.6 %collective-permute-done.2.refs_3_ = bf16[224,768]{1,0:T(8,128)(2,1)S(1)} collective-permute-done((bf16[224,768]{1,0:T(8,128)(2,1)S(1)}, bf16[224,768]{1,0:T(8,128)(2,1)S(1)}, u32[]{:S(2)}, u32[]{:S(2)}) %collective-permute-start.2) | collective-permute-done | bytes 344096 | tf_op jit(solution)/shard_map/ppermute | solution.py:362
  54.1 0.0 copy-done.1
  54.2 0.0 copy-done.3
  54.2 0.9 add_grads.1
  55.0 1.3 collective-permute-start.3
  56.3 9.7 %collective-permute-done.3.came_ref = bf16[112,768]{1,0:T(8,128)(2,1)S(1)} collective-permute-done((bf16[112,768]{1,0:T(8,128)(2,1)S(1)}, bf16[112,768]{1,0:T(8,128)(2,1)S(1)}, u32[]{:S(2)}, u32[]{:S(2)}) %collective-permute-start.3) | collective-permute-done | bytes 172064 | tf_op jit(solution)/shard_map/ppermute | solution.py:369
  66.1 6.0 %all-to-all-done.1.parts_ref = bf16[16,48,1024]{2,1,0:T(8,128)(2,1)S(1)} async-done(((bf16[16,48,1024]{2,1,0:T(8,128)(2,1)}), bf16[16,48,1024]{2,1,0:T(8,128)(2,1)S(1)}, u32[]{:S(2)}, u32[]{:S(2)}) %all-to-all-start.1) | async-done | bytes 1572896 | tf_op jit(solution)/shard_map/all_to_all | solution.py:367
  72.1 1.5 add_parts.1
  73.6 6.1 %all-to-all-start.2 = ((bf16[16,48,1024]{2,1,0:T(8,128)(2,1)}), bf16[16,48,1024]{2,1,0:T(8,128)(2,1)S(1)}, u32[]{:S(2)}, u32[]{:S(2)}) async-start(bf16[16,48,1024]{2,1,0:T(8,128)(2,1)} %get-tuple-element.24), calls=%async_computation.2 | async-start | bytes 3145728 | tf_op jit(solution)/shard_map/all_to_all | solution.py:370
  79.7 1.3 collective-permute-start.4
  81.0 10.8 %collective-permute-done.4.other_ref = bf16[112,768]{1,0:T(8,128)(2,1)S(1)} collective-permute-done((bf16[112,768]{1,0:T(8,128)(2,1)S(1)}, bf16[112,768]{1,0:T(8,128)(2,1)S(1)}, u32[]{:S(2)}, u32[]{:S(2)}) %collective-permute-start.4) | collective-permute-done | bytes 172064 | tf_op jit(solution)/shard_map/ppermute | solution.py:371
  91.7 0.6 pair_grads.1.refs_0_
  92.3 0.8 collective-permute-start.7
  93.1 1.5 %collective-permute-start.6 = (bf16[224,768]{1,0:T(8,128)(2,1)S(1)}, bf16[224,768]{1,0:T(8,128)(2,1)S(1)}, u32[]{:S(2)}, u32[]{:S(2)}) collective-permute-start(bf16[224,768]{1,0:T(8,128)(2,1)S(1)} %pair_grads.1.refs_0_), channel_id=1, source_target_pairs={{0,8},{2,10},{4,12},{6,14},{8,0},{10,2},{12,4},{14,6},{1,9},{3,11}... | collective-permute-start | bytes 1032200 | tf_op jit(solution)/shard_map/ppermute | solution.py:362
  94.6 0.0 collective-permute-start.5
  94.6 5.1 %collective-permute-done.7.refs_3_ = bf16[224,768]{1,0:T(8,128)(2,1)S(1)} collective-permute-done((bf16[224,768]{1,0:T(8,128)(2,1)S(1)}, bf16[224,768]{1,0:T(8,128)(2,1)S(1)}, u32[]{:S(2)}, u32[]{:S(2)}) %collective-permute-start.7) | collective-permute-done | bytes 344096 | tf_op jit(solution)/shard_map/ppermute | solution.py:362
  99.7 1.4 collective-permute-done.6.refs_2_
  101.1 10.3 %collective-permute-done.5.refs_1_ = bf16[224,768]{1,0:T(8,128)(2,1)S(1)} collective-permute-done((bf16[224,768]{1,0:T(8,128)(2,1)S(1)}, bf16[224,768]{1,0:T(8,128)(2,1)S(1)}, u32[]{:S(2)}, u32[]{:S(2)}) %collective-permute-start.5) | collective-permute-done | bytes 344096 | tf_op jit(solution)/shard_map/ppermute | solution.py:362
  111.4 0.7 join_grads.1
  112.1 1.1 collective-permute-start.8
  113.2 1.4 collective-permute-done.8.after_ref.go_ref
  114.6 1.2 all-to-all-done.2
  115.9 0.1 query_rows.1
  115.9 2.6 %collective-permute-start.9 = (bf16[256,1024]{1,0:T(8,128)(2,1)S(1)}, bf16[256,1024]{1,0:T(8,128)(2,1)S(1)}, u32[]{:S(2)}, u32[]{:S(2)}) collective-permute-start(bf16[256,1024]{1,0:T(8,128)(2,1)S(1)} %query_rows.1), channel_id=1, source_target_pairs={{0,1},{1,0},{2,3},{3,2},{4,5},{5,4},{6,7},{7,6},{8,9},{9,8},{10,11... | collective-permute-start | bytes 1572872 | tf_op jit(solution)/shard_map/ppermute | solution.py:374
  118.6 1.5 collective-permute-done.9.ao_ref
  120.1 0.0 copy-start.4
  120.1 2.0 %copy-done.4 = f32[896,1024]{1,0:T(8,128)S(1)} copy-done((f32[896,1024]{1,0:T(8,128)S(1)}, f32[896,1024]{1,0:T(8,128)}, u32[]{:S(2)}) %copy-start.4) | copy-done | bytes 3670040
  122.2 10.9 %tile_scores.1 = f32[8,128]{1,0:T(8,128)S(1)} custom-call(s32[3]{0:T(128)S(1)} %copy-done.3, bf16[896,768]{1,0:T(8,128)(2,1)S(1)} %get-tuple-element.22.g_ref, bf16[896,256]{1,0:T(8,128)(2,1)S(1)} %collective-permute-done.8.after_ref.go_ref, bf16[768,1024]{1,0:T(8,128)(2,1)S(1)} %bitcast.10, bf16[256,1024]{1,0:T(8,128)(2,1)S(1)} %collective-permute-done.9.ao_ref, ...), custom_call_target="tpu_custom_call" | custom-call | flops 3758096384 | bytes 8388608 | tf_op jit(solution)/shard_map/tile_scores/pallas_call | solution.py:342
  133.1 20.6 %all_to_all.20 = f32[128,1,128]{2,1,0:T(1,128)S(1)} all-to-all(f32[128,1,128]{2,1,0:T(1,128)S(1)} %broadcast_in_dim.9), channel_id=1, replica_groups=mesh['shard'=16,'dp'=8,'buffer'=2] {'shard','dp'}, dimensions={0} | all-to-all | bytes 131072 | tf_op jit(solution)/shard_map/all_to_all | solution.py:377
  153.8 0.7 reshape.22
  (3 shorter events, 0.1 us)
Async XLA Ops:
  3.0 20.7 %all-to-all-start = ((bf16[8,96,512]{2,1,0:T(8,128)(2,1)}), bf16[8,96,512]{2,1,0:T(8,128)(2,1)S(1)}, u32[]{:S(2)}, u32[]{:S(2)}) async-start(bf16[8,96,512]{2,1,0:T(8,128)(2,1)} %pack_acts.1), calls=%async_computation | async-start | bytes 1572864 | tf_op jit(solution)/shard_map/all_to_all | solution.py:364
  10.5 13.2 %copy-start.2 = (bf16[1024,512]{1,0:T(8,128)(2,1)S(1)}, bf16[1024,512]{1,0:T(8,128)(2,1)}, u32[]{:S(2)}) copy-start(bf16[1024,512]{1,0:T(8,128)(2,1)} %basis_ref.3) | copy-start | bytes 3145732
  23.7 1.0 copy-start
  27.5 8.5 %copy-start.7 = (bf16[224,768]{1,0:T(8,128)(2,1)S(1)}, bf16[224,768]{1,0:T(8,128)(2,1)}, u32[]{:S(2)}) copy-start(bf16[224,768]{1,0:T(8,128)(2,1)} %get-tuple-element.16) | copy-start | bytes 1032196
  27.5 8.6 %copy-start.6 = (bf16[224,768]{1,0:T(8,128)(2,1)S(1)}, bf16[224,768]{1,0:T(8,128)(2,1)}, u32[]{:S(2)}) copy-start(bf16[224,768]{1,0:T(8,128)(2,1)} %get-tuple-element.17) | copy-start | bytes 1032196
  27.5 10.6 %copy-start.5 = (bf16[224,768]{1,0:T(8,128)(2,1)S(1)}, bf16[224,768]{1,0:T(8,128)(2,1)}, u32[]{:S(2)}) copy-start(bf16[224,768]{1,0:T(8,128)(2,1)} %get-tuple-element.18) | copy-start | bytes 1032196
  27.5 26.6 %copy-start.1 = (bf16[224,768]{1,0:T(8,128)(2,1)S(1)}, bf16[224,768]{1,0:T(8,128)(2,1)}, u32[]{:S(2)}) copy-start(bf16[224,768]{1,0:T(8,128)(2,1)} %get-tuple-element.15.after_ref.refs_0_) | copy-start | bytes 1032196
  27.5 26.6 %copy-start.3 = (s32[3]{0:T(128)S(1)}, s32[3]{0:T(128)}, u32[]{:S(2)}) copy-start(s32[3]{0:T(128)} %pad_add_fusion.core_ref.where_ref) | copy-start | bytes 40
  27.5 44.6 %all-to-all-start.1 = ((bf16[16,48,1024]{2,1,0:T(8,128)(2,1)}), bf16[16,48,1024]{2,1,0:T(8,128)(2,1)S(1)}, u32[]{:S(2)}, u32[]{:S(2)}) async-start(bf16[16,48,1024]{2,1,0:T(8,128)(2,1)} %bitcast.3), calls=%async_computation.1 | async-start | bytes 3145728 | tf_op jit(solution)/shard_map/all_to_all | solution.py:367
  36.0 8.7 %collective-permute-start = (bf16[224,768]{1,0:T(8,128)(2,1)S(1)}, bf16[224,768]{1,0:T(8,128)(2,1)S(1)}, u32[]{:S(2)}, u32[]{:S(2)}) collective-permute-start(bf16[224,768]{1,0:T(8,128)(2,1)S(1)} %copy-done.7), channel_id=1, source_target_pairs={{0,4},{2,6},{4,8},{6,10},{8,12},{10,14},{12,0},{14,2},{1,5},{3,7},... | collective-permute-start | bytes 1032200 | tf_op jit(solution)/shard_map/ppermute | solution.py:362
  36.1 15.4 %collective-permute-start.1 = (bf16[224,768]{1,0:T(8,128)(2,1)S(1)}, bf16[224,768]{1,0:T(8,128)(2,1)S(1)}, u32[]{:S(2)}, u32[]{:S(2)}) collective-permute-start(bf16[224,768]{1,0:T(8,128)(2,1)S(1)} %copy-done.6), channel_id=1, source_target_pairs={{0,8},{2,10},{4,12},{6,14},{8,0},{10,2},{12,4},{14,6},{1,9},{3,11}... | collective-permute-start | bytes 1032200 | tf_op jit(solution)/shard_map/ppermute | solution.py:362
  38.1 16.0 %collective-permute-start.2 = (bf16[224,768]{1,0:T(8,128)(2,1)S(1)}, bf16[224,768]{1,0:T(8,128)(2,1)S(1)}, u32[]{:S(2)}, u32[]{:S(2)}) collective-permute-start(bf16[224,768]{1,0:T(8,128)(2,1)S(1)} %copy-done.5), channel_id=1, source_target_pairs={{0,12},{2,14},{4,0},{6,2},{8,4},{10,6},{12,8},{14,10},{1,13},{3,15... | collective-permute-start | bytes 1032200 | tf_op jit(solution)/shard_map/ppermute | solution.py:362
  55.0 11.0 %collective-permute-start.3 = (bf16[112,768]{1,0:T(8,128)(2,1)S(1)}, bf16[112,768]{1,0:T(8,128)(2,1)S(1)}, u32[]{:S(2)}, u32[]{:S(2)}) collective-permute-start(bf16[112,768]{1,0:T(8,128)(2,1)S(1)} %get-tuple-element.20), channel_id=1, source_target_pairs={{0,2},{2,0},{4,6},{6,4},{8,10},{10,8},{12,14},{14,12},{1,3},{3,1},... | collective-permute-start | bytes 516104 | tf_op jit(solution)/shard_map/ppermute | solution.py:369
  73.6 42.3 %all-to-all-start.2 = ((bf16[16,48,1024]{2,1,0:T(8,128)(2,1)}), bf16[16,48,1024]{2,1,0:T(8,128)(2,1)S(1)}, u32[]{:S(2)}, u32[]{:S(2)}) async-start(bf16[16,48,1024]{2,1,0:T(8,128)(2,1)} %get-tuple-element.24), calls=%async_computation.2 | async-start | bytes 3145728 | tf_op jit(solution)/shard_map/all_to_all | solution.py:370
  79.7 12.0 %collective-permute-start.4 = (bf16[112,768]{1,0:T(8,128)(2,1)S(1)}, bf16[112,768]{1,0:T(8,128)(2,1)S(1)}, u32[]{:S(2)}, u32[]{:S(2)}) collective-permute-start(bf16[112,768]{1,0:T(8,128)(2,1)S(1)} %get-tuple-element.21.own_ref), channel_id=1, source_target_pairs={{0,2},{2,0},{4,6},{6,4},{8,10},{10,8},{12,14},{14,12},{1,3},{3,1},... | collective-permute-start | bytes 516104 | tf_op jit(solution)/shard_map/ppermute | solution.py:371
  92.3 7.4 %collective-permute-start.7 = (bf16[224,768]{1,0:T(8,128)(2,1)S(1)}, bf16[224,768]{1,0:T(8,128)(2,1)S(1)}, u32[]{:S(2)}, u32[]{:S(2)}) collective-permute-start(bf16[224,768]{1,0:T(8,128)(2,1)S(1)} %pair_grads.1.refs_0_), channel_id=1, source_target_pairs={{0,12},{2,14},{4,0},{6,2},{8,4},{10,6},{12,8},{14,10},{1,13},{3,15... | collective-permute-start | bytes 1032200 | tf_op jit(solution)/shard_map/ppermute | solution.py:362
  93.1 8.0 %collective-permute-start.6 = (bf16[224,768]{1,0:T(8,128)(2,1)S(1)}, bf16[224,768]{1,0:T(8,128)(2,1)S(1)}, u32[]{:S(2)}, u32[]{:S(2)}) collective-permute-start(bf16[224,768]{1,0:T(8,128)(2,1)S(1)} %pair_grads.1.refs_0_), channel_id=1, source_target_pairs={{0,8},{2,10},{4,12},{6,14},{8,0},{10,2},{12,4},{14,6},{1,9},{3,11}... | collective-permute-start | bytes 1032200 | tf_op jit(solution)/shard_map/ppermute | solution.py:362
  94.6 16.8 %collective-permute-start.5 = (bf16[224,768]{1,0:T(8,128)(2,1)S(1)}, bf16[224,768]{1,0:T(8,128)(2,1)S(1)}, u32[]{:S(2)}, u32[]{:S(2)}) collective-permute-start(bf16[224,768]{1,0:T(8,128)(2,1)S(1)} %pair_grads.1.refs_0_), channel_id=1, source_target_pairs={{0,4},{2,6},{4,8},{6,10},{8,12},{10,14},{12,0},{14,2},{1,5},{3,7},... | collective-permute-start | bytes 1032200 | tf_op jit(solution)/shard_map/ppermute | solution.py:362
  112.1 2.5 %collective-permute-start.8 = (bf16[896,256]{1,0:T(8,128)(2,1)S(1)}, bf16[896,256]{1,0:T(8,128)(2,1)S(1)}, u32[]{:S(2)}, u32[]{:S(2)}) collective-permute-start(bf16[896,256]{1,0:T(8,128)(2,1)S(1)} %get-tuple-element.23), channel_id=1, source_target_pairs={{0,1},{1,0},{2,3},{3,2},{4,5},{5,4},{6,7},{7,6},{8,9},{9,8},{10,11... | collective-permute-start | bytes 1376264 | tf_op jit(solution)/shard_map/ppermute | solution.py:373
  115.9 4.2 %collective-permute-start.9 = (bf16[256,1024]{1,0:T(8,128)(2,1)S(1)}, bf16[256,1024]{1,0:T(8,128)(2,1)S(1)}, u32[]{:S(2)}, u32[]{:S(2)}) collective-permute-start(bf16[256,1024]{1,0:T(8,128)(2,1)S(1)} %query_rows.1), channel_id=1, source_target_pairs={{0,1},{1,0},{2,3},{3,2},{4,5},{5,4},{6,7},{7,6},{8,9},{9,8},{10,11... | collective-permute-start | bytes 1572872 | tf_op jit(solution)/shard_map/ppermute | solution.py:374
  120.1 2.0 %copy-start.4 = (f32[896,1024]{1,0:T(8,128)S(1)}, f32[896,1024]{1,0:T(8,128)}, u32[]{:S(2)}) copy-start(f32[896,1024]{1,0:T(8,128)} %eig_ref.1) | copy-start | bytes 11010052

commit v3 on v2

--- a/solution.py
+++ b/solution.py
@@ -14,6 +14,9 @@
 F32 = jnp.float32
 BF16 = jnp.bfloat16
 NT = (((1,), (1,)), ((), ()))
+
+
+TOKEN = pl.BlockSpec((16, 128), lambda *_: (0, 0))
 
 
 def params(mib):
@@ -202,7 +205,7 @@
         in_specs=[
             pl.BlockSpec((n_dp, rows, inner), lambda i: (0, 0, 0)),
             pl.BlockSpec((256, inner), lambda i: (i, 0)),
-            pl.BlockSpec(memory_space=pl.ANY),
+            TOKEN,
         ],
         out_specs=pl.BlockSpec((768, 256), lambda i: (0, i)),
         out_shape=jax.ShapeDtypeStruct((768, outer), BF16),
@@ -255,7 +258,7 @@
     return pl.pallas_call(
         query_rows_kernel,
         grid=(2,),
-        in_specs=[pl.BlockSpec((rows // 2, width), lambda i: (i, 0)), pl.BlockSpec(memory_space=pl.ANY)],
+        in_specs=[pl.BlockSpec((rows // 2, width), lambda i: (i, 0)), TOKEN],
         out_specs=pl.BlockSpec((rows // 2, width), lambda i: (i, 0)),
         out_shape=jax.ShapeDtypeStruct((rows, width), BF16),
         compiler_params=params(40),
@@ -267,77 +270,49 @@
 PIECE = 64
 
 
-def scores_kernel(core_ref, g_ref, go_ref, a_ref, ao_ref, eig_ref, out_ref, inverse, left, right, total):
-    step = pl.program_id(0)
-    eigen = g_ref.shape[0]
-    width = a_ref.shape[1]
-    inverse[...] = 1.0 / (eig_ref[...] + DAMPING)
-
-    def tile(grads, acts, n):
+def scores_kernel(core_ref, g_ref, go_ref, a_ref, ao_ref, eig_ref, out_ref, left, right):
+    eigen, width = eig_ref.shape
+
+    def tile(grads, acts, rows, n):
         part = slice(n * T_SIZE, (n + 1) * T_SIZE)
-        return jnp.dot(grads[:, part], acts[part, :], preferred_element_type=F32)
-
-    def keep(ref, slot, block):
-        for c in range(eigen // PIECE):
-            ref[slot * PIECE:(slot + 1) * PIECE, c * width:(c + 1) * width] = block[c * PIECE:(c + 1) * PIECE, :]
-
-    for i in range(2):
-        keep(left, i, (tile(g_ref, a_ref, i) * inverse[...]).astype(BF16))
-    for j in range(4):
-        keep(right, j, tile(g_ref, a_ref, 2 + j).astype(BF16))
-    for i in range(2):
-        keep(left, 2 + i, (tile(go_ref, ao_ref, i) * inverse[...]).astype(BF16))
+        return jnp.dot(grads[rows, part], acts[part, :], preferred_element_type=F32)
+
+    for c in range(eigen // PIECE):
+        rows = slice(c * PIECE, (c + 1) * PIECE)
+        columns = slice(c * width, (c + 1) * width)
+        inverse = 1.0 / (eig_ref[rows, :] + DAMPING)
+        for i in range(2):
+            left[i * PIECE:(i + 1) * PIECE, columns] = (tile(g_ref, a_ref, rows, i) * inverse).astype(BF16)
+            left[(2 + i) * PIECE:(3 + i) * PIECE, columns] = (tile(go_ref, ao_ref, rows, i) * inverse).astype(BF16)
+        for j in range(4):
+            right[j * PIECE:(j + 1) * PIECE, columns] = tile(g_ref, a_ref, rows, 2 + j).astype(BF16)
     product = lax.dot_general(left[...], right[...], NT, preferred_element_type=F32)
-
-    @pl.when(step == 0)
-    def _():
-        total[...] = product
-
-    @pl.when(step > 0)
-    def _():
-        total[...] += product
-
-    @pl.when(step == pl.num_programs(0) - 1)
-    def _():
-        size = total.shape[0]
-        row = lax.broadcasted_iota(jnp.int32, (size, size), 0)
-        column = lax.broadcasted_iota(jnp.int32, (size, size), 1)
-        own = jnp.where(row % PIECE == column % PIECE, total[...], 0.0)
-        lane = lax.broadcasted_iota(jnp.int32, (1, size), 1)
-        place = lax.broadcasted_iota(jnp.int32, (8, 128), 1)
-        result = jnp.zeros((8, 128), F32)
-        for i in range(4):
-            line = jnp.sum(own[i * PIECE:(i + 1) * PIECE, :], axis=0, keepdims=True)
-            query = (i + 2 * core_ref[0]) % 4
-            for j in range(4):
-                value = jnp.sum(jnp.where(lane // PIECE == j, line, 0.0), axis=1, keepdims=True) * NORM
-                result = result + jnp.where(place == query * 4 + j, value, 0.0)
-        out_ref[...] = result
+    size = product.shape[0]
+    row = lax.broadcasted_iota(jnp.int32, (size, size), 0)
+    column = lax.broadcasted_iota(jnp.int32, (size, size), 1)
+    own = jnp.where(row % PIECE == column % PIECE, product, 0.0)
+    lane = lax.broadcasted_iota(jnp.int32, (1, size), 1)
+    place = lax.broadcasted_iota(jnp.int32, (8, 128), 1)
+    result = jnp.zeros((8, 128), F32)
+    for i in range(4):
+        line = jnp.sum(own[i * PIECE:(i + 1) * PIECE, :], axis=0, keepdims=True)
+        query = (i + 2 * core_ref[0]) % 4
+        for j in range(4):
+            value = jnp.sum(jnp.where(lane // PIECE == j, line, 0.0), axis=1, keepdims=True) * NORM
+            result = result + jnp.where(place == query * 4 + j, value, 0.0)
+    out_ref[...] = result
 
 
 def tile_scores(core, grads, grads_other, acts, acts_other, eigenvalues):
-    eigen = grads.shape[0]
-    rows = acts.shape[0]
-    width = eigenvalues.shape[1]
-    block = 256
-    pieces = eigen // PIECE
-    grid_spec = pltpu.PrefetchScalarGridSpec(
-        num_scalar_prefetch=1,
-        grid=(width // block,),
-        in_specs=[
-            pl.BlockSpec(grads.shape, lambda i, c: (0, 0)),
-            pl.BlockSpec(grads_other.shape, lambda i, c: (0, 0)),
-            pl.BlockSpec((rows, block), lambda i, c: (0, i)),
-            pl.BlockSpec((256, block), lambda i, c: (0, i)),
-            pl.BlockSpec((eigen, block), lambda i, c: (0, i)),
-        ],
+    eigen, width = eigenvalues.shape
+    operands = (grads, grads_other, acts, acts_other, eigenvalues)
+    scratch = pltpu.VMEM((4 * PIECE, eigen // PIECE * width), BF16)
+    grid_spec = pltpu.PrefetchScalarGridSpec(
+        num_scalar_prefetch=1,
+        grid=(1,),
+        in_specs=[pl.BlockSpec(operand.shape, lambda i, c: (0, 0)) for operand in operands],
         out_specs=pl.BlockSpec((8, 128), lambda i, c: (0, 0)),
-        scratch_shapes=[
-            pltpu.VMEM((eigen, block), F32),
-            pltpu.VMEM((4 * PIECE, pieces * block), BF16),
-            pltpu.VMEM((4 * PIECE, pieces * block), BF16),
-            pltpu.VMEM((4 * PIECE, 4 * PIECE), F32),
-        ],
+        scratch_shapes=[scratch, scratch],
     )
     return pl.pallas_call(
         scores_kernel,
@@ -346,7 +321,7 @@
         compiler_params=params(40),
         cost_estimate=pl.CostEstimate(flops=4 * 8 * T_SIZE * eigen * width, bytes_accessed=8 * 1024 * 1024, transcendentals=0),
         name="tile_scores",
-    )(core, grads, grads_other, acts, acts_other, eigenvalues)
+    )(core, *operands)
 
 
 def local(query_grad, query_act, buffer_grad, buffer_act, grad_basis, act_basis, eigenvalues):

time: 155 us -> 151 us (0.974)
  Pallas kernels: 27.4 us -> 23.3 us
    pallas_call x1, Pallas kernels: 10.9 us -> 6.84 us  [tile_scores(): pl.pallas_call(scores_kernel, grid_spec=grid_spec, out_shape=jax.ShapeDty...]
where the time goes in v3:
time: 151 us
  waiting for transfers between devices  68.2 us (45%)
  starting transfers between devices  33.9 us (22%)
  Pallas kernels  23.3 us (15%)
  blocking collectives  20.6 us (14%)
  local copies, waits for them, and re-layouts  3.75 us (2%)
    ppermute x6, waiting for transfers between devices, along_y(): lax.ppermute(piece, 'dp', [(d, (d + 2 * k) % n_dp) for d in range(n_dp)])  31.9 us
    all_to_all x1, blocking collectives, local(): lax.all_to_all(jnp.broadcast_to(mine[None, :1], (count, 1, 128)), ('shard...  20.6 us
    ppermute x1, waiting for transfers between devices, local(): pair = pair_grads(where, piece, lax.ppermute(piece, 'dp', partner))  10.8 us
    ppermute x1, waiting for transfers between devices, local(): sums, piece = add_parts(parts, keep, lax.ppermute(send, 'dp', partner))  9.73 us
    all_to_all x1, starting transfers between devices, local(): lax.all_to_all(act_part.reshape(n_shard, -1, act_part.shape[1]), 'shard',...  8.46 us
    pallas_call x1, Pallas kernels, rotate_grad(): pl.pallas_call(rotate_grad_kernel, grid_spec=grid_spec, out_shape=[jax.Sh...  7.59 us
    all_to_all x1, starting transfers between devices, local(): lax.all_to_all(pack_acts(where, query_act, buffer_act, n_dp), 'dp', 0, 0,...  7.48 us
    pallas_call x1, Pallas kernels, tile_scores(): pl.pallas_call(scores_kernel, grid_spec=grid_spec, out_shape=jax.ShapeDty...  6.84 us
  transfers between devices with their start and end apart: 13, of which 13 were waited for; matrix products, arithmetic and copies ran while one was open for 0% of the time, Pallas kernels for 6%

profile of v3, /device:TPU:1, one launch (start us, length us, event | category | flops | bytes accessed | tf_op | source)
XLA Modules:
  0.0 150.6 jit_solution(16005969461025928578)
XLA Ops:
  0.0 0.6 pad_add_fusion.core_ref.where_ref
  0.6 2.4 %pack_acts.1 = bf16[8,96,512]{2,1,0:T(8,128)(2,1)} custom-call(s32[3]{0:T(128)} %pad_add_fusion.core_ref.where_ref, bf16[4,16,512]{2,1,0:T(8,128)(2,1)} %qa_ref.1, bf16[4,16,512]{2,1,0:T(8,128)(2,1)} %ba_ref.1), custom_call_target="tpu_custom_call" | custom-call | bytes 2097152 | tf_op jit(solution)/shard_map/pack_acts/pallas_call | solution.py:45
  3.0 7.5 %all-to-all-start = ((bf16[8,96,512]{2,1,0:T(8,128)(2,1)}), bf16[8,96,512]{2,1,0:T(8,128)(2,1)S(1)}, u32[]{:S(2)}, u32[]{:S(2)}) async-start(bf16[8,96,512]{2,1,0:T(8,128)(2,1)} %pack_acts.1), calls=%async_computation | async-start | bytes 1572864 | tf_op jit(solution)/shard_map/all_to_all | solution.py:339
  10.5 0.0 copy-start.2
  10.5 7.6 %rotate_grad.1 = (bf16[224,768]{1,0:T(8,128)(2,1)}, bf16[224,768]{1,0:T(8,128)(2,1)}, bf16[224,768]{1,0:T(8,128)(2,1)}, bf16[224,768]{1,0:T(8,128)(2,1)}) custom-call(s32[3]{0:T(128)} %pad_add_fusion.core_ref.where_ref, bf16[4,128,1792]{2,1,0:T(8,128)(2,1)} %qg_ref.1, bf16[4,128,1792]{2,1,0:T(8,128)(2,1)} %bg_ref.1, bf16[896,1792]{1,0:T(8,128)(2,1)} %basis_ref.2), custom_call_target="tpu_custom_call" | custom-call | flops 2466250752 | bytes 8388608 | tf_op jit(solution)/shard_map/rotate_grad/pallas_call | solution.py:91
  18.1 5.6 %all-to-all-done.recv_ref = bf16[8,96,512]{2,1,0:T(8,128)(2,1)S(1)} async-done(((bf16[8,96,512]{2,1,0:T(8,128)(2,1)}), bf16[8,96,512]{2,1,0:T(8,128)(2,1)S(1)}, u32[]{:S(2)}, u32[]{:S(2)}) %all-to-all-start) | async-done | bytes 786464 | tf_op jit(solution)/shard_map/all_to_all | solution.py:339
  23.7 0.0 copy-done.2
  23.7 0.0 copy-start
  23.7 1.0 copy-done
  24.7 2.8 %rotate_act.1 = bf16[768,1024]{1,0:T(8,128)(2,1)} custom-call(bf16[8,96,512]{2,1,0:T(8,128)(2,1)S(1)} %all-to-all-done.recv_ref, bf16[1024,512]{1,0:T(8,128)(2,1)S(1)} %copy-done.2, bf16[224,768]{1,0:T(8,128)(2,1)S(1)} %copy-done), custom_call_target="tpu_custom_call" | custom-call | flops 805306368 | bytes 6291456 | tf_op jit(solution)/shard_map/rotate_act/pallas_call | solution.py:202
  27.5 0.0 copy-start.7
  27.5 0.0 copy-start.6
  27.5 0.0 copy-start.5
  27.5 0.0 copy-start.1
  27.5 0.0 copy-start.3
  27.5 8.5 %all-to-all-start.1 = ((bf16[16,48,1024]{2,1,0:T(8,128)(2,1)}), bf16[16,48,1024]{2,1,0:T(8,128)(2,1)S(1)}, u32[]{:S(2)}, u32[]{:S(2)}) async-start(bf16[16,48,1024]{2,1,0:T(8,128)(2,1)} %bitcast.3), calls=%async_computation.1 | async-start | bytes 3145728 | tf_op jit(solution)/shard_map/all_to_all | solution.py:342
  36.0 0.0 copy-done.7
  36.0 0.1 collective-permute-start
  36.1 0.0 copy-done.6
  36.1 2.0 %collective-permute-start.1 = (bf16[224,768]{1,0:T(8,128)(2,1)S(1)}, bf16[224,768]{1,0:T(8,128)(2,1)S(1)}, u32[]{:S(2)}, u32[]{:S(2)}) collective-permute-start(bf16[224,768]{1,0:T(8,128)(2,1)S(1)} %copy-done.6), channel_id=1, source_target_pairs={{0,8},{2,10},{4,12},{6,14},{8,0},{10,2},{12,4},{14,6},{1,9},{3,11}... | collective-permute-start | bytes 1032200 | tf_op jit(solution)/shard_map/ppermute | solution.py:337
  38.1 0.0 copy-done.5
  38.1 0.9 collective-permute-start.2
  39.0 5.7 %collective-permute-done.refs_1_ = bf16[224,768]{1,0:T(8,128)(2,1)S(1)} collective-permute-done((bf16[224,768]{1,0:T(8,128)(2,1)S(1)}, bf16[224,768]{1,0:T(8,128)(2,1)S(1)}, u32[]{:S(2)}, u32[]{:S(2)}) %collective-permute-start) | collective-permute-done | bytes 344096 | tf_op jit(solution)/shard_map/ppermute | solution.py:337
  44.7 6.8 %collective-permute-done.1.refs_2_ = bf16[224,768]{1,0:T(8,128)(2,1)S(1)} collective-permute-done((bf16[224,768]{1,0:T(8,128)(2,1)S(1)}, bf16[224,768]{1,0:T(8,128)(2,1)S(1)}, u32[]{:S(2)}, u32[]{:S(2)}) %collective-permute-start.1) | collective-permute-done | bytes 344096 | tf_op jit(solution)/shard_map/ppermute | solution.py:337
  51.5 2.7 %collective-permute-done.2.refs_3_ = bf16[224,768]{1,0:T(8,128)(2,1)S(1)} collective-permute-done((bf16[224,768]{1,0:T(8,128)(2,1)S(1)}, bf16[224,768]{1,0:T(8,128)(2,1)S(1)}, u32[]{:S(2)}, u32[]{:S(2)}) %collective-permute-start.2) | collective-permute-done | bytes 344096 | tf_op jit(solution)/shard_map/ppermute | solution.py:337
  54.2 0.0 copy-done.1
  54.2 0.0 copy-done.3
  54.2 0.9 add_grads.1
  55.0 1.3 collective-permute-start.3
  56.4 9.7 %collective-permute-done.3.came_ref = bf16[112,768]{1,0:T(8,128)(2,1)S(1)} collective-permute-done((bf16[112,768]{1,0:T(8,128)(2,1)S(1)}, bf16[112,768]{1,0:T(8,128)(2,1)S(1)}, u32[]{:S(2)}, u32[]{:S(2)}) %collective-permute-start.3) | collective-permute-done | bytes 172064 | tf_op jit(solution)/shard_map/ppermute | solution.py:344
  66.1 6.0 %all-to-all-done.1.parts_ref = bf16[16,48,1024]{2,1,0:T(8,128)(2,1)S(1)} async-done(((bf16[16,48,1024]{2,1,0:T(8,128)(2,1)}), bf16[16,48,1024]{2,1,0:T(8,128)(2,1)S(1)}, u32[]{:S(2)}, u32[]{:S(2)}) %all-to-all-start.1) | async-done | bytes 1572896 | tf_op jit(solution)/shard_map/all_to_all | solution.py:342
  72.1 1.5 add_parts.1
  73.6 6.1 %all-to-all-start.2 = ((bf16[16,48,1024]{2,1,0:T(8,128)(2,1)}), bf16[16,48,1024]{2,1,0:T(8,128)(2,1)S(1)}, u32[]{:S(2)}, u32[]{:S(2)}) async-start(bf16[16,48,1024]{2,1,0:T(8,128)(2,1)} %get-tuple-element.24), calls=%async_computation.2 | async-start | bytes 3145728 | tf_op jit(solution)/shard_map/all_to_all | solution.py:345
  79.7 1.3 collective-permute-start.4
  81.0 10.8 %collective-permute-done.4.other_ref = bf16[112,768]{1,0:T(8,128)(2,1)S(1)} collective-permute-done((bf16[112,768]{1,0:T(8,128)(2,1)S(1)}, bf16[112,768]{1,0:T(8,128)(2,1)S(1)}, u32[]{:S(2)}, u32[]{:S(2)}) %collective-permute-start.4) | collective-permute-done | bytes 172064 | tf_op jit(solution)/shard_map/ppermute | solution.py:346
  91.7 0.6 pair_grads.1.refs_0_
  92.3 0.8 collective-permute-start.7
  93.1 1.6 %collective-permute-start.6 = (bf16[224,768]{1,0:T(8,128)(2,1)S(1)}, bf16[224,768]{1,0:T(8,128)(2,1)S(1)}, u32[]{:S(2)}, u32[]{:S(2)}) collective-permute-start(bf16[224,768]{1,0:T(8,128)(2,1)S(1)} %pair_grads.1.refs_0_), channel_id=1, source_target_pairs={{0,8},{2,10},{4,12},{6,14},{8,0},{10,2},{12,4},{14,6},{1,9},{3,11}... | collective-permute-start | bytes 1032200 | tf_op jit(solution)/shard_map/ppermute | solution.py:337
  94.7 0.0 collective-permute-start.5
  94.7 5.1 %collective-permute-done.7.refs_3_ = bf16[224,768]{1,0:T(8,128)(2,1)S(1)} collective-permute-done((bf16[224,768]{1,0:T(8,128)(2,1)S(1)}, bf16[224,768]{1,0:T(8,128)(2,1)S(1)}, u32[]{:S(2)}, u32[]{:S(2)}) %collective-permute-start.7) | collective-permute-done | bytes 344096 | tf_op jit(solution)/shard_map/ppermute | solution.py:337
  99.8 1.3 collective-permute-done.6.refs_2_
  101.1 10.3 %collective-permute-done.5.refs_1_ = bf16[224,768]{1,0:T(8,128)(2,1)S(1)} collective-permute-done((bf16[224,768]{1,0:T(8,128)(2,1)S(1)}, bf16[224,768]{1,0:T(8,128)(2,1)S(1)}, u32[]{:S(2)}, u32[]{:S(2)}) %collective-permute-start.5) | collective-permute-done | bytes 344096 | tf_op jit(solution)/shard_map/ppermute | solution.py:337
  111.4 0.7 join_grads.1
  112.1 1.1 collective-permute-start.8
  113.2 1.4 collective-permute-done.8.after_ref.go_ref
  114.6 1.2 all-to-all-done.2
  115.9 0.1 query_rows.1
  116.0 2.8 %collective-permute-start.9 = (bf16[256,1024]{1,0:T(8,128)(2,1)S(1)}, bf16[256,1024]{1,0:T(8,128)(2,1)S(1)}, u32[]{:S(2)}, u32[]{:S(2)}) collective-permute-start(bf16[256,1024]{1,0:T(8,128)(2,1)S(1)} %query_rows.1), channel_id=1, source_target_pairs={{0,1},{1,0},{2,3},{3,2},{4,5},{5,4},{6,7},{7,6},{8,9},{9,8},{10,11... | collective-permute-start | bytes 1572872 | tf_op jit(solution)/shard_map/ppermute | solution.py:349
  118.8 1.5 %collective-permute-done.9.ao_ref = bf16[256,1024]{1,0:T(8,128)(2,1)S(1)} collective-permute-done((bf16[256,1024]{1,0:T(8,128)(2,1)S(1)}, bf16[256,1024]{1,0:T(8,128)(2,1)S(1)}, u32[]{:S(2)}, u32[]{:S(2)}) %collective-permute-start.9) | collective-permute-done | bytes 524320 | tf_op jit(solution)/shard_map/ppermute | solution.py:349
  120.3 0.0 copy-start.4
  120.3 2.0 %copy-done.4 = f32[896,1024]{1,0:T(8,128)S(1)} copy-done((f32[896,1024]{1,0:T(8,128)S(1)}, f32[896,1024]{1,0:T(8,128)}, u32[]{:S(2)}) %copy-start.4) | copy-done | bytes 3670040
  122.4 6.8 %tile_scores.1 = f32[8,128]{1,0:T(8,128)S(1)} custom-call(s32[3]{0:T(128)S(1)} %copy-done.3, bf16[896,768]{1,0:T(8,128)(2,1)S(1)} %get-tuple-element.22.g_ref, bf16[896,256]{1,0:T(8,128)(2,1)S(1)} %collective-permute-done.8.after_ref.go_ref, bf16[768,1024]{1,0:T(8,128)(2,1)S(1)} %bitcast.10, bf16[256,1024]{1,0:T(8,128)(2,1)S(1)} %collective-permute-done.9.ao_ref, ...), custom_call_target="tpu_custom_call" | custom-call | flops 3758096384 | bytes 8388608 | tf_op jit(solution)/shard_map/tile_scores/pallas_call | solution.py:317
  129.3 20.6 %all_to_all.20 = f32[128,1,128]{2,1,0:T(1,128)S(1)} all-to-all(f32[128,1,128]{2,1,0:T(1,128)S(1)} %broadcast_in_dim.9), channel_id=1, replica_groups=mesh['shard'=16,'dp'=8,'buffer'=2] {'shard','dp'}, dimensions={0} | all-to-all | bytes 131072 | tf_op jit(solution)/shard_map/all_to_all | solution.py:352
  149.9 0.7 reshape.22
  (3 shorter events, 0.1 us)
Async XLA Ops:
  3.0 20.7 %all-to-all-start = ((bf16[8,96,512]{2,1,0:T(8,128)(2,1)}), bf16[8,96,512]{2,1,0:T(8,128)(2,1)S(1)}, u32[]{:S(2)}, u32[]{:S(2)}) async-start(bf16[8,96,512]{2,1,0:T(8,128)(2,1)} %pack_acts.1), calls=%async_computation | async-start | bytes 1572864 | tf_op jit(solution)/shard_map/all_to_all | solution.py:339
  10.5 13.2 %copy-start.2 = (bf16[1024,512]{1,0:T(8,128)(2,1)S(1)}, bf16[1024,512]{1,0:T(8,128)(2,1)}, u32[]{:S(2)}) copy-start(bf16[1024,512]{1,0:T(8,128)(2,1)} %basis_ref.3) | copy-start | bytes 3145732
  23.7 1.0 copy-start
  27.5 8.5 %copy-start.7 = (bf16[224,768]{1,0:T(8,128)(2,1)S(1)}, bf16[224,768]{1,0:T(8,128)(2,1)}, u32[]{:S(2)}) copy-start(bf16[224,768]{1,0:T(8,128)(2,1)} %get-tuple-element.16) | copy-start | bytes 1032196
  27.5 8.6 %copy-start.6 = (bf16[224,768]{1,0:T(8,128)(2,1)S(1)}, bf16[224,768]{1,0:T(8,128)(2,1)}, u32[]{:S(2)}) copy-start(bf16[224,768]{1,0:T(8,128)(2,1)} %get-tuple-element.17) | copy-start | bytes 1032196
  27.5 10.6 %copy-start.5 = (bf16[224,768]{1,0:T(8,128)(2,1)S(1)}, bf16[224,768]{1,0:T(8,128)(2,1)}, u32[]{:S(2)}) copy-start(bf16[224,768]{1,0:T(8,128)(2,1)} %get-tuple-element.18) | copy-start | bytes 1032196
  27.5 26.7 %copy-start.1 = (bf16[224,768]{1,0:T(8,128)(2,1)S(1)}, bf16[224,768]{1,0:T(8,128)(2,1)}, u32[]{:S(2)}) copy-start(bf16[224,768]{1,0:T(8,128)(2,1)} %get-tuple-element.15.after_ref.refs_0_) | copy-start | bytes 1032196
  27.5 26.7 %copy-start.3 = (s32[3]{0:T(128)S(1)}, s32[3]{0:T(128)}, u32[]{:S(2)}) copy-start(s32[3]{0:T(128)} %pad_add_fusion.core_ref.where_ref) | copy-start | bytes 40
  27.5 44.6 %all-to-all-start.1 = ((bf16[16,48,1024]{2,1,0:T(8,128)(2,1)}), bf16[16,48,1024]{2,1,0:T(8,128)(2,1)S(1)}, u32[]{:S(2)}, u32[]{:S(2)}) async-start(bf16[16,48,1024]{2,1,0:T(8,128)(2,1)} %bitcast.3), calls=%async_computation.1 | async-start | bytes 3145728 | tf_op jit(solution)/shard_map/all_to_all | solution.py:342
  36.0 8.7 %collective-permute-start = (bf16[224,768]{1,0:T(8,128)(2,1)S(1)}, bf16[224,768]{1,0:T(8,128)(2,1)S(1)}, u32[]{:S(2)}, u32[]{:S(2)}) collective-permute-start(bf16[224,768]{1,0:T(8,128)(2,1)S(1)} %copy-done.7), channel_id=1, source_target_pairs={{0,4},{2,6},{4,8},{6,10},{8,12},{10,14},{12,0},{14,2},{1,5},{3,7},... | collective-permute-start | bytes 1032200 | tf_op jit(solution)/shard_map/ppermute | solution.py:337
  36.1 15.4 %collective-permute-start.1 = (bf16[224,768]{1,0:T(8,128)(2,1)S(1)}, bf16[224,768]{1,0:T(8,128)(2,1)S(1)}, u32[]{:S(2)}, u32[]{:S(2)}) collective-permute-start(bf16[224,768]{1,0:T(8,128)(2,1)S(1)} %copy-done.6), channel_id=1, source_target_pairs={{0,8},{2,10},{4,12},{6,14},{8,0},{10,2},{12,4},{14,6},{1,9},{3,11}... | collective-permute-start | bytes 1032200 | tf_op jit(solution)/shard_map/ppermute | solution.py:337
  38.1 16.0 %collective-permute-start.2 = (bf16[224,768]{1,0:T(8,128)(2,1)S(1)}, bf16[224,768]{1,0:T(8,128)(2,1)S(1)}, u32[]{:S(2)}, u32[]{:S(2)}) collective-permute-start(bf16[224,768]{1,0:T(8,128)(2,1)S(1)} %copy-done.5), channel_id=1, source_target_pairs={{0,12},{2,14},{4,0},{6,2},{8,4},{10,6},{12,8},{14,10},{1,13},{3,15... | collective-permute-start | bytes 1032200 | tf_op jit(solution)/shard_map/ppermute | solution.py:337
  55.0 11.0 %collective-permute-start.3 = (bf16[112,768]{1,0:T(8,128)(2,1)S(1)}, bf16[112,768]{1,0:T(8,128)(2,1)S(1)}, u32[]{:S(2)}, u32[]{:S(2)}) collective-permute-start(bf16[112,768]{1,0:T(8,128)(2,1)S(1)} %get-tuple-element.20), channel_id=1, source_target_pairs={{0,2},{2,0},{4,6},{6,4},{8,10},{10,8},{12,14},{14,12},{1,3},{3,1},... | collective-permute-start | bytes 516104 | tf_op jit(solution)/shard_map/ppermute | solution.py:344
  73.6 42.3 %all-to-all-start.2 = ((bf16[16,48,1024]{2,1,0:T(8,128)(2,1)}), bf16[16,48,1024]{2,1,0:T(8,128)(2,1)S(1)}, u32[]{:S(2)}, u32[]{:S(2)}) async-start(bf16[16,48,1024]{2,1,0:T(8,128)(2,1)} %get-tuple-element.24), calls=%async_computation.2 | async-start | bytes 3145728 | tf_op jit(solution)/shard_map/all_to_all | solution.py:345
  79.7 12.0 %collective-permute-start.4 = (bf16[112,768]{1,0:T(8,128)(2,1)S(1)}, bf16[112,768]{1,0:T(8,128)(2,1)S(1)}, u32[]{:S(2)}, u32[]{:S(2)}) collective-permute-start(bf16[112,768]{1,0:T(8,128)(2,1)S(1)} %get-tuple-element.21.own_ref), channel_id=1, source_target_pairs={{0,2},{2,0},{4,6},{6,4},{8,10},{10,8},{12,14},{14,12},{1,3},{3,1},... | collective-permute-start | bytes 516104 | tf_op jit(solution)/shard_map/ppermute | solution.py:346
  92.3 7.5 %collective-permute-start.7 = (bf16[224,768]{1,0:T(8,128)(2,1)S(1)}, bf16[224,768]{1,0:T(8,128)(2,1)S(1)}, u32[]{:S(2)}, u32[]{:S(2)}) collective-permute-start(bf16[224,768]{1,0:T(8,128)(2,1)S(1)} %pair_grads.1.refs_0_), channel_id=1, source_target_pairs={{0,12},{2,14},{4,0},{6,2},{8,4},{10,6},{12,8},{14,10},{1,13},{3,15... | collective-permute-start | bytes 1032200 | tf_op jit(solution)/shard_map/ppermute | solution.py:337
  93.1 8.0 %collective-permute-start.6 = (bf16[224,768]{1,0:T(8,128)(2,1)S(1)}, bf16[224,768]{1,0:T(8,128)(2,1)S(1)}, u32[]{:S(2)}, u32[]{:S(2)}) collective-permute-start(bf16[224,768]{1,0:T(8,128)(2,1)S(1)} %pair_grads.1.refs_0_), channel_id=1, source_target_pairs={{0,8},{2,10},{4,12},{6,14},{8,0},{10,2},{12,4},{14,6},{1,9},{3,11}... | collective-permute-start | bytes 1032200 | tf_op jit(solution)/shard_map/ppermute | solution.py:337
  94.7 16.8 %collective-permute-start.5 = (bf16[224,768]{1,0:T(8,128)(2,1)S(1)}, bf16[224,768]{1,0:T(8,128)(2,1)S(1)}, u32[]{:S(2)}, u32[]{:S(2)}) collective-permute-start(bf16[224,768]{1,0:T(8,128)(2,1)S(1)} %pair_grads.1.refs_0_), channel_id=1, source_target_pairs={{0,4},{2,6},{4,8},{6,10},{8,12},{10,14},{12,0},{14,2},{1,5},{3,7},... | collective-permute-start | bytes 1032200 | tf_op jit(solution)/shard_map/ppermute | solution.py:337
  112.1 2.5 %collective-permute-start.8 = (bf16[896,256]{1,0:T(8,128)(2,1)S(1)}, bf16[896,256]{1,0:T(8,128)(2,1)S(1)}, u32[]{:S(2)}, u32[]{:S(2)}) collective-permute-start(bf16[896,256]{1,0:T(8,128)(2,1)S(1)} %get-tuple-element.23), channel_id=1, source_target_pairs={{0,1},{1,0},{2,3},{3,2},{4,5},{5,4},{6,7},{7,6},{8,9},{9,8},{10,11... | collective-permute-start | bytes 1376264 | tf_op jit(solution)/shard_map/ppermute | solution.py:348
  116.0 4.4 %collective-permute-start.9 = (bf16[256,1024]{1,0:T(8,128)(2,1)S(1)}, bf16[256,1024]{1,0:T(8,128)(2,1)S(1)}, u32[]{:S(2)}, u32[]{:S(2)}) collective-permute-start(bf16[256,1024]{1,0:T(8,128)(2,1)S(1)} %query_rows.1), channel_id=1, source_target_pairs={{0,1},{1,0},{2,3},{3,2},{4,5},{5,4},{6,7},{7,6},{8,9},{9,8},{10,11... | collective-permute-start | bytes 1572872 | tf_op jit(solution)/shard_map/ppermute | solution.py:349
  120.3 2.0 %copy-start.4 = (f32[896,1024]{1,0:T(8,128)S(1)}, f32[896,1024]{1,0:T(8,128)}, u32[]{:S(2)}) copy-start(f32[896,1024]{1,0:T(8,128)} %eig_ref.1) | copy-start | bytes 11010052

commit v4 on v3

--- a/solution.py
+++ b/solution.py
@@ -53,7 +53,8 @@
 
 
 def rotate_grad_kernel(where_ref, qg_ref, bg_ref, basis_ref, *refs):
-    outs, part = refs[:-1], refs[-1]
+    outs, token_ref, part = refs[:-2], refs[-2], refs[-1]
+    token_ref[...] = jnp.zeros_like(token_ref)
     width = part.shape[1]
     rows = outs[0].shape[0]
 
@@ -85,13 +86,13 @@
             pl.BlockSpec((2, T_SIZE, inner), lambda i, c: (jnp.maximum(i - 1, 0), 0, 0)),
             pl.BlockSpec((outer, inner), lambda i, c: (0, 0)),
         ],
-        out_specs=[pl.BlockSpec((rows, 256), lambda i, c: (0, i))] * n_y,
+        out_specs=[pl.BlockSpec((rows, 256), lambda i, c: (0, i))] * n_y + [TOKEN],
         scratch_shapes=[pltpu.VMEM((outer, 256), BF16)],
     )
     return pl.pallas_call(
         rotate_grad_kernel,
         grid_spec=grid_spec,
-        out_shape=[jax.ShapeDtypeStruct((rows, 768), BF16)] * n_y,
+        out_shape=[jax.ShapeDtypeStruct((rows, 768), BF16)] * n_y + [jax.ShapeDtypeStruct((16, 128), BF16)],
         compiler_params=params(60),
         cost_estimate=pl.CostEstimate(flops=2 * 768 * outer * inner, bytes_accessed=8 * 1024 * 1024, transcendentals=0),
         name="rotate_grad",
@@ -124,7 +125,7 @@
         add_grads_kernel,
         grid_spec=grid_spec,
         out_shape=[half, half],
-        compiler_params=params(40),
+        compiler_params=params(16),
         cost_estimate=pl.CostEstimate(flops=4 * rows * width, bytes_accessed=12 * rows * width, transcendentals=0),
         name="add_grads",
     )(where, *parts)
@@ -149,14 +150,15 @@
         pair_grads_kernel,
         grid_spec=grid_spec,
         out_shape=jax.ShapeDtypeStruct((2 * rows, width), BF16),
-        compiler_params=params(40),
+        compiler_params=params(16),
         cost_estimate=pl.CostEstimate(flops=0, bytes_accessed=8 * rows * width, transcendentals=0),
         name="pair_grads",
     )(where, own, other)
 
 
 def join_grads_kernel(where_ref, *refs):
-    parts, out_ref, query_ref = refs[:-2], refs[-2], refs[-1]
+    parts, out_ref, query_ref, token_ref = refs[:-4], refs[-3], refs[-2], refs[-1]
+    token_ref[...] = jnp.zeros_like(token_ref)
     rows = parts[0].shape[0]
     half = query_ref.shape[1]
     count = len(parts)
@@ -166,23 +168,31 @@
         query_ref[pl.ds(start, rows), :] = part[:, :half]
 
 
-def join_grads(where, parts):
+def join_grads(where, parts, after):
     rows, width = parts[0].shape
     full = rows * len(parts)
     grid_spec = pltpu.PrefetchScalarGridSpec(
         num_scalar_prefetch=1,
         grid=(1,),
-        in_specs=[pl.BlockSpec((rows, width), lambda i, c: (0, 0))] * len(parts),
-        out_specs=[pl.BlockSpec((full, width), lambda i, c: (0, 0)), pl.BlockSpec((full, 256), lambda i, c: (0, 0))],
+        in_specs=[pl.BlockSpec((rows, width), lambda i, c: (0, 0))] * len(parts) + [TOKEN],
+        out_specs=[
+            pl.BlockSpec((full, width), lambda i, c: (0, 0)),
+            pl.BlockSpec((full, 256), lambda i, c: (0, 0)),
+            TOKEN,
+        ],
     )
     return pl.pallas_call(
         join_grads_kernel,
         grid_spec=grid_spec,
-        out_shape=[jax.ShapeDtypeStruct((full, width), BF16), jax.ShapeDtypeStruct((full, 256), BF16)],
-        compiler_params=params(40),
+        out_shape=[
+            jax.ShapeDtypeStruct((full, width), BF16),
+            jax.ShapeDtypeStruct((full, 256), BF16),
+            jax.ShapeDtypeStruct((16, 128), BF16),
+        ],
+        compiler_params=params(16),
         cost_estimate=pl.CostEstimate(flops=0, bytes_accessed=5 * full * width, transcendentals=0),
         name="join_grads",
-    )(where, *parts)
+    )(where, *parts, after)
 
 
 def rotate_act_kernel(recv_ref, basis_ref, after_ref, out_ref, acts):
@@ -210,10 +220,28 @@
         out_specs=pl.BlockSpec((768, 256), lambda i: (0, i)),
         out_shape=jax.ShapeDtypeStruct((768, outer), BF16),
         scratch_shapes=[pltpu.VMEM((768, inner), BF16)],
-        compiler_params=params(40),
+        compiler_params=params(16),
         cost_estimate=pl.CostEstimate(flops=2 * 768 * outer * inner, bytes_accessed=6 * 1024 * 1024, transcendentals=0),
         name="rotate_act",
     )(received, basis, after)
+
+
+def inverse_kernel(eig_ref, out_ref):
+    out_ref[...] = (1.0 / (eig_ref[...] + DAMPING)).astype(BF16)
+
+
+def inverse_of(eigenvalues):
+    rows, width = eigenvalues.shape
+    return pl.pallas_call(
+        inverse_kernel,
+        grid=(4,),
+        in_specs=[pl.BlockSpec((rows // 4, width), lambda i: (i, 0))],
+        out_specs=pl.BlockSpec((rows // 4, width), lambda i: (i, 0)),
+        out_shape=jax.ShapeDtypeStruct((rows, width), BF16),
+        compiler_params=params(16),
+        cost_estimate=pl.CostEstimate(flops=2 * rows * width, bytes_accessed=8 * rows * width, transcendentals=0),
+        name="inverse_of",
+    )(eigenvalues)
 
 
 def add_parts_kernel(parts_ref, keep_ref, came_ref, out_ref, piece_ref):
@@ -243,7 +271,7 @@
             pl.BlockSpec((high, wide // 2), lambda i: (0, i)),
         ],
         out_shape=[jax.ShapeDtypeStruct(parts.shape, BF16), jax.ShapeDtypeStruct(keep.shape, BF16)],
-        compiler_params=params(40),
+        compiler_params=params(16),
         cost_estimate=pl.CostEstimate(flops=parts.size, bytes_accessed=4 * parts.size, transcendentals=0),
         name="add_parts",
     )(parts, keep, came)
@@ -261,7 +289,7 @@
         in_specs=[pl.BlockSpec((rows // 2, width), lambda i: (i, 0)), TOKEN],
         out_specs=pl.BlockSpec((rows // 2, width), lambda i: (i, 0)),
         out_shape=jax.ShapeDtypeStruct((rows, width), BF16),
-        compiler_params=params(40),
+        compiler_params=params(16),
         cost_estimate=pl.CostEstimate(flops=0, bytes_accessed=4 * rows * width, transcendentals=0),
         name="query_rows",
     )(acts, after)
@@ -270,8 +298,8 @@
 PIECE = 64
 
 
-def scores_kernel(core_ref, g_ref, go_ref, a_ref, ao_ref, eig_ref, out_ref, left, right):
-    eigen, width = eig_ref.shape
+def scores_kernel(core_ref, g_ref, go_ref, a_ref, ao_ref, inverse_ref, out_ref, left, right):
+    eigen, width = inverse_ref.shape
 
     def tile(grads, acts, rows, n):
         part = slice(n * T_SIZE, (n + 1) * T_SIZE)
@@ -280,7 +308,7 @@
     for c in range(eigen // PIECE):
         rows = slice(c * PIECE, (c + 1) * PIECE)
         columns = slice(c * width, (c + 1) * width)
-        inverse = 1.0 / (eig_ref[rows, :] + DAMPING)
+        inverse = inverse_ref[rows, :].astype(F32)
         for i in range(2):
             left[i * PIECE:(i + 1) * PIECE, columns] = (tile(g_ref, a_ref, rows, i) * inverse).astype(BF16)
             left[(2 + i) * PIECE:(3 + i) * PIECE, columns] = (tile(go_ref, ao_ref, rows, i) * inverse).astype(BF16)
@@ -292,33 +320,33 @@
     column = lax.broadcasted_iota(jnp.int32, (size, size), 1)
     own = jnp.where(row % PIECE == column % PIECE, product, 0.0)
     lane = lax.broadcasted_iota(jnp.int32, (1, size), 1)
-    place = lax.broadcasted_iota(jnp.int32, (8, 128), 1)
-    result = jnp.zeros((8, 128), F32)
+    place = lax.broadcasted_iota(jnp.int32, (1, 128), 1)
+    result = jnp.zeros((1, 128), F32)
     for i in range(4):
         line = jnp.sum(own[i * PIECE:(i + 1) * PIECE, :], axis=0, keepdims=True)
         query = (i + 2 * core_ref[0]) % 4
         for j in range(4):
             value = jnp.sum(jnp.where(lane // PIECE == j, line, 0.0), axis=1, keepdims=True) * NORM
             result = result + jnp.where(place == query * 4 + j, value, 0.0)
-    out_ref[...] = result
-
-
-def tile_scores(core, grads, grads_other, acts, acts_other, eigenvalues):
-    eigen, width = eigenvalues.shape
-    operands = (grads, grads_other, acts, acts_other, eigenvalues)
+    out_ref[...] = jnp.broadcast_to(result[None], out_ref.shape)
+
+
+def tile_scores(core, grads, grads_other, acts, acts_other, inverse, copies):
+    eigen, width = inverse.shape
+    operands = (grads, grads_other, acts, acts_other, inverse)
     scratch = pltpu.VMEM((4 * PIECE, eigen // PIECE * width), BF16)
     grid_spec = pltpu.PrefetchScalarGridSpec(
         num_scalar_prefetch=1,
         grid=(1,),
         in_specs=[pl.BlockSpec(operand.shape, lambda i, c: (0, 0)) for operand in operands],
-        out_specs=pl.BlockSpec((8, 128), lambda i, c: (0, 0)),
+        out_specs=pl.BlockSpec((copies, 1, 128), lambda i, c: (0, 0, 0)),
         scratch_shapes=[scratch, scratch],
     )
     return pl.pallas_call(
         scores_kernel,
         grid_spec=grid_spec,
-        out_shape=jax.ShapeDtypeStruct((8, 128), F32),
-        compiler_params=params(40),
+        out_shape=jax.ShapeDtypeStruct((copies, 1, 128), F32),
+        compiler_params=params(28),
         cost_estimate=pl.CostEstimate(flops=4 * 8 * T_SIZE * eigen * width, bytes_accessed=8 * 1024 * 1024, transcendentals=0),
         name="tile_scores",
     )(core, *operands)
@@ -337,19 +365,19 @@
         return lax.ppermute(piece, "dp", [(d, (d + 2 * k) % n_dp) for d in range(n_dp)])
 
     received = lax.all_to_all(pack_acts(where, query_act, buffer_act, n_dp), "dp", 0, 0, tiled=True)
-    blocks = rotate_grad(where, query_grad, buffer_grad, grad_basis, n_y)
-    act_part = rotate_act(received, act_basis, blocks[0])
+    *blocks, token = rotate_grad(where, query_grad, buffer_grad, grad_basis, n_y)
+    act_part = rotate_act(received, act_basis, token)
     parts = lax.all_to_all(act_part.reshape(n_shard, -1, act_part.shape[1]), "shard", 0, 0, tiled=True)
     keep, send = add_grads(where, [blocks[0]] + [along_y(blocks[k], k) for k in range(1, n_y)])
     sums, piece = add_parts(parts, keep, lax.ppermute(send, "dp", partner))
     acts = lax.all_to_all(sums, "shard", 0, 0, tiled=True).reshape(act_part.shape)
     pair = pair_grads(where, piece, lax.ppermute(piece, "dp", partner))
-    grads, grads_query = join_grads(where, [pair] + [along_y(pair, k) for k in range(1, n_y)])
+    inverse = inverse_of(eigenvalues)
+    grads, grads_query, joined = join_grads(where, [pair] + [along_y(pair, k) for k in range(1, n_y)], inverse)
     grads_other = lax.ppermute(grads_query, "buffer", swap)
-    acts_other = lax.ppermute(query_rows(acts, grads_other), "buffer", swap)
-    mine = tile_scores(where, grads, grads_other, acts, acts_other, eigenvalues)
-    count = n_dp * n_shard
-    every = lax.all_to_all(jnp.broadcast_to(mine[None, :1], (count, 1, 128)), ("shard", "dp"), 0, 0, tiled=True)
+    acts_other = lax.ppermute(query_rows(acts, joined), "buffer", swap)
+    mine = tile_scores(where, grads, grads_other, acts, acts_other, inverse, n_dp * n_shard)
+    every = lax.all_to_all(mine, ("shard", "dp"), 0, 0, tiled=True)
     return jnp.sum(every, axis=(0, 1))[:16].reshape(4, 4)
 
 

time: 151 us -> 149 us (0.987)
  waiting for transfers between devices: 68.2 us -> 64.9 us
  local copies, waits for them, and re-layouts: 3.75 us -> 5.27 us
    ppermute x6, waiting for transfers between devices: 31.9 us -> 29.4 us  [along_y(): lax.ppermute(piece, 'dp', [(d, (d + 2 * k) % n_dp) for d in range(n_dp)])]
    unnamed x16 -> x24, local copies, waits for them, and re-layouts: 3.04 us -> 4.61 us
    ppermute x1, waiting for transfers between devices: 1.54 us -> 0.01 us  [local(): acts_other = lax.ppermute(query_rows(acts, joined), 'buffer', swap)]
  transfers between devices with their start and end apart: 13 -> 13, of which waited for: 13 -> 12; matrix products, arithmetic and copies ran while one was open for 0% -> 0% of each run, Pallas kernels for 6% -> 7%
where the time goes in v4:
time: 149 us
  waiting for transfers between devices  64.9 us (44%)
  starting transfers between devices  33.3 us (22%)
  Pallas kernels  23.9 us (16%)
  blocking collectives  20.6 us (14%)
  local copies, waits for them, and re-layouts  5.27 us (4%)
    ppermute x6, waiting for transfers between devices, along_y(): lax.ppermute(piece, 'dp', [(d, (d + 2 * k) % n_dp) for d in range(n_dp)])  29.4 us
    all_to_all x1, blocking collectives, local(): every = lax.all_to_all(mine, ('shard', 'dp'), 0, 0, tiled=True)  20.6 us
    ppermute x1, waiting for transfers between devices, local(): pair = pair_grads(where, piece, lax.ppermute(piece, 'dp', partner))  10.8 us
    ppermute x1, waiting for transfers between devices, local(): sums, piece = add_parts(parts, keep, lax.ppermute(send, 'dp', partner))  9.74 us
    all_to_all x1, starting transfers between devices, local(): lax.all_to_all(act_part.reshape(n_shard, -1, act_part.shape[1]), 'shard',...  8.46 us
    pallas_call x1, Pallas kernels, rotate_grad(): pl.pallas_call(rotate_grad_kernel, grid_spec=grid_spec, out_shape=[jax.Sh...  7.64 us
    all_to_all x1, starting transfers between devices, local(): lax.all_to_all(pack_acts(where, query_act, buffer_act, n_dp), 'dp', 0, 0,...  7.48 us
    pallas_call x1, Pallas kernels, tile_scores(): pl.pallas_call(scores_kernel, grid_spec=grid_spec, out_shape=jax.ShapeDty...  6.8 us
  transfers between devices with their start and end apart: 13, of which 12 were waited for; matrix products, arithmetic and copies ran while one was open for 0% of the time, Pallas kernels for 7%

profile of v4, /device:TPU:1, one launch (start us, length us, event | category | flops | bytes accessed | tf_op | source)
XLA Modules:
  0.0 148.9 jit_solution(756473794391508071)
XLA Ops:
  0.0 0.7 pad_add_fusion.core_ref.where_ref
  0.7 2.4 %pack_acts.1 = bf16[8,96,512]{2,1,0:T(8,128)(2,1)} custom-call(s32[3]{0:T(128)} %pad_add_fusion.core_ref.where_ref, bf16[4,16,512]{2,1,0:T(8,128)(2,1)} %qa_ref.1, bf16[4,16,512]{2,1,0:T(8,128)(2,1)} %ba_ref.1), custom_call_target="tpu_custom_call" | custom-call | bytes 2097152 | tf_op jit(solution)/shard_map/pack_acts/pallas_call | solution.py:45
  3.1 7.5 %all-to-all-start = ((bf16[8,96,512]{2,1,0:T(8,128)(2,1)}), bf16[8,96,512]{2,1,0:T(8,128)(2,1)S(1)}, u32[]{:S(2)}, u32[]{:S(2)}) async-start(bf16[8,96,512]{2,1,0:T(8,128)(2,1)} %pack_acts.1), calls=%async_computation | async-start | bytes 1572864 | tf_op jit(solution)/shard_map/all_to_all | solution.py:367
  10.6 0.0 copy-start.1
  10.6 7.6 %rotate_grad.1 = (bf16[224,768]{1,0:T(8,128)(2,1)}, bf16[224,768]{1,0:T(8,128)(2,1)}, bf16[224,768]{1,0:T(8,128)(2,1)}, bf16[224,768]{1,0:T(8,128)(2,1)}, bf16[16,128]{1,0:T(8,128)(2,1)}) custom-call(s32[3]{0:T(128)} %pad_add_fusion.core_ref.where_ref, bf16[4,128,1792]{2,1,0:T(8,128)(2,1)} %qg_ref.1, bf16[4,128,1792]{2,1,0:T(8,128)(2,1)} %bg_ref.1, ...), custom_call_target="tpu_custom_call" | custom-call | flops 2466250752 | bytes 8388608 | tf_op jit(solution)/shard_map/rotate_grad/pallas_call | solution.py:92
  18.2 5.5 %all-to-all-done.recv_ref = bf16[8,96,512]{2,1,0:T(8,128)(2,1)S(1)} async-done(((bf16[8,96,512]{2,1,0:T(8,128)(2,1)}), bf16[8,96,512]{2,1,0:T(8,128)(2,1)S(1)}, u32[]{:S(2)}, u32[]{:S(2)}) %all-to-all-start) | async-done | bytes 786464 | tf_op jit(solution)/shard_map/all_to_all | solution.py:367
  23.8 0.0 copy-done.1
  23.8 0.0 copy-start.4
  23.8 0.7 copy-done.4
  24.5 2.8 %rotate_act.1 = bf16[768,1024]{1,0:T(8,128)(2,1)} custom-call(bf16[8,96,512]{2,1,0:T(8,128)(2,1)S(1)} %all-to-all-done.recv_ref, bf16[1024,512]{1,0:T(8,128)(2,1)S(1)} %copy-done.1, bf16[16,128]{1,0:T(8,128)(2,1)S(1)} %copy-done.4), custom_call_target="tpu_custom_call" | custom-call | flops 805306368 | bytes 6291456 | tf_op jit(solution)/shard_map/rotate_act/pallas_call | solution.py:212
  27.3 0.0 copy-start.11
  27.3 0.0 copy-start.10
  27.3 0.0 copy-start.9
  27.3 0.0 copy-start.2
  27.3 0.0 copy-start.3
  27.3 8.5 %all-to-all-start.1 = ((bf16[16,48,1024]{2,1,0:T(8,128)(2,1)}), bf16[16,48,1024]{2,1,0:T(8,128)(2,1)S(1)}, u32[]{:S(2)}, u32[]{:S(2)}) async-start(bf16[16,48,1024]{2,1,0:T(8,128)(2,1)} %bitcast.3), calls=%async_computation.1 | async-start | bytes 3145728 | tf_op jit(solution)/shard_map/all_to_all | solution.py:370
  35.8 0.0 copy-done.11
  35.8 0.1 collective-permute-start
  35.9 0.0 copy-done.10
  35.9 2.0 %collective-permute-start.1 = (bf16[224,768]{1,0:T(8,128)(2,1)S(1)}, bf16[224,768]{1,0:T(8,128)(2,1)S(1)}, u32[]{:S(2)}, u32[]{:S(2)}) collective-permute-start(bf16[224,768]{1,0:T(8,128)(2,1)S(1)} %copy-done.10), channel_id=1, source_target_pairs={{0,8},{2,10},{4,12},{6,14},{8,0},{10,2},{12,4},{14,6},{1,9},{3,11}... | collective-permute-start | bytes 1032200 | tf_op jit(solution)/shard_map/ppermute | solution.py:365
  37.9 0.0 copy-done.9
  37.9 0.9 collective-permute-start.2
  38.8 5.7 %collective-permute-done.refs_1_ = bf16[224,768]{1,0:T(8,128)(2,1)S(1)} collective-permute-done((bf16[224,768]{1,0:T(8,128)(2,1)S(1)}, bf16[224,768]{1,0:T(8,128)(2,1)S(1)}, u32[]{:S(2)}, u32[]{:S(2)}) %collective-permute-start) | collective-permute-done | bytes 344096 | tf_op jit(solution)/shard_map/ppermute | solution.py:365
  44.6 6.7 %collective-permute-done.1.refs_2_ = bf16[224,768]{1,0:T(8,128)(2,1)S(1)} collective-permute-done((bf16[224,768]{1,0:T(8,128)(2,1)S(1)}, bf16[224,768]{1,0:T(8,128)(2,1)S(1)}, u32[]{:S(2)}, u32[]{:S(2)}) %collective-permute-start.1) | collective-permute-done | bytes 344096 | tf_op jit(solution)/shard_map/ppermute | solution.py:365
  51.3 2.7 %collective-permute-done.2.refs_3_ = bf16[224,768]{1,0:T(8,128)(2,1)S(1)} collective-permute-done((bf16[224,768]{1,0:T(8,128)(2,1)S(1)}, bf16[224,768]{1,0:T(8,128)(2,1)S(1)}, u32[]{:S(2)}, u32[]{:S(2)}) %collective-permute-start.2) | collective-permute-done | bytes 344096 | tf_op jit(solution)/shard_map/ppermute | solution.py:365
  53.9 0.0 copy-done.2
  54.0 0.0 copy-done.3
  54.0 0.9 add_grads.1
  54.8 1.3 collective-permute-start.3
  56.1 9.7 %collective-permute-done.3.came_ref = bf16[112,768]{1,0:T(8,128)(2,1)S(1)} collective-permute-done((bf16[112,768]{1,0:T(8,128)(2,1)S(1)}, bf16[112,768]{1,0:T(8,128)(2,1)S(1)}, u32[]{:S(2)}, u32[]{:S(2)}) %collective-permute-start.3) | collective-permute-done | bytes 172064 | tf_op jit(solution)/shard_map/ppermute | solution.py:372
  65.9 6.0 %all-to-all-done.1.parts_ref = bf16[16,48,1024]{2,1,0:T(8,128)(2,1)S(1)} async-done(((bf16[16,48,1024]{2,1,0:T(8,128)(2,1)}), bf16[16,48,1024]{2,1,0:T(8,128)(2,1)S(1)}, u32[]{:S(2)}, u32[]{:S(2)}) %all-to-all-start.1) | async-done | bytes 1572896 | tf_op jit(solution)/shard_map/all_to_all | solution.py:370
  71.9 1.5 %add_parts.1 = (bf16[16,48,1024]{2,1,0:T(8,128)(2,1)}, bf16[112,768]{1,0:T(8,128)(2,1)S(1)}) custom-call(bf16[16,48,1024]{2,1,0:T(8,128)(2,1)S(1)} %all-to-all-done.1.parts_ref, bf16[112,768]{1,0:T(8,128)(2,1)S(1)} %get-tuple-element.22.keep_ref, bf16[112,768]{1,0:T(8,128)(2,1)S(1)} %collective-permute-done.3.came_ref), custom_call_target="tpu_custom_call" | custom-call | flops 786432 | bytes 3145728 | tf_op jit(solution)/shard_map/add_parts/pallas_call | solution.py:261
  73.4 6.2 %all-to-all-start.2 = ((bf16[16,48,1024]{2,1,0:T(8,128)(2,1)}), bf16[16,48,1024]{2,1,0:T(8,128)(2,1)S(1)}, u32[]{:S(2)}, u32[]{:S(2)}) async-start(bf16[16,48,1024]{2,1,0:T(8,128)(2,1)} %get-tuple-element.27), calls=%async_computation.2 | async-start | bytes 3145728 | tf_op jit(solution)/shard_map/all_to_all | solution.py:373
  79.5 1.2 collective-permute-start.4
  80.8 10.8 %collective-permute-done.4.other_ref = bf16[112,768]{1,0:T(8,128)(2,1)S(1)} collective-permute-done((bf16[112,768]{1,0:T(8,128)(2,1)S(1)}, bf16[112,768]{1,0:T(8,128)(2,1)S(1)}, u32[]{:S(2)}, u32[]{:S(2)}) %collective-permute-start.4) | collective-permute-done | bytes 172064 | tf_op jit(solution)/shard_map/ppermute | solution.py:374
  91.6 0.6 pair_grads.1.refs_0_
  92.1 0.7 collective-permute-start.7
  92.9 1.5 collective-permute-start.6
  94.3 0.0 collective-permute-start.5
  94.3 0.0 copy-start
  94.3 2.0 %copy-done = f32[896,1024]{1,0:T(8,128)S(1)} copy-done((f32[896,1024]{1,0:T(8,128)S(1)}, f32[896,1024]{1,0:T(8,128)}, u32[]{:S(2)}) %copy-start) | copy-done | bytes 3670040
  96.4 0.5 inverse_of.1.refs_4_.inverse_ref
  96.9 2.7 %collective-permute-done.7.refs_3_ = bf16[224,768]{1,0:T(8,128)(2,1)S(1)} collective-permute-done((bf16[224,768]{1,0:T(8,128)(2,1)S(1)}, bf16[224,768]{1,0:T(8,128)(2,1)S(1)}, u32[]{:S(2)}, u32[]{:S(2)}) %collective-permute-start.7) | collective-permute-done | bytes 344096 | tf_op jit(solution)/shard_map/ppermute | solution.py:365
  99.6 1.2 collective-permute-done.6.refs_2_
  100.9 10.3 %collective-permute-done.5.refs_1_ = bf16[224,768]{1,0:T(8,128)(2,1)S(1)} collective-permute-done((bf16[224,768]{1,0:T(8,128)(2,1)S(1)}, bf16[224,768]{1,0:T(8,128)(2,1)S(1)}, u32[]{:S(2)}, u32[]{:S(2)}) %collective-permute-start.5) | collective-permute-done | bytes 344096 | tf_op jit(solution)/shard_map/ppermute | solution.py:365
  111.2 0.7 join_grads.1
  111.9 0.0 copy-start.5
  111.9 1.1 copy-done.5
  113.0 0.0 copy-start.7
  113.0 0.8 copy-done.7
  113.7 2.0 %all-to-all-done.2 = bf16[16,48,1024]{2,1,0:T(8,128)(2,1)S(1)} async-done(((bf16[16,48,1024]{2,1,0:T(8,128)(2,1)}), bf16[16,48,1024]{2,1,0:T(8,128)(2,1)S(1)}, u32[]{:S(2)}, u32[]{:S(2)}) %all-to-all-start.2) | async-done | bytes 1572896 | tf_op jit(solution)/shard_map/all_to_all | solution.py:373
  115.7 0.0 copy-start.8
  115.7 0.0 copy-start.6
  115.7 0.1 query_rows.1
  115.8 2.6 %collective-permute-start.9 = (bf16[256,1024]{1,0:T(8,128)(2,1)S(1)}, bf16[256,1024]{1,0:T(8,128)(2,1)S(1)}, u32[]{:S(2)}, u32[]{:S(2)}) collective-permute-start(bf16[256,1024]{1,0:T(8,128)(2,1)S(1)} %query_rows.1), channel_id=1, source_target_pairs={{0,1},{1,0},{2,3},{3,2},{4,5},{5,4},{6,7},{7,6},{8,9},{9,8},{10,11... | collective-permute-start | bytes 1572872 | tf_op jit(solution)/shard_map/ppermute | solution.py:378
  118.4 0.0 copy-done.8
  118.4 0.9 collective-permute-start.8
  119.3 1.4 collective-permute-done.8.go_ref
  120.7 0.0 collective-permute-done.9.ao_ref
  120.7 0.0 copy-done.6
  120.7 6.8 %tile_scores.1 = f32[128,1,128]{2,1,0:T(1,128)S(1)} custom-call(s32[3]{0:T(128)S(1)} %copy-done.3, bf16[896,768]{1,0:T(8,128)(2,1)S(1)} %copy-done.6, bf16[896,256]{1,0:T(8,128)(2,1)S(1)} %collective-permute-done.8.go_ref, bf16[768,1024]{1,0:T(8,128)(2,1)S(1)} %bitcast.7, bf16[256,1024]{1,0:T(8,128)(2,1)S(1)} %collective-permute-done.9.ao_ref, ...), custom_call_target="tpu_custom_call" | custom-call | flops 3758096384 | bytes 8388608 | tf_op jit(solution)/shard_map/tile_scores/pallas_call | solution.py:345
  127.5 20.6 %all_to_all.20 = f32[128,1,128]{2,1,0:T(1,128)S(1)} all-to-all(f32[128,1,128]{2,1,0:T(1,128)S(1)} %tile_scores.1), channel_id=1, replica_groups=mesh['shard'=16,'dp'=8,'buffer'=2] {'shard','dp'}, dimensions={0} | all-to-all | bytes 131072 | tf_op jit(solution)/shard_map/all_to_all | solution.py:380
  148.1 0.2 reduce_sum.9
  148.3 0.7 reshape.19
Async XLA Ops:
  3.1 20.7 %all-to-all-start = ((bf16[8,96,512]{2,1,0:T(8,128)(2,1)}), bf16[8,96,512]{2,1,0:T(8,128)(2,1)S(1)}, u32[]{:S(2)}, u32[]{:S(2)}) async-start(bf16[8,96,512]{2,1,0:T(8,128)(2,1)} %pack_acts.1), calls=%async_computation | async-start | bytes 1572864 | tf_op jit(solution)/shard_map/all_to_all | solution.py:367
  10.6 13.2 %copy-start.1 = (bf16[1024,512]{1,0:T(8,128)(2,1)S(1)}, bf16[1024,512]{1,0:T(8,128)(2,1)}, u32[]{:S(2)}) copy-start(bf16[1024,512]{1,0:T(8,128)(2,1)} %basis_ref.3) | copy-start | bytes 3145732
  23.8 0.7 copy-start.4
  27.3 8.5 %copy-start.11 = (bf16[224,768]{1,0:T(8,128)(2,1)S(1)}, bf16[224,768]{1,0:T(8,128)(2,1)}, u32[]{:S(2)}) copy-start(bf16[224,768]{1,0:T(8,128)(2,1)} %get-tuple-element.19) | copy-start | bytes 1032196
  27.3 8.6 %copy-start.10 = (bf16[224,768]{1,0:T(8,128)(2,1)S(1)}, bf16[224,768]{1,0:T(8,128)(2,1)}, u32[]{:S(2)}) copy-start(bf16[224,768]{1,0:T(8,128)(2,1)} %get-tuple-element.20) | copy-start | bytes 1032196
  27.3 10.6 %copy-start.9 = (bf16[224,768]{1,0:T(8,128)(2,1)S(1)}, bf16[224,768]{1,0:T(8,128)(2,1)}, u32[]{:S(2)}) copy-start(bf16[224,768]{1,0:T(8,128)(2,1)} %get-tuple-element.21) | copy-start | bytes 1032196
  27.3 26.7 %copy-start.2 = (bf16[224,768]{1,0:T(8,128)(2,1)S(1)}, bf16[224,768]{1,0:T(8,128)(2,1)}, u32[]{:S(2)}) copy-start(bf16[224,768]{1,0:T(8,128)(2,1)} %get-tuple-element.18.refs_0_) | copy-start | bytes 1032196
  27.3 26.6 %copy-start.3 = (s32[3]{0:T(128)S(1)}, s32[3]{0:T(128)}, u32[]{:S(2)}) copy-start(s32[3]{0:T(128)} %pad_add_fusion.core_ref.where_ref) | copy-start | bytes 40
  27.3 44.6 %all-to-all-start.1 = ((bf16[16,48,1024]{2,1,0:T(8,128)(2,1)}), bf16[16,48,1024]{2,1,0:T(8,128)(2,1)S(1)}, u32[]{:S(2)}, u32[]{:S(2)}) async-start(bf16[16,48,1024]{2,1,0:T(8,128)(2,1)} %bitcast.3), calls=%async_computation.1 | async-start | bytes 3145728 | tf_op jit(solution)/shard_map/all_to_all | solution.py:370
  35.8 8.8 %collective-permute-start = (bf16[224,768]{1,0:T(8,128)(2,1)S(1)}, bf16[224,768]{1,0:T(8,128)(2,1)S(1)}, u32[]{:S(2)}, u32[]{:S(2)}) collective-permute-start(bf16[224,768]{1,0:T(8,128)(2,1)S(1)} %copy-done.11), channel_id=1, source_target_pairs={{0,4},{2,6},{4,8},{6,10},{8,12},{10,14},{12,0},{14,2},{1,5},{3,7},... | collective-permute-start | bytes 1032200 | tf_op jit(solution)/shard_map/ppermute | solution.py:365
  35.9 15.4 %collective-permute-start.1 = (bf16[224,768]{1,0:T(8,128)(2,1)S(1)}, bf16[224,768]{1,0:T(8,128)(2,1)S(1)}, u32[]{:S(2)}, u32[]{:S(2)}) collective-permute-start(bf16[224,768]{1,0:T(8,128)(2,1)S(1)} %copy-done.10), channel_id=1, source_target_pairs={{0,8},{2,10},{4,12},{6,14},{8,0},{10,2},{12,4},{14,6},{1,9},{3,11}... | collective-permute-start | bytes 1032200 | tf_op jit(solution)/shard_map/ppermute | solution.py:365
  37.9 16.0 %collective-permute-start.2 = (bf16[224,768]{1,0:T(8,128)(2,1)S(1)}, bf16[224,768]{1,0:T(8,128)(2,1)S(1)}, u32[]{:S(2)}, u32[]{:S(2)}) collective-permute-start(bf16[224,768]{1,0:T(8,128)(2,1)S(1)} %copy-done.9), channel_id=1, source_target_pairs={{0,12},{2,14},{4,0},{6,2},{8,4},{10,6},{12,8},{14,10},{1,13},{3,15... | collective-permute-start | bytes 1032200 | tf_op jit(solution)/shard_map/ppermute | solution.py:365
  54.8 11.0 %collective-permute-start.3 = (bf16[112,768]{1,0:T(8,128)(2,1)S(1)}, bf16[112,768]{1,0:T(8,128)(2,1)S(1)}, u32[]{:S(2)}, u32[]{:S(2)}) collective-permute-start(bf16[112,768]{1,0:T(8,128)(2,1)S(1)} %get-tuple-element.23), channel_id=1, source_target_pairs={{0,2},{2,0},{4,6},{6,4},{8,10},{10,8},{12,14},{14,12},{1,3},{3,1},... | collective-permute-start | bytes 516104 | tf_op jit(solution)/shard_map/ppermute | solution.py:372
  73.4 42.4 %all-to-all-start.2 = ((bf16[16,48,1024]{2,1,0:T(8,128)(2,1)}), bf16[16,48,1024]{2,1,0:T(8,128)(2,1)S(1)}, u32[]{:S(2)}, u32[]{:S(2)}) async-start(bf16[16,48,1024]{2,1,0:T(8,128)(2,1)} %get-tuple-element.27), calls=%async_computation.2 | async-start | bytes 3145728 | tf_op jit(solution)/shard_map/all_to_all | solution.py:373
  79.5 12.0 %collective-permute-start.4 = (bf16[112,768]{1,0:T(8,128)(2,1)S(1)}, bf16[112,768]{1,0:T(8,128)(2,1)S(1)}, u32[]{:S(2)}, u32[]{:S(2)}) collective-permute-start(bf16[112,768]{1,0:T(8,128)(2,1)S(1)} %get-tuple-element.24.own_ref), channel_id=1, source_target_pairs={{0,2},{2,0},{4,6},{6,4},{8,10},{10,8},{12,14},{14,12},{1,3},{3,1},... | collective-permute-start | bytes 516104 | tf_op jit(solution)/shard_map/ppermute | solution.py:374
  92.1 7.5 %collective-permute-start.7 = (bf16[224,768]{1,0:T(8,128)(2,1)S(1)}, bf16[224,768]{1,0:T(8,128)(2,1)S(1)}, u32[]{:S(2)}, u32[]{:S(2)}) collective-permute-start(bf16[224,768]{1,0:T(8,128)(2,1)S(1)} %pair_grads.1.refs_0_), channel_id=1, source_target_pairs={{0,12},{2,14},{4,0},{6,2},{8,4},{10,6},{12,8},{14,10},{1,13},{3,15... | collective-permute-start | bytes 1032200 | tf_op jit(solution)/shard_map/ppermute | solution.py:365
  92.9 8.0 %collective-permute-start.6 = (bf16[224,768]{1,0:T(8,128)(2,1)S(1)}, bf16[224,768]{1,0:T(8,128)(2,1)S(1)}, u32[]{:S(2)}, u32[]{:S(2)}) collective-permute-start(bf16[224,768]{1,0:T(8,128)(2,1)S(1)} %pair_grads.1.refs_0_), channel_id=1, source_target_pairs={{0,8},{2,10},{4,12},{6,14},{8,0},{10,2},{12,4},{14,6},{1,9},{3,11}... | collective-permute-start | bytes 1032200 | tf_op jit(solution)/shard_map/ppermute | solution.py:365
  94.3 16.9 %collective-permute-start.5 = (bf16[224,768]{1,0:T(8,128)(2,1)S(1)}, bf16[224,768]{1,0:T(8,128)(2,1)S(1)}, u32[]{:S(2)}, u32[]{:S(2)}) collective-permute-start(bf16[224,768]{1,0:T(8,128)(2,1)S(1)} %pair_grads.1.refs_0_), channel_id=1, source_target_pairs={{0,4},{2,6},{4,8},{6,10},{8,12},{10,14},{12,0},{14,2},{1,5},{3,7},... | collective-permute-start | bytes 1032200 | tf_op jit(solution)/shard_map/ppermute | solution.py:365
  94.3 2.0 %copy-start = (f32[896,1024]{1,0:T(8,128)S(1)}, f32[896,1024]{1,0:T(8,128)}, u32[]{:S(2)}) copy-start(f32[896,1024]{1,0:T(8,128)} %eig_ref.1) | copy-start | bytes 11010052
  111.9 1.1 copy-start.5
  113.0 0.8 copy-start.7
  115.7 2.7 %copy-start.8 = (bf16[896,256]{1,0:T(8,128)(2,1)S(1)}, bf16[896,256]{1,0:T(8,128)(2,1)}, u32[]{:S(2)}) copy-start(bf16[896,256]{1,0:T(8,128)(2,1)} %copy-done.7) | copy-start | bytes 1376260
  115.7 5.0 %copy-start.6 = (bf16[896,768]{1,0:T(8,128)(2,1)S(1)}, bf16[896,768]{1,0:T(8,128)(2,1)}, u32[]{:S(2)}) copy-start(bf16[896,768]{1,0:T(8,128)(2,1)} %copy-done.5) | copy-start | bytes 4128772
  115.8 4.9 %collective-permute-start.9 = (bf16[256,1024]{1,0:T(8,128)(2,1)S(1)}, bf16[256,1024]{1,0:T(8,128)(2,1)S(1)}, u32[]{:S(2)}, u32[]{:S(2)}) collective-permute-start(bf16[256,1024]{1,0:T(8,128)(2,1)S(1)} %query_rows.1), channel_id=1, source_target_pairs={{0,1},{1,0},{2,3},{3,2},{4,5},{5,4},{6,7},{7,6},{8,9},{9,8},{10,11... | collective-permute-start | bytes 1572872 | tf_op jit(solution)/shard_map/ppermute | solution.py:378
  118.4 2.3 %collective-permute-start.8 = (bf16[896,256]{1,0:T(8,128)(2,1)S(1)}, bf16[896,256]{1,0:T(8,128)(2,1)S(1)}, u32[]{:S(2)}, u32[]{:S(2)}) collective-permute-start(bf16[896,256]{1,0:T(8,128)(2,1)S(1)} %copy-done.8), channel_id=1, source_target_pairs={{0,1},{1,0},{2,3},{3,2},{4,5},{5,4},{6,7},{7,6},{8,9},{9,8},{10,11... | collective-permute-start | bytes 1376264 | tf_op jit(solution)/shard_map/ppermute | solution.py:377

commit v5 on v4

--- a/solution.py
+++ b/solution.py
@@ -195,35 +195,39 @@
     )(where, *parts, after)
 
 
-def rotate_act_kernel(recv_ref, basis_ref, after_ref, out_ref, acts):
+def rotate_act_kernel(where_ref, *refs):
+    pieces, basis_ref, out_ref, acts = refs[:-4], refs[-4], refs[-2], refs[-1]
+    count = len(pieces)
+
     @pl.when(pl.program_id(0) == 0)
     def _():
-        for d in range(recv_ref.shape[0]):
+        for k, piece in enumerate(pieces):
+            source = lax.rem(2 * where_ref[1] + where_ref[2] + count - k, count)
             for n in range(6):
-                to = n * T_SIZE + d * 16
-                acts[to:to + 16, :] = recv_ref[d, n * 16:(n + 1) * 16, :]
+                to = pl.multiple_of(n * T_SIZE + source * 16, 16)
+                acts[pl.ds(to, 16), :] = piece[n * 16:(n + 1) * 16, :]
 
     out_ref[...] = lax.dot_general(acts[...], basis_ref[...], NT, preferred_element_type=F32).astype(BF16)
 
 
-def rotate_act(received, basis, after):
-    n_dp, rows, inner = received.shape
-    outer = basis.shape[0]
+def rotate_act(where, pieces, basis, after):
+    outer, inner = basis.shape
+    grid_spec = pltpu.PrefetchScalarGridSpec(
+        num_scalar_prefetch=1,
+        grid=(outer // 256,),
+        in_specs=[pl.BlockSpec(piece.shape, lambda i, c: (0, 0)) for piece in pieces]
+        + [pl.BlockSpec((256, inner), lambda i, c: (i, 0)), TOKEN],
+        out_specs=pl.BlockSpec((768, 256), lambda i, c: (0, i)),
+        scratch_shapes=[pltpu.VMEM((768, inner), BF16)],
+    )
     return pl.pallas_call(
         rotate_act_kernel,
-        grid=(outer // 256,),
-        in_specs=[
-            pl.BlockSpec((n_dp, rows, inner), lambda i: (0, 0, 0)),
-            pl.BlockSpec((256, inner), lambda i: (i, 0)),
-            TOKEN,
-        ],
-        out_specs=pl.BlockSpec((768, 256), lambda i: (0, i)),
+        grid_spec=grid_spec,
         out_shape=jax.ShapeDtypeStruct((768, outer), BF16),
-        scratch_shapes=[pltpu.VMEM((768, inner), BF16)],
         compiler_params=params(16),
         cost_estimate=pl.CostEstimate(flops=2 * 768 * outer * inner, bytes_accessed=6 * 1024 * 1024, transcendentals=0),
         name="rotate_act",
-    )(received, basis, after)
+    )(where, *pieces, basis, after)
 
 
 def inverse_kernel(eig_ref, out_ref):
@@ -364,9 +368,12 @@
     def along_y(piece, k):
         return lax.ppermute(piece, "dp", [(d, (d + 2 * k) % n_dp) for d in range(n_dp)])
 
-    received = lax.all_to_all(pack_acts(where, query_act, buffer_act, n_dp), "dp", 0, 0, tiled=True)
+    tokens = pack_acts(where, query_act, buffer_act, 1)[0]
+    pieces = [tokens] + [
+        lax.ppermute(tokens, "dp", [(d, (d + k) % n_dp) for d in range(n_dp)]) for k in range(1, n_dp)
+    ]
     *blocks, token = rotate_grad(where, query_grad, buffer_grad, grad_basis, n_y)
-    act_part = rotate_act(received, act_basis, token)
+    act_part = rotate_act(where, pieces, act_basis, token)
     parts = lax.all_to_all(act_part.reshape(n_shard, -1, act_part.shape[1]), "shard", 0, 0, tiled=True)
     keep, send = add_grads(where, [blocks[0]] + [along_y(blocks[k], k) for k in range(1, n_y)])
     sums, piece = add_parts(parts, keep, lax.ppermute(send, "dp", partner))

time: 149 us -> 149 us (level)
  starting transfers between devices: 33.3 us -> 50.9 us
  waiting for transfers between devices: 64.9 us -> 47.8 us
    ppermute x0 -> x7, starting transfers between devices: none -> 13.2 us  [local(): lax.ppermute(tokens, 'dp', [(d, (d + k) % n_dp) for d in range(n_dp)])]
    ppermute x6, waiting for transfers between devices: 29.4 us -> 21.7 us  [along_y(): lax.ppermute(piece, 'dp', [(d, (d + 2 * k) % n_dp) for d in range(n_dp)])]
    all_to_all x1 -> x0, starting transfers between devices: 7.48 us -> none  [local(): lax.all_to_all(pack_acts(where, query_act, buffer_act, n_dp), 'dp', 0, 0,...]
    all_to_all x1 -> x0, waiting for transfers between devices: 5.54 us -> none  [local(): lax.all_to_all(pack_acts(where, query_act, buffer_act, n_dp), 'dp', 0, 0,...]
    ppermute x1, starting transfers between devices: 1.31 us -> 4.67 us  [local(): sums, piece = add_parts(parts, keep, lax.ppermute(send, 'dp', partner))]
    all_to_all x1, waiting for transfers between devices: 1.97 us -> 5.31 us  [local(): lax.all_to_all(sums, 'shard', 0, 0, tiled=True).reshape(act_part.shape)]
    ppermute x1, waiting for transfers between devices: 10.8 us -> 7.76 us  [local(): pair = pair_grads(where, piece, lax.ppermute(piece, 'dp', partner))]
    ppermute x6, starting transfers between devices: 5.2 us -> 7.96 us  [along_y(): lax.ppermute(piece, 'dp', [(d, (d + 2 * k) % n_dp) for d in range(n_dp)])]
  transfers between devices with their start and end apart: 13 -> 19, of which waited for: 12 -> 11; matrix products, arithmetic and copies ran while one was open for 0% -> 0% of each run, Pallas kernels for 7% -> 7%
where the time goes in v5:
time: 149 us
  starting transfers between devices  50.9 us (34%)
  waiting for transfers between devices  47.8 us (32%)
  Pallas kernels  23.9 us (16%)
  blocking collectives  19.9 us (13%)
  local copies, waits for them, and re-layouts  5.23 us (4%)
    ppermute x6, waiting for transfers between devices, along_y(): lax.ppermute(piece, 'dp', [(d, (d + 2 * k) % n_dp) for d in range(n_dp)])  21.7 us
    all_to_all x1, blocking collectives, local(): every = lax.all_to_all(mine, ('shard', 'dp'), 0, 0, tiled=True)  19.9 us
    ppermute x7, starting transfers between devices, local(): lax.ppermute(tokens, 'dp', [(d, (d + k) % n_dp) for d in range(n_dp)])  13.2 us
    all_to_all x1, starting transfers between devices, local(): lax.all_to_all(act_part.reshape(n_shard, -1, act_part.shape[1]), 'shard',...  9.15 us
    ppermute x6, starting transfers between devices, along_y(): lax.ppermute(piece, 'dp', [(d, (d + 2 * k) % n_dp) for d in range(n_dp)])  7.96 us
    all_to_all x1, starting transfers between devices, local(): lax.all_to_all(sums, 'shard', 0, 0, tiled=True).reshape(act_part.shape)  7.78 us
    ppermute x1, waiting for transfers between devices, local(): pair = pair_grads(where, piece, lax.ppermute(piece, 'dp', partner))  7.76 us
    pallas_call x1, Pallas kernels, rotate_grad(): pl.pallas_call(rotate_grad_kernel, grid_spec=grid_spec, out_shape=[jax.Sh...  7.48 us
  transfers between devices with their start and end apart: 19, of which 11 were waited for; matrix products, arithmetic and copies ran while one was open for 0% of the time, Pallas kernels for 7%

profile of v5, /device:TPU:1, one launch (start us, length us, event | category | flops | bytes accessed | tf_op | source)
XLA Modules:
  0.0 148.7 jit_solution(13244387388423566540)
XLA Ops:
  0.0 0.6 pad_add_fusion.core_ref.where_ref
  0.6 2.1 %pack_acts.1 = bf16[1,96,512]{2,1,0:T(8,128)(2,1)} custom-call(s32[3]{0:T(128)} %pad_add_fusion.core_ref.where_ref, bf16[4,16,512]{2,1,0:T(8,128)(2,1)} %qa_ref.1, bf16[4,16,512]{2,1,0:T(8,128)(2,1)} %ba_ref.1), custom_call_target="tpu_custom_call" | custom-call | bytes 2097152 | tf_op jit(solution)/shard_map/pack_acts/pallas_call | solution.py:45
  2.7 6.0 %collective-permute-start.6 = (bf16[96,512]{1,0:T(8,128)(2,1)}, bf16[96,512]{1,0:T(8,128)(2,1)S(1)}, u32[]{:S(2)}, u32[]{:S(2)}) collective-permute-start(bf16[96,512]{1,0:T(8,128)(2,1)} %bitcast.9), channel_id=1, source_target_pairs={{0,14},{2,0},{4,2},{6,4},{8,6},{10,8},{12,10},{14,12},{1,15},{3,1}... | collective-permute-start | bytes 294920 | tf_op jit(solution)/shard_map/ppermute | solution.py:373
  8.8 0.5 collective-permute-start.5
  9.2 0.1 collective-permute-start.4
  9.3 2.6 %collective-permute-start.3 = (bf16[96,512]{1,0:T(8,128)(2,1)}, bf16[96,512]{1,0:T(8,128)(2,1)S(1)}, u32[]{:S(2)}, u32[]{:S(2)}) collective-permute-start(bf16[96,512]{1,0:T(8,128)(2,1)} %bitcast.12), channel_id=1, source_target_pairs={{0,8},{2,10},{4,12},{6,14},{8,0},{10,2},{12,4},{14,6},{1,9},{3,11}... | collective-permute-start | bytes 294920 | tf_op jit(solution)/shard_map/ppermute | solution.py:373
  12.0 1.1 collective-permute-start.2
  13.1 0.0 collective-permute-done.6.refs_7_
  13.1 1.4 collective-permute-start.1
  14.5 0.0 collective-permute-done.5.refs_6_
  14.5 1.4 collective-permute-start
  15.9 7.5 %rotate_grad.1 = (bf16[224,768]{1,0:T(8,128)(2,1)}, bf16[224,768]{1,0:T(8,128)(2,1)}, bf16[224,768]{1,0:T(8,128)(2,1)}, bf16[224,768]{1,0:T(8,128)(2,1)}, bf16[16,128]{1,0:T(8,128)(2,1)}) custom-call(s32[3]{0:T(128)} %pad_add_fusion.core_ref.where_ref, bf16[4,128,1792]{2,1,0:T(8,128)(2,1)} %qg_ref.1, bf16[4,128,1792]{2,1,0:T(8,128)(2,1)} %bg_ref.1, ...), custom_call_target="tpu_custom_call" | custom-call | flops 2466250752 | bytes 8388608 | tf_op jit(solution)/shard_map/rotate_grad/pallas_call | solution.py:92
  23.4 0.0 collective-permute-done.4.refs_5_
  23.4 0.0 collective-permute-done.3.refs_4_
  23.4 0.0 collective-permute-done.2.refs_3_
  23.4 0.0 collective-permute-done.1.refs_2_
  23.4 0.0 collective-permute-done.refs_1_
  23.4 0.0 copy-done.1
  23.4 0.0 copy-done.2
  23.5 0.0 copy-done.4
  23.5 0.0 copy-start.5
  23.5 0.7 copy-done.5
  24.1 3.4 %rotate_act.1 = bf16[768,1024]{1,0:T(8,128)(2,1)} custom-call(s32[3]{0:T(128)S(1)} %copy-done.4, bf16[96,512]{1,0:T(8,128)(2,1)S(1)} %bitcast.16, bf16[96,512]{1,0:T(8,128)(2,1)S(1)} %collective-permute-done.refs_1_, bf16[96,512]{1,0:T(8,128)(2,1)S(1)} %collective-permute-done.1.refs_2_, bf16[96,512]{1,0:T(8,128)(2,1)S(1)} %collective-permute-done.2.refs_3_, ...), custom_call_target="tpu_custom_call" | custom-call | flops 805306368 | bytes 6291456 | tf_op jit(solution)/shard_map/rotate_act/pallas_call | solution.py:223
  27.6 9.2 %all-to-all-start = ((bf16[16,48,1024]{2,1,0:T(8,128)(2,1)}), bf16[16,48,1024]{2,1,0:T(8,128)(2,1)S(1)}, u32[]{:S(2)}, u32[]{:S(2)}) async-start(bf16[16,48,1024]{2,1,0:T(8,128)(2,1)} %bitcast.4), calls=%async_computation | async-start | bytes 3145728 | tf_op jit(solution)/shard_map/all_to_all | solution.py:377
  36.7 0.0 copy-done.12
  36.8 1.7 %collective-permute-start.7 = (bf16[224,768]{1,0:T(8,128)(2,1)S(1)}, bf16[224,768]{1,0:T(8,128)(2,1)S(1)}, u32[]{:S(2)}, u32[]{:S(2)}) collective-permute-start(bf16[224,768]{1,0:T(8,128)(2,1)S(1)} %copy-done.12), channel_id=1, source_target_pairs={{0,4},{2,6},{4,8},{6,10},{8,12},{10,14},{12,0},{14,2},{1,5},{3,7},... | collective-permute-start | bytes 1032200 | tf_op jit(solution)/shard_map/ppermute | solution.py:369
  38.4 0.0 copy-done.11
  38.4 1.6 %collective-permute-start.8 = (bf16[224,768]{1,0:T(8,128)(2,1)S(1)}, bf16[224,768]{1,0:T(8,128)(2,1)S(1)}, u32[]{:S(2)}, u32[]{:S(2)}) collective-permute-start(bf16[224,768]{1,0:T(8,128)(2,1)S(1)} %copy-done.11), channel_id=1, source_target_pairs={{0,8},{2,10},{4,12},{6,14},{8,0},{10,2},{12,4},{14,6},{1,9},{3,11}... | collective-permute-start | bytes 1032200 | tf_op jit(solution)/shard_map/ppermute | solution.py:369
  40.0 0.0 copy-done.10
  40.0 0.9 collective-permute-start.9
  41.0 3.2 %collective-permute-done.7.refs_1_ = bf16[224,768]{1,0:T(8,128)(2,1)S(1)} collective-permute-done((bf16[224,768]{1,0:T(8,128)(2,1)S(1)}, bf16[224,768]{1,0:T(8,128)(2,1)S(1)}, u32[]{:S(2)}, u32[]{:S(2)}) %collective-permute-start.7) | collective-permute-done | bytes 344096 | tf_op jit(solution)/shard_map/ppermute | solution.py:369
  44.1 6.1 %collective-permute-done.8.refs_2_ = bf16[224,768]{1,0:T(8,128)(2,1)S(1)} collective-permute-done((bf16[224,768]{1,0:T(8,128)(2,1)S(1)}, bf16[224,768]{1,0:T(8,128)(2,1)S(1)}, u32[]{:S(2)}, u32[]{:S(2)}) %collective-permute-start.8) | collective-permute-done | bytes 344096 | tf_op jit(solution)/shard_map/ppermute | solution.py:369
  50.3 2.5 %collective-permute-done.9.refs_3_ = bf16[224,768]{1,0:T(8,128)(2,1)S(1)} collective-permute-done((bf16[224,768]{1,0:T(8,128)(2,1)S(1)}, bf16[224,768]{1,0:T(8,128)(2,1)S(1)}, u32[]{:S(2)}, u32[]{:S(2)}) %collective-permute-start.9) | collective-permute-done | bytes 344096 | tf_op jit(solution)/shard_map/ppermute | solution.py:369
  52.8 0.9 add_grads.1
  53.6 4.7 %collective-permute-start.10 = (bf16[112,768]{1,0:T(8,128)(2,1)S(1)}, bf16[112,768]{1,0:T(8,128)(2,1)S(1)}, u32[]{:S(2)}, u32[]{:S(2)}) collective-permute-start(bf16[112,768]{1,0:T(8,128)(2,1)S(1)} %get-tuple-element.23), channel_id=1, source_target_pairs={{0,2},{2,0},{4,6},{6,4},{8,10},{10,8},{12,14},{14,12},{1,3},{3,1},... | collective-permute-start | bytes 516104 | tf_op jit(solution)/shard_map/ppermute | solution.py:379
  58.3 7.5 %collective-permute-done.10.came_ref = bf16[112,768]{1,0:T(8,128)(2,1)S(1)} collective-permute-done((bf16[112,768]{1,0:T(8,128)(2,1)S(1)}, bf16[112,768]{1,0:T(8,128)(2,1)S(1)}, u32[]{:S(2)}, u32[]{:S(2)}) %collective-permute-start.10) | collective-permute-done | bytes 172064 | tf_op jit(solution)/shard_map/ppermute | solution.py:379
  65.8 4.1 %all-to-all-done.parts_ref = bf16[16,48,1024]{2,1,0:T(8,128)(2,1)S(1)} async-done(((bf16[16,48,1024]{2,1,0:T(8,128)(2,1)}), bf16[16,48,1024]{2,1,0:T(8,128)(2,1)S(1)}, u32[]{:S(2)}, u32[]{:S(2)}) %all-to-all-start) | async-done | bytes 1572896 | tf_op jit(solution)/shard_map/all_to_all | solution.py:377
  69.9 1.5 %add_parts.1 = (bf16[16,48,1024]{2,1,0:T(8,128)(2,1)}, bf16[112,768]{1,0:T(8,128)(2,1)S(1)}) custom-call(bf16[16,48,1024]{2,1,0:T(8,128)(2,1)S(1)} %all-to-all-done.parts_ref, bf16[112,768]{1,0:T(8,128)(2,1)S(1)} %get-tuple-element.22.keep_ref, bf16[112,768]{1,0:T(8,128)(2,1)S(1)} %collective-permute-done.10.came_ref), custom_call_target="tpu_custom_call" | custom-call | flops 786432 | bytes 3145728 | tf_op jit(solution)/shard_map/add_parts/pallas_call | solution.py:265
  71.3 7.8 %all-to-all-start.1 = ((bf16[16,48,1024]{2,1,0:T(8,128)(2,1)}), bf16[16,48,1024]{2,1,0:T(8,128)(2,1)S(1)}, u32[]{:S(2)}, u32[]{:S(2)}) async-start(bf16[16,48,1024]{2,1,0:T(8,128)(2,1)} %get-tuple-element.27), calls=%async_computation.1 | async-start | bytes 3145728 | tf_op jit(solution)/shard_map/all_to_all | solution.py:380
  79.1 3.4 %collective-permute-start.11 = (bf16[112,768]{1,0:T(8,128)(2,1)S(1)}, bf16[112,768]{1,0:T(8,128)(2,1)S(1)}, u32[]{:S(2)}, u32[]{:S(2)}) collective-permute-start(bf16[112,768]{1,0:T(8,128)(2,1)S(1)} %get-tuple-element.24.own_ref), channel_id=1, source_target_pairs={{0,2},{2,0},{4,6},{6,4},{8,10},{10,8},{12,14},{14,12},{1,3},{3,1},... | collective-permute-start | bytes 516104 | tf_op jit(solution)/shard_map/ppermute | solution.py:381
  82.5 7.8 %collective-permute-done.11.other_ref = bf16[112,768]{1,0:T(8,128)(2,1)S(1)} collective-permute-done((bf16[112,768]{1,0:T(8,128)(2,1)S(1)}, bf16[112,768]{1,0:T(8,128)(2,1)S(1)}, u32[]{:S(2)}, u32[]{:S(2)}) %collective-permute-start.11) | collective-permute-done | bytes 172064 | tf_op jit(solution)/shard_map/ppermute | solution.py:381
  90.3 0.6 pair_grads.1.refs_0_
  90.8 0.3 collective-permute-start.14
  91.1 3.5 %collective-permute-start.13 = (bf16[224,768]{1,0:T(8,128)(2,1)S(1)}, bf16[224,768]{1,0:T(8,128)(2,1)S(1)}, u32[]{:S(2)}, u32[]{:S(2)}) collective-permute-start(bf16[224,768]{1,0:T(8,128)(2,1)S(1)} %pair_grads.1.refs_0_), channel_id=1, source_target_pairs={{0,8},{2,10},{4,12},{6,14},{8,0},{10,2},{12,4},{14,6},{1,9},{3,11}... | collective-permute-start | bytes 1032200 | tf_op jit(solution)/shard_map/ppermute | solution.py:369
  94.6 0.0 collective-permute-start.12
  94.6 2.0 %copy-done = f32[896,1024]{1,0:T(8,128)S(1)} copy-done((f32[896,1024]{1,0:T(8,128)S(1)}, f32[896,1024]{1,0:T(8,128)}, u32[]{:S(2)}) %copy-start) | copy-done | bytes 3670040
  96.7 0.5 inverse_of.1.refs_4_.inverse_ref
  97.2 0.5 collective-permute-done.14.refs_3_
  97.8 1.8 %collective-permute-done.13.refs_2_ = bf16[224,768]{1,0:T(8,128)(2,1)S(1)} collective-permute-done((bf16[224,768]{1,0:T(8,128)(2,1)S(1)}, bf16[224,768]{1,0:T(8,128)(2,1)S(1)}, u32[]{:S(2)}, u32[]{:S(2)}) %collective-permute-start.13) | collective-permute-done | bytes 344096 | tf_op jit(solution)/shard_map/ppermute | solution.py:369
  99.5 7.5 %collective-permute-done.12.refs_1_ = bf16[224,768]{1,0:T(8,128)(2,1)S(1)} collective-permute-done((bf16[224,768]{1,0:T(8,128)(2,1)S(1)}, bf16[224,768]{1,0:T(8,128)(2,1)S(1)}, u32[]{:S(2)}, u32[]{:S(2)}) %collective-permute-start.12) | collective-permute-done | bytes 344096 | tf_op jit(solution)/shard_map/ppermute | solution.py:369
  107.1 0.7 join_grads.1
  107.8 0.0 copy-start.6
  107.8 1.1 copy-done.6
  108.8 0.8 copy-done.8
  109.6 5.3 %all-to-all-done.1 = bf16[16,48,1024]{2,1,0:T(8,128)(2,1)S(1)} async-done(((bf16[16,48,1024]{2,1,0:T(8,128)(2,1)}), bf16[16,48,1024]{2,1,0:T(8,128)(2,1)S(1)}, u32[]{:S(2)}, u32[]{:S(2)}) %all-to-all-start.1) | async-done | bytes 1572896 | tf_op jit(solution)/shard_map/all_to_all | solution.py:380
  114.9 0.1 query_rows.1
  115.0 4.0 %collective-permute-start.16 = (bf16[256,1024]{1,0:T(8,128)(2,1)S(1)}, bf16[256,1024]{1,0:T(8,128)(2,1)S(1)}, u32[]{:S(2)}, u32[]{:S(2)}) collective-permute-start(bf16[256,1024]{1,0:T(8,128)(2,1)S(1)} %query_rows.1), channel_id=1, source_target_pairs={{0,1},{1,0},{2,3},{3,2},{4,5},{5,4},{6,7},{7,6},{8,9},{9,8},{10,11... | collective-permute-start | bytes 1572872 | tf_op jit(solution)/shard_map/ppermute | solution.py:385
  119.0 0.9 collective-permute-start.15
  119.8 1.4 collective-permute-done.15.go_ref
  121.3 0.0 collective-permute-done.16.ao_ref
  121.3 6.6 %tile_scores.1 = f32[128,1,128]{2,1,0:T(1,128)S(1)} custom-call(s32[3]{0:T(128)S(1)} %copy-done.4, bf16[896,768]{1,0:T(8,128)(2,1)S(1)} %copy-done.7, bf16[896,256]{1,0:T(8,128)(2,1)S(1)} %collective-permute-done.15.go_ref, bf16[768,1024]{1,0:T(8,128)(2,1)S(1)} %bitcast.8, bf16[256,1024]{1,0:T(8,128)(2,1)S(1)} %collective-permute-done.16.ao_ref, ...), custom_call_target="tpu_custom_call" | custom-call | flops 3758096384 | bytes 8388608 | tf_op jit(solution)/shard_map/tile_scores/pallas_call | solution.py:349
  127.9 19.9 %all_to_all.15 = f32[128,1,128]{2,1,0:T(1,128)S(1)} all-to-all(f32[128,1,128]{2,1,0:T(1,128)S(1)} %tile_scores.1), channel_id=1, replica_groups=mesh['shard'=16,'dp'=8,'buffer'=2] {'shard','dp'}, dimensions={0} | all-to-all | bytes 131072 | tf_op jit(solution)/shard_map/all_to_all | solution.py:387
  147.9 0.2 reduce_sum.9
  148.0 0.7 reshape.19
  (14 shorter events, 0.0 us)
Async XLA Ops:
  2.7 20.7 %copy-start.1 = (bf16[1024,512]{1,0:T(8,128)(2,1)S(1)}, bf16[1024,512]{1,0:T(8,128)(2,1)}, u32[]{:S(2)}) copy-start(bf16[1024,512]{1,0:T(8,128)(2,1)} %refs_8_.1) | copy-start | bytes 3145732
  2.7 20.7 %copy-start.2 = (bf16[1,96,512]{2,1,0:T(8,128)(2,1)S(1)}, bf16[1,96,512]{2,1,0:T(8,128)(2,1)}, u32[]{:S(2)}) copy-start(bf16[1,96,512]{2,1,0:T(8,128)(2,1)} %pack_acts.1) | copy-start | bytes 294916
  2.7 20.7 %copy-start.4 = (s32[3]{0:T(128)S(1)}, s32[3]{0:T(128)}, u32[]{:S(2)}) copy-start(s32[3]{0:T(128)} %pad_add_fusion.core_ref.where_ref) | copy-start | bytes 40
  2.7 10.4 %collective-permute-start.6 = (bf16[96,512]{1,0:T(8,128)(2,1)}, bf16[96,512]{1,0:T(8,128)(2,1)S(1)}, u32[]{:S(2)}, u32[]{:S(2)}) collective-permute-start(bf16[96,512]{1,0:T(8,128)(2,1)} %bitcast.9), channel_id=1, source_target_pairs={{0,14},{2,0},{4,2},{6,4},{8,6},{10,8},{12,10},{14,12},{1,15},{3,1}... | collective-permute-start | bytes 294920 | tf_op jit(solution)/shard_map/ppermute | solution.py:373
  8.8 5.7 %collective-permute-start.5 = (bf16[96,512]{1,0:T(8,128)(2,1)}, bf16[96,512]{1,0:T(8,128)(2,1)S(1)}, u32[]{:S(2)}, u32[]{:S(2)}) collective-permute-start(bf16[96,512]{1,0:T(8,128)(2,1)} %bitcast.10), channel_id=1, source_target_pairs={{0,12},{2,14},{4,0},{6,2},{8,4},{10,6},{12,8},{14,10},{1,13},{3,15... | collective-permute-start | bytes 294920 | tf_op jit(solution)/shard_map/ppermute | solution.py:373
  9.2 14.2 %collective-permute-start.4 = (bf16[96,512]{1,0:T(8,128)(2,1)}, bf16[96,512]{1,0:T(8,128)(2,1)S(1)}, u32[]{:S(2)}, u32[]{:S(2)}) collective-permute-start(bf16[96,512]{1,0:T(8,128)(2,1)} %bitcast.11), channel_id=1, source_target_pairs={{0,10},{2,12},{4,14},{6,0},{8,2},{10,4},{12,6},{14,8},{1,11},{3,13... | collective-permute-start | bytes 294920 | tf_op jit(solution)/shard_map/ppermute | solution.py:373
  9.3 14.0 %collective-permute-start.3 = (bf16[96,512]{1,0:T(8,128)(2,1)}, bf16[96,512]{1,0:T(8,128)(2,1)S(1)}, u32[]{:S(2)}, u32[]{:S(2)}) collective-permute-start(bf16[96,512]{1,0:T(8,128)(2,1)} %bitcast.12), channel_id=1, source_target_pairs={{0,8},{2,10},{4,12},{6,14},{8,0},{10,2},{12,4},{14,6},{1,9},{3,11}... | collective-permute-start | bytes 294920 | tf_op jit(solution)/shard_map/ppermute | solution.py:373
  12.0 11.4 %collective-permute-start.2 = (bf16[96,512]{1,0:T(8,128)(2,1)}, bf16[96,512]{1,0:T(8,128)(2,1)S(1)}, u32[]{:S(2)}, u32[]{:S(2)}) collective-permute-start(bf16[96,512]{1,0:T(8,128)(2,1)} %bitcast.13), channel_id=1, source_target_pairs={{0,6},{2,8},{4,10},{6,12},{8,14},{10,0},{12,2},{14,4},{1,7},{3,9},... | collective-permute-start | bytes 294920 | tf_op jit(solution)/shard_map/ppermute | solution.py:373
  13.1 10.3 %collective-permute-start.1 = (bf16[96,512]{1,0:T(8,128)(2,1)}, bf16[96,512]{1,0:T(8,128)(2,1)S(1)}, u32[]{:S(2)}, u32[]{:S(2)}) collective-permute-start(bf16[96,512]{1,0:T(8,128)(2,1)} %bitcast.14), channel_id=1, source_target_pairs={{0,4},{2,6},{4,8},{6,10},{8,12},{10,14},{12,0},{14,2},{1,5},{3,7},... | collective-permute-start | bytes 294920 | tf_op jit(solution)/shard_map/ppermute | solution.py:373
  14.5 9.0 %collective-permute-start = (bf16[96,512]{1,0:T(8,128)(2,1)}, bf16[96,512]{1,0:T(8,128)(2,1)S(1)}, u32[]{:S(2)}, u32[]{:S(2)}) collective-permute-start(bf16[96,512]{1,0:T(8,128)(2,1)} %bitcast.15), channel_id=1, source_target_pairs={{0,2},{2,4},{4,6},{6,8},{8,10},{10,12},{12,14},{14,0},{1,3},{3,5},... | collective-permute-start | bytes 294920 | tf_op jit(solution)/shard_map/ppermute | solution.py:373
  23.5 0.7 copy-start.5
  27.6 9.2 %copy-start.12 = (bf16[224,768]{1,0:T(8,128)(2,1)S(1)}, bf16[224,768]{1,0:T(8,128)(2,1)}, u32[]{:S(2)}) copy-start(bf16[224,768]{1,0:T(8,128)(2,1)} %get-tuple-element.19) | copy-start | bytes 1032196
  27.6 10.9 %copy-start.11 = (bf16[224,768]{1,0:T(8,128)(2,1)S(1)}, bf16[224,768]{1,0:T(8,128)(2,1)}, u32[]{:S(2)}) copy-start(bf16[224,768]{1,0:T(8,128)(2,1)} %get-tuple-element.20) | copy-start | bytes 1032196
  27.6 12.4 %copy-start.10 = (bf16[224,768]{1,0:T(8,128)(2,1)S(1)}, bf16[224,768]{1,0:T(8,128)(2,1)}, u32[]{:S(2)}) copy-start(bf16[224,768]{1,0:T(8,128)(2,1)} %get-tuple-element.21) | copy-start | bytes 1032196
  27.6 25.2 %copy-start.3 = (bf16[224,768]{1,0:T(8,128)(2,1)S(1)}, bf16[224,768]{1,0:T(8,128)(2,1)}, u32[]{:S(2)}) copy-start(bf16[224,768]{1,0:T(8,128)(2,1)} %get-tuple-element.18.refs_0_) | copy-start | bytes 1032196
  27.6 42.3 %all-to-all-start = ((bf16[16,48,1024]{2,1,0:T(8,128)(2,1)}), bf16[16,48,1024]{2,1,0:T(8,128)(2,1)S(1)}, u32[]{:S(2)}, u32[]{:S(2)}) async-start(bf16[16,48,1024]{2,1,0:T(8,128)(2,1)} %bitcast.4), calls=%async_computation | async-start | bytes 3145728 | tf_op jit(solution)/shard_map/all_to_all | solution.py:377
  36.8 7.4 %collective-permute-start.7 = (bf16[224,768]{1,0:T(8,128)(2,1)S(1)}, bf16[224,768]{1,0:T(8,128)(2,1)S(1)}, u32[]{:S(2)}, u32[]{:S(2)}) collective-permute-start(bf16[224,768]{1,0:T(8,128)(2,1)S(1)} %copy-done.12), channel_id=1, source_target_pairs={{0,4},{2,6},{4,8},{6,10},{8,12},{10,14},{12,0},{14,2},{1,5},{3,7},... | collective-permute-start | bytes 1032200 | tf_op jit(solution)/shard_map/ppermute | solution.py:369
  38.4 11.8 %collective-permute-start.8 = (bf16[224,768]{1,0:T(8,128)(2,1)S(1)}, bf16[224,768]{1,0:T(8,128)(2,1)S(1)}, u32[]{:S(2)}, u32[]{:S(2)}) collective-permute-start(bf16[224,768]{1,0:T(8,128)(2,1)S(1)} %copy-done.11), channel_id=1, source_target_pairs={{0,8},{2,10},{4,12},{6,14},{8,0},{10,2},{12,4},{14,6},{1,9},{3,11}... | collective-permute-start | bytes 1032200 | tf_op jit(solution)/shard_map/ppermute | solution.py:369
  40.0 12.8 %collective-permute-start.9 = (bf16[224,768]{1,0:T(8,128)(2,1)S(1)}, bf16[224,768]{1,0:T(8,128)(2,1)S(1)}, u32[]{:S(2)}, u32[]{:S(2)}) collective-permute-start(bf16[224,768]{1,0:T(8,128)(2,1)S(1)} %copy-done.10), channel_id=1, source_target_pairs={{0,12},{2,14},{4,0},{6,2},{8,4},{10,6},{12,8},{14,10},{1,13},{3,15... | collective-permute-start | bytes 1032200 | tf_op jit(solution)/shard_map/ppermute | solution.py:369
  53.6 12.1 %collective-permute-start.10 = (bf16[112,768]{1,0:T(8,128)(2,1)S(1)}, bf16[112,768]{1,0:T(8,128)(2,1)S(1)}, u32[]{:S(2)}, u32[]{:S(2)}) collective-permute-start(bf16[112,768]{1,0:T(8,128)(2,1)S(1)} %get-tuple-element.23), channel_id=1, source_target_pairs={{0,2},{2,0},{4,6},{6,4},{8,10},{10,8},{12,14},{14,12},{1,3},{3,1},... | collective-permute-start | bytes 516104 | tf_op jit(solution)/shard_map/ppermute | solution.py:379
  71.3 43.6 %all-to-all-start.1 = ((bf16[16,48,1024]{2,1,0:T(8,128)(2,1)}), bf16[16,48,1024]{2,1,0:T(8,128)(2,1)S(1)}, u32[]{:S(2)}, u32[]{:S(2)}) async-start(bf16[16,48,1024]{2,1,0:T(8,128)(2,1)} %get-tuple-element.27), calls=%async_computation.1 | async-start | bytes 3145728 | tf_op jit(solution)/shard_map/all_to_all | solution.py:380
  79.1 11.1 %collective-permute-start.11 = (bf16[112,768]{1,0:T(8,128)(2,1)S(1)}, bf16[112,768]{1,0:T(8,128)(2,1)S(1)}, u32[]{:S(2)}, u32[]{:S(2)}) collective-permute-start(bf16[112,768]{1,0:T(8,128)(2,1)S(1)} %get-tuple-element.24.own_ref), channel_id=1, source_target_pairs={{0,2},{2,0},{4,6},{6,4},{8,10},{10,8},{12,14},{14,12},{1,3},{3,1},... | collective-permute-start | bytes 516104 | tf_op jit(solution)/shard_map/ppermute | solution.py:381
  90.8 6.9 %collective-permute-start.14 = (bf16[224,768]{1,0:T(8,128)(2,1)S(1)}, bf16[224,768]{1,0:T(8,128)(2,1)S(1)}, u32[]{:S(2)}, u32[]{:S(2)}) collective-permute-start(bf16[224,768]{1,0:T(8,128)(2,1)S(1)} %pair_grads.1.refs_0_), channel_id=1, source_target_pairs={{0,12},{2,14},{4,0},{6,2},{8,4},{10,6},{12,8},{14,10},{1,13},{3,15... | collective-permute-start | bytes 1032200 | tf_op jit(solution)/shard_map/ppermute | solution.py:369
  91.1 8.4 %collective-permute-start.13 = (bf16[224,768]{1,0:T(8,128)(2,1)S(1)}, bf16[224,768]{1,0:T(8,128)(2,1)S(1)}, u32[]{:S(2)}, u32[]{:S(2)}) collective-permute-start(bf16[224,768]{1,0:T(8,128)(2,1)S(1)} %pair_grads.1.refs_0_), channel_id=1, source_target_pairs={{0,8},{2,10},{4,12},{6,14},{8,0},{10,2},{12,4},{14,6},{1,9},{3,11}... | collective-permute-start | bytes 1032200 | tf_op jit(solution)/shard_map/ppermute | solution.py:369
  94.6 12.5 %collective-permute-start.12 = (bf16[224,768]{1,0:T(8,128)(2,1)S(1)}, bf16[224,768]{1,0:T(8,128)(2,1)S(1)}, u32[]{:S(2)}, u32[]{:S(2)}) collective-permute-start(bf16[224,768]{1,0:T(8,128)(2,1)S(1)} %pair_grads.1.refs_0_), channel_id=1, source_target_pairs={{0,4},{2,6},{4,8},{6,10},{8,12},{10,14},{12,0},{14,2},{1,5},{3,7},... | collective-permute-start | bytes 1032200 | tf_op jit(solution)/shard_map/ppermute | solution.py:369
  94.6 2.0 %copy-start = (f32[896,1024]{1,0:T(8,128)S(1)}, f32[896,1024]{1,0:T(8,128)}, u32[]{:S(2)}) copy-start(f32[896,1024]{1,0:T(8,128)} %eig_ref.1) | copy-start | bytes 11010052
  107.8 1.1 copy-start.6
  108.8 0.8 copy-start.8
  114.9 4.1 %copy-start.9 = (bf16[896,256]{1,0:T(8,128)(2,1)S(1)}, bf16[896,256]{1,0:T(8,128)(2,1)}, u32[]{:S(2)}) copy-start(bf16[896,256]{1,0:T(8,128)(2,1)} %copy-done.8) | copy-start | bytes 1376260
  114.9 6.4 %copy-start.7 = (bf16[896,768]{1,0:T(8,128)(2,1)S(1)}, bf16[896,768]{1,0:T(8,128)(2,1)}, u32[]{:S(2)}) copy-start(bf16[896,768]{1,0:T(8,128)(2,1)} %copy-done.6) | copy-start | bytes 4128772
  115.0 6.3 %collective-permute-start.16 = (bf16[256,1024]{1,0:T(8,128)(2,1)S(1)}, bf16[256,1024]{1,0:T(8,128)(2,1)S(1)}, u32[]{:S(2)}, u32[]{:S(2)}) collective-permute-start(bf16[256,1024]{1,0:T(8,128)(2,1)S(1)} %query_rows.1), channel_id=1, source_target_pairs={{0,1},{1,0},{2,3},{3,2},{4,5},{5,4},{6,7},{7,6},{8,9},{9,8},{10,11... | collective-permute-start | bytes 1572872 | tf_op jit(solution)/shard_map/ppermute | solution.py:385
  119.0 2.3 %collective-permute-start.15 = (bf16[896,256]{1,0:T(8,128)(2,1)S(1)}, bf16[896,256]{1,0:T(8,128)(2,1)S(1)}, u32[]{:S(2)}, u32[]{:S(2)}) collective-permute-start(bf16[896,256]{1,0:T(8,128)(2,1)S(1)} %copy-done.9), channel_id=1, source_target_pairs={{0,1},{1,0},{2,3},{3,2},{4,5},{5,4},{6,7},{7,6},{8,9},{9,8},{10,11... | collective-permute-start | bytes 1376264 | tf_op jit(solution)/shard_map/ppermute | solution.py:384

commit v6 on v4

--- a/solution.py
+++ b/solution.py
@@ -211,13 +211,13 @@
     outer = basis.shape[0]
     return pl.pallas_call(
         rotate_act_kernel,
-        grid=(outer // 256,),
+        grid=(outer // 512,),
         in_specs=[
             pl.BlockSpec((n_dp, rows, inner), lambda i: (0, 0, 0)),
-            pl.BlockSpec((256, inner), lambda i: (i, 0)),
+            pl.BlockSpec((512, inner), lambda i: (i, 0)),
             TOKEN,
         ],
-        out_specs=pl.BlockSpec((768, 256), lambda i: (0, i)),
+        out_specs=pl.BlockSpec((768, 512), lambda i: (0, i)),
         out_shape=jax.ShapeDtypeStruct((768, outer), BF16),
         scratch_shapes=[pltpu.VMEM((768, inner), BF16)],
         compiler_params=params(16),
@@ -260,15 +260,15 @@
     high, wide = keep.shape
     return pl.pallas_call(
         add_parts_kernel,
-        grid=(2,),
+        grid=(1,),
         in_specs=[
-            pl.BlockSpec((count, rows, width // 2), lambda i: (0, 0, i)),
-            pl.BlockSpec((high, wide // 2), lambda i: (0, i)),
-            pl.BlockSpec((high, wide // 2), lambda i: (0, i)),
+            pl.BlockSpec((count, rows, width), lambda i: (0, 0, i)),
+            pl.BlockSpec((high, wide), lambda i: (0, i)),
+            pl.BlockSpec((high, wide), lambda i: (0, i)),
         ],
         out_specs=[
-            pl.BlockSpec((count, rows, width // 2), lambda i: (0, 0, i)),
-            pl.BlockSpec((high, wide // 2), lambda i: (0, i)),
+            pl.BlockSpec((count, rows, width), lambda i: (0, 0, i)),
+            pl.BlockSpec((high, wide), lambda i: (0, i)),
         ],
         out_shape=[jax.ShapeDtypeStruct(parts.shape, BF16), jax.ShapeDtypeStruct(keep.shape, BF16)],
         compiler_params=params(16),

time: 149 us -> 149 us (level)
  no operation moved by 1% of the time
where the time goes in v6:
time: 149 us; the launch traced here: 148 us
  waiting for transfers between devices  64.8 us (43%)
  starting transfers between devices  33.4 us (22%)
  Pallas kernels  23.3 us (16%)
  blocking collectives  20.6 us (14%)
  local copies, waits for them, and re-layouts  5.27 us (4%)
    ppermute x6, waiting for transfers between devices, along_y(): lax.ppermute(piece, 'dp', [(d, (d + 2 * k) % n_dp) for d in range(n_dp)])  29.4 us
    all_to_all x1, blocking collectives, local(): every = lax.all_to_all(mine, ('shard', 'dp'), 0, 0, tiled=True)  20.6 us
    ppermute x1, waiting for transfers between devices, local(): pair = pair_grads(where, piece, lax.ppermute(piece, 'dp', partner))  10.8 us
    ppermute x1, waiting for transfers between devices, local(): sums, piece = add_parts(parts, keep, lax.ppermute(send, 'dp', partner))  9.73 us
    all_to_all x1, starting transfers between devices, local(): lax.all_to_all(act_part.reshape(n_shard, -1, act_part.shape[1]), 'shard',...  8.46 us
    pallas_call x1, Pallas kernels, rotate_grad(): pl.pallas_call(rotate_grad_kernel, grid_spec=grid_spec, out_shape=[jax.Sh...  7.64 us
    all_to_all x1, starting transfers between devices, local(): lax.all_to_all(pack_acts(where, query_act, buffer_act, n_dp), 'dp', 0, 0,...  7.48 us
    pallas_call x1, Pallas kernels, tile_scores(): pl.pallas_call(scores_kernel, grid_spec=grid_spec, out_shape=jax.ShapeDty...  6.8 us
  transfers between devices with their start and end apart: 13, of which 12 were waited for; matrix products, arithmetic and copies ran while one was open for 0% of the time, Pallas kernels for 7%

profile of v6, /device:TPU:1, one launch (start us, length us, event | category | flops | bytes accessed | tf_op | source)
XLA Modules:
  0.0 148.3 jit_solution(9523185961145386063)
XLA Ops:
  0.0 0.7 pad_add_fusion.core_ref.where_ref
  0.7 2.4 %pack_acts.1 = bf16[8,96,512]{2,1,0:T(8,128)(2,1)} custom-call(s32[3]{0:T(128)} %pad_add_fusion.core_ref.where_ref, bf16[4,16,512]{2,1,0:T(8,128)(2,1)} %qa_ref.1, bf16[4,16,512]{2,1,0:T(8,128)(2,1)} %ba_ref.1), custom_call_target="tpu_custom_call" | custom-call | bytes 2097152 | tf_op jit(solution)/shard_map/pack_acts/pallas_call | solution.py:45
  3.1 7.5 %all-to-all-start = ((bf16[8,96,512]{2,1,0:T(8,128)(2,1)}), bf16[8,96,512]{2,1,0:T(8,128)(2,1)S(1)}, u32[]{:S(2)}, u32[]{:S(2)}) async-start(bf16[8,96,512]{2,1,0:T(8,128)(2,1)} %pack_acts.1), calls=%async_computation | async-start | bytes 1572864 | tf_op jit(solution)/shard_map/all_to_all | solution.py:367
  10.6 0.0 copy-start.1
  10.6 7.6 %rotate_grad.1 = (bf16[224,768]{1,0:T(8,128)(2,1)}, bf16[224,768]{1,0:T(8,128)(2,1)}, bf16[224,768]{1,0:T(8,128)(2,1)}, bf16[224,768]{1,0:T(8,128)(2,1)}, bf16[16,128]{1,0:T(8,128)(2,1)}) custom-call(s32[3]{0:T(128)} %pad_add_fusion.core_ref.where_ref, bf16[4,128,1792]{2,1,0:T(8,128)(2,1)} %qg_ref.1, bf16[4,128,1792]{2,1,0:T(8,128)(2,1)} %bg_ref.1, ...), custom_call_target="tpu_custom_call" | custom-call | flops 2466250752 | bytes 8388608 | tf_op jit(solution)/shard_map/rotate_grad/pallas_call | solution.py:92
  18.2 5.5 %all-to-all-done.recv_ref = bf16[8,96,512]{2,1,0:T(8,128)(2,1)S(1)} async-done(((bf16[8,96,512]{2,1,0:T(8,128)(2,1)}), bf16[8,96,512]{2,1,0:T(8,128)(2,1)S(1)}, u32[]{:S(2)}, u32[]{:S(2)}) %all-to-all-start) | async-done | bytes 786464 | tf_op jit(solution)/shard_map/all_to_all | solution.py:367
  23.8 0.0 copy-done.1
  23.8 0.0 copy-start.4
  23.8 0.7 copy-done.4
  24.5 2.2 %rotate_act.1 = bf16[768,1024]{1,0:T(8,128)(2,1)} custom-call(bf16[8,96,512]{2,1,0:T(8,128)(2,1)S(1)} %all-to-all-done.recv_ref, bf16[1024,512]{1,0:T(8,128)(2,1)S(1)} %copy-done.1, bf16[16,128]{1,0:T(8,128)(2,1)S(1)} %copy-done.4), custom_call_target="tpu_custom_call" | custom-call | flops 805306368 | bytes 6291456 | tf_op jit(solution)/shard_map/rotate_act/pallas_call | solution.py:212
  26.7 0.0 copy-start.11
  26.7 0.0 copy-start.10
  26.7 0.0 copy-start.9
  26.7 0.0 copy-start.2
  26.7 0.0 copy-start.3
  26.7 8.5 %all-to-all-start.1 = ((bf16[16,48,1024]{2,1,0:T(8,128)(2,1)}), bf16[16,48,1024]{2,1,0:T(8,128)(2,1)S(1)}, u32[]{:S(2)}, u32[]{:S(2)}) async-start(bf16[16,48,1024]{2,1,0:T(8,128)(2,1)} %bitcast.3), calls=%async_computation.1 | async-start | bytes 3145728 | tf_op jit(solution)/shard_map/all_to_all | solution.py:370
  35.2 0.0 copy-done.11
  35.2 0.1 collective-permute-start
  35.3 0.0 copy-done.10
  35.3 2.0 %collective-permute-start.1 = (bf16[224,768]{1,0:T(8,128)(2,1)S(1)}, bf16[224,768]{1,0:T(8,128)(2,1)S(1)}, u32[]{:S(2)}, u32[]{:S(2)}) collective-permute-start(bf16[224,768]{1,0:T(8,128)(2,1)S(1)} %copy-done.10), channel_id=1, source_target_pairs={{0,8},{2,10},{4,12},{6,14},{8,0},{10,2},{12,4},{14,6},{1,9},{3,11}... | collective-permute-start | bytes 1032200 | tf_op jit(solution)/shard_map/ppermute | solution.py:365
  37.3 0.0 copy-done.9
  37.3 0.9 collective-permute-start.2
  38.2 5.7 %collective-permute-done.refs_1_ = bf16[224,768]{1,0:T(8,128)(2,1)S(1)} collective-permute-done((bf16[224,768]{1,0:T(8,128)(2,1)S(1)}, bf16[224,768]{1,0:T(8,128)(2,1)S(1)}, u32[]{:S(2)}, u32[]{:S(2)}) %collective-permute-start) | collective-permute-done | bytes 344096 | tf_op jit(solution)/shard_map/ppermute | solution.py:365
  43.9 6.8 %collective-permute-done.1.refs_2_ = bf16[224,768]{1,0:T(8,128)(2,1)S(1)} collective-permute-done((bf16[224,768]{1,0:T(8,128)(2,1)S(1)}, bf16[224,768]{1,0:T(8,128)(2,1)S(1)}, u32[]{:S(2)}, u32[]{:S(2)}) %collective-permute-start.1) | collective-permute-done | bytes 344096 | tf_op jit(solution)/shard_map/ppermute | solution.py:365
  50.7 2.7 %collective-permute-done.2.refs_3_ = bf16[224,768]{1,0:T(8,128)(2,1)S(1)} collective-permute-done((bf16[224,768]{1,0:T(8,128)(2,1)S(1)}, bf16[224,768]{1,0:T(8,128)(2,1)S(1)}, u32[]{:S(2)}, u32[]{:S(2)}) %collective-permute-start.2) | collective-permute-done | bytes 344096 | tf_op jit(solution)/shard_map/ppermute | solution.py:365
  53.3 0.0 copy-done.2
  53.3 0.0 copy-done.3
  53.3 0.9 add_grads.1
  54.2 1.3 collective-permute-start.3
  55.5 9.7 %collective-permute-done.3.came_ref = bf16[112,768]{1,0:T(8,128)(2,1)S(1)} collective-permute-done((bf16[112,768]{1,0:T(8,128)(2,1)S(1)}, bf16[112,768]{1,0:T(8,128)(2,1)S(1)}, u32[]{:S(2)}, u32[]{:S(2)}) %collective-permute-start.3) | collective-permute-done | bytes 172064 | tf_op jit(solution)/shard_map/ppermute | solution.py:372
  65.3 6.0 %all-to-all-done.1.parts_ref = bf16[16,48,1024]{2,1,0:T(8,128)(2,1)S(1)} async-done(((bf16[16,48,1024]{2,1,0:T(8,128)(2,1)}), bf16[16,48,1024]{2,1,0:T(8,128)(2,1)S(1)}, u32[]{:S(2)}, u32[]{:S(2)}) %all-to-all-start.1) | async-done | bytes 1572896 | tf_op jit(solution)/shard_map/all_to_all | solution.py:370
  71.3 1.5 %add_parts.1 = (bf16[16,48,1024]{2,1,0:T(8,128)(2,1)}, bf16[112,768]{1,0:T(8,128)(2,1)S(1)}) custom-call(bf16[16,48,1024]{2,1,0:T(8,128)(2,1)S(1)} %all-to-all-done.1.parts_ref, bf16[112,768]{1,0:T(8,128)(2,1)S(1)} %get-tuple-element.22.keep_ref, bf16[112,768]{1,0:T(8,128)(2,1)S(1)} %collective-permute-done.3.came_ref), custom_call_target="tpu_custom_call" | custom-call | flops 786432 | bytes 3145728 | tf_op jit(solution)/shard_map/add_parts/pallas_call | solution.py:261
  72.8 6.1 %all-to-all-start.2 = ((bf16[16,48,1024]{2,1,0:T(8,128)(2,1)}), bf16[16,48,1024]{2,1,0:T(8,128)(2,1)S(1)}, u32[]{:S(2)}, u32[]{:S(2)}) async-start(bf16[16,48,1024]{2,1,0:T(8,128)(2,1)} %get-tuple-element.27), calls=%async_computation.2 | async-start | bytes 3145728 | tf_op jit(solution)/shard_map/all_to_all | solution.py:373
  78.9 1.2 collective-permute-start.4
  80.2 10.8 %collective-permute-done.4.other_ref = bf16[112,768]{1,0:T(8,128)(2,1)S(1)} collective-permute-done((bf16[112,768]{1,0:T(8,128)(2,1)S(1)}, bf16[112,768]{1,0:T(8,128)(2,1)S(1)}, u32[]{:S(2)}, u32[]{:S(2)}) %collective-permute-start.4) | collective-permute-done | bytes 172064 | tf_op jit(solution)/shard_map/ppermute | solution.py:374
  91.0 0.6 pair_grads.1.refs_0_
  91.5 0.8 collective-permute-start.7
  92.3 1.5 collective-permute-start.6
  93.8 0.0 collective-permute-start.5
  93.8 0.0 copy-start
  93.8 2.0 %copy-done = f32[896,1024]{1,0:T(8,128)S(1)} copy-done((f32[896,1024]{1,0:T(8,128)S(1)}, f32[896,1024]{1,0:T(8,128)}, u32[]{:S(2)}) %copy-start) | copy-done | bytes 3670040
  95.8 0.5 inverse_of.1.refs_4_.inverse_ref
  96.4 2.6 %collective-permute-done.7.refs_3_ = bf16[224,768]{1,0:T(8,128)(2,1)S(1)} collective-permute-done((bf16[224,768]{1,0:T(8,128)(2,1)S(1)}, bf16[224,768]{1,0:T(8,128)(2,1)S(1)}, u32[]{:S(2)}, u32[]{:S(2)}) %collective-permute-start.7) | collective-permute-done | bytes 344096 | tf_op jit(solution)/shard_map/ppermute | solution.py:365
  99.0 1.3 collective-permute-done.6.refs_2_
  100.3 10.3 %collective-permute-done.5.refs_1_ = bf16[224,768]{1,0:T(8,128)(2,1)S(1)} collective-permute-done((bf16[224,768]{1,0:T(8,128)(2,1)S(1)}, bf16[224,768]{1,0:T(8,128)(2,1)S(1)}, u32[]{:S(2)}, u32[]{:S(2)}) %collective-permute-start.5) | collective-permute-done | bytes 344096 | tf_op jit(solution)/shard_map/ppermute | solution.py:365
  110.7 0.7 join_grads.1
  111.3 0.0 copy-start.5
  111.3 1.1 copy-done.5
  112.4 0.0 copy-start.7
  112.4 0.8 copy-done.7
  113.2 1.9 %all-to-all-done.2 = bf16[16,48,1024]{2,1,0:T(8,128)(2,1)S(1)} async-done(((bf16[16,48,1024]{2,1,0:T(8,128)(2,1)}), bf16[16,48,1024]{2,1,0:T(8,128)(2,1)S(1)}, u32[]{:S(2)}, u32[]{:S(2)}) %all-to-all-start.2) | async-done | bytes 1572896 | tf_op jit(solution)/shard_map/all_to_all | solution.py:373
  115.1 0.0 copy-start.8
  115.1 0.0 copy-start.6
  115.1 0.1 query_rows.1
  115.2 2.6 %collective-permute-start.9 = (bf16[256,1024]{1,0:T(8,128)(2,1)S(1)}, bf16[256,1024]{1,0:T(8,128)(2,1)S(1)}, u32[]{:S(2)}, u32[]{:S(2)}) collective-permute-start(bf16[256,1024]{1,0:T(8,128)(2,1)S(1)} %query_rows.1), channel_id=1, source_target_pairs={{0,1},{1,0},{2,3},{3,2},{4,5},{5,4},{6,7},{7,6},{8,9},{9,8},{10,11... | collective-permute-start | bytes 1572872 | tf_op jit(solution)/shard_map/ppermute | solution.py:378
  117.8 0.0 copy-done.8
  117.8 0.9 collective-permute-start.8
  118.7 1.4 collective-permute-done.8.go_ref
  120.1 0.0 collective-permute-done.9.ao_ref
  120.1 0.0 copy-done.6
  120.1 6.8 %tile_scores.1 = f32[128,1,128]{2,1,0:T(1,128)S(1)} custom-call(s32[3]{0:T(128)S(1)} %copy-done.3, bf16[896,768]{1,0:T(8,128)(2,1)S(1)} %copy-done.6, bf16[896,256]{1,0:T(8,128)(2,1)S(1)} %collective-permute-done.8.go_ref, bf16[768,1024]{1,0:T(8,128)(2,1)S(1)} %bitcast.7, bf16[256,1024]{1,0:T(8,128)(2,1)S(1)} %collective-permute-done.9.ao_ref, ...), custom_call_target="tpu_custom_call" | custom-call | flops 3758096384 | bytes 8388608 | tf_op jit(solution)/shard_map/tile_scores/pallas_call | solution.py:345
  127.0 20.6 %all_to_all.20 = f32[128,1,128]{2,1,0:T(1,128)S(1)} all-to-all(f32[128,1,128]{2,1,0:T(1,128)S(1)} %tile_scores.1), channel_id=1, replica_groups=mesh['shard'=16,'dp'=8,'buffer'=2] {'shard','dp'}, dimensions={0} | all-to-all | bytes 131072 | tf_op jit(solution)/shard_map/all_to_all | solution.py:380
  147.5 0.2 reduce_sum.9
  147.7 0.7 reshape.19
Async XLA Ops:
  3.1 20.7 %all-to-all-start = ((bf16[8,96,512]{2,1,0:T(8,128)(2,1)}), bf16[8,96,512]{2,1,0:T(8,128)(2,1)S(1)}, u32[]{:S(2)}, u32[]{:S(2)}) async-start(bf16[8,96,512]{2,1,0:T(8,128)(2,1)} %pack_acts.1), calls=%async_computation | async-start | bytes 1572864 | tf_op jit(solution)/shard_map/all_to_all | solution.py:367
  10.6 13.2 %copy-start.1 = (bf16[1024,512]{1,0:T(8,128)(2,1)S(1)}, bf16[1024,512]{1,0:T(8,128)(2,1)}, u32[]{:S(2)}) copy-start(bf16[1024,512]{1,0:T(8,128)(2,1)} %basis_ref.3) | copy-start | bytes 3145732
  23.8 0.7 copy-start.4
  26.7 8.5 %copy-start.11 = (bf16[224,768]{1,0:T(8,128)(2,1)S(1)}, bf16[224,768]{1,0:T(8,128)(2,1)}, u32[]{:S(2)}) copy-start(bf16[224,768]{1,0:T(8,128)(2,1)} %get-tuple-element.19) | copy-start | bytes 1032196
  26.7 8.6 %copy-start.10 = (bf16[224,768]{1,0:T(8,128)(2,1)S(1)}, bf16[224,768]{1,0:T(8,128)(2,1)}, u32[]{:S(2)}) copy-start(bf16[224,768]{1,0:T(8,128)(2,1)} %get-tuple-element.20) | copy-start | bytes 1032196
  26.7 10.6 %copy-start.9 = (bf16[224,768]{1,0:T(8,128)(2,1)S(1)}, bf16[224,768]{1,0:T(8,128)(2,1)}, u32[]{:S(2)}) copy-start(bf16[224,768]{1,0:T(8,128)(2,1)} %get-tuple-element.21) | copy-start | bytes 1032196
  26.7 26.6 %copy-start.2 = (bf16[224,768]{1,0:T(8,128)(2,1)S(1)}, bf16[224,768]{1,0:T(8,128)(2,1)}, u32[]{:S(2)}) copy-start(bf16[224,768]{1,0:T(8,128)(2,1)} %get-tuple-element.18.refs_0_) | copy-start | bytes 1032196
  26.7 26.6 %copy-start.3 = (s32[3]{0:T(128)S(1)}, s32[3]{0:T(128)}, u32[]{:S(2)}) copy-start(s32[3]{0:T(128)} %pad_add_fusion.core_ref.where_ref) | copy-start | bytes 40
  26.7 44.6 %all-to-all-start.1 = ((bf16[16,48,1024]{2,1,0:T(8,128)(2,1)}), bf16[16,48,1024]{2,1,0:T(8,128)(2,1)S(1)}, u32[]{:S(2)}, u32[]{:S(2)}) async-start(bf16[16,48,1024]{2,1,0:T(8,128)(2,1)} %bitcast.3), calls=%async_computation.1 | async-start | bytes 3145728 | tf_op jit(solution)/shard_map/all_to_all | solution.py:370
  35.2 8.7 %collective-permute-start = (bf16[224,768]{1,0:T(8,128)(2,1)S(1)}, bf16[224,768]{1,0:T(8,128)(2,1)S(1)}, u32[]{:S(2)}, u32[]{:S(2)}) collective-permute-start(bf16[224,768]{1,0:T(8,128)(2,1)S(1)} %copy-done.11), channel_id=1, source_target_pairs={{0,4},{2,6},{4,8},{6,10},{8,12},{10,14},{12,0},{14,2},{1,5},{3,7},... | collective-permute-start | bytes 1032200 | tf_op jit(solution)/shard_map/ppermute | solution.py:365
  35.3 15.4 %collective-permute-start.1 = (bf16[224,768]{1,0:T(8,128)(2,1)S(1)}, bf16[224,768]{1,0:T(8,128)(2,1)S(1)}, u32[]{:S(2)}, u32[]{:S(2)}) collective-permute-start(bf16[224,768]{1,0:T(8,128)(2,1)S(1)} %copy-done.10), channel_id=1, source_target_pairs={{0,8},{2,10},{4,12},{6,14},{8,0},{10,2},{12,4},{14,6},{1,9},{3,11}... | collective-permute-start | bytes 1032200 | tf_op jit(solution)/shard_map/ppermute | solution.py:365
  37.3 16.0 %collective-permute-start.2 = (bf16[224,768]{1,0:T(8,128)(2,1)S(1)}, bf16[224,768]{1,0:T(8,128)(2,1)S(1)}, u32[]{:S(2)}, u32[]{:S(2)}) collective-permute-start(bf16[224,768]{1,0:T(8,128)(2,1)S(1)} %copy-done.9), channel_id=1, source_target_pairs={{0,12},{2,14},{4,0},{6,2},{8,4},{10,6},{12,8},{14,10},{1,13},{3,15... | collective-permute-start | bytes 1032200 | tf_op jit(solution)/shard_map/ppermute | solution.py:365
  54.2 11.0 %collective-permute-start.3 = (bf16[112,768]{1,0:T(8,128)(2,1)S(1)}, bf16[112,768]{1,0:T(8,128)(2,1)S(1)}, u32[]{:S(2)}, u32[]{:S(2)}) collective-permute-start(bf16[112,768]{1,0:T(8,128)(2,1)S(1)} %get-tuple-element.23), channel_id=1, source_target_pairs={{0,2},{2,0},{4,6},{6,4},{8,10},{10,8},{12,14},{14,12},{1,3},{3,1},... | collective-permute-start | bytes 516104 | tf_op jit(solution)/shard_map/ppermute | solution.py:372
  72.8 42.3 %all-to-all-start.2 = ((bf16[16,48,1024]{2,1,0:T(8,128)(2,1)}), bf16[16,48,1024]{2,1,0:T(8,128)(2,1)S(1)}, u32[]{:S(2)}, u32[]{:S(2)}) async-start(bf16[16,48,1024]{2,1,0:T(8,128)(2,1)} %get-tuple-element.27), calls=%async_computation.2 | async-start | bytes 3145728 | tf_op jit(solution)/shard_map/all_to_all | solution.py:373
  78.9 12.0 %collective-permute-start.4 = (bf16[112,768]{1,0:T(8,128)(2,1)S(1)}, bf16[112,768]{1,0:T(8,128)(2,1)S(1)}, u32[]{:S(2)}, u32[]{:S(2)}) collective-permute-start(bf16[112,768]{1,0:T(8,128)(2,1)S(1)} %get-tuple-element.24.own_ref), channel_id=1, source_target_pairs={{0,2},{2,0},{4,6},{6,4},{8,10},{10,8},{12,14},{14,12},{1,3},{3,1},... | collective-permute-start | bytes 516104 | tf_op jit(solution)/shard_map/ppermute | solution.py:374
  91.5 7.5 %collective-permute-start.7 = (bf16[224,768]{1,0:T(8,128)(2,1)S(1)}, bf16[224,768]{1,0:T(8,128)(2,1)S(1)}, u32[]{:S(2)}, u32[]{:S(2)}) collective-permute-start(bf16[224,768]{1,0:T(8,128)(2,1)S(1)} %pair_grads.1.refs_0_), channel_id=1, source_target_pairs={{0,12},{2,14},{4,0},{6,2},{8,4},{10,6},{12,8},{14,10},{1,13},{3,15... | collective-permute-start | bytes 1032200 | tf_op jit(solution)/shard_map/ppermute | solution.py:365
  92.3 8.0 %collective-permute-start.6 = (bf16[224,768]{1,0:T(8,128)(2,1)S(1)}, bf16[224,768]{1,0:T(8,128)(2,1)S(1)}, u32[]{:S(2)}, u32[]{:S(2)}) collective-permute-start(bf16[224,768]{1,0:T(8,128)(2,1)S(1)} %pair_grads.1.refs_0_), channel_id=1, source_target_pairs={{0,8},{2,10},{4,12},{6,14},{8,0},{10,2},{12,4},{14,6},{1,9},{3,11}... | collective-permute-start | bytes 1032200 | tf_op jit(solution)/shard_map/ppermute | solution.py:365
  93.8 16.9 %collective-permute-start.5 = (bf16[224,768]{1,0:T(8,128)(2,1)S(1)}, bf16[224,768]{1,0:T(8,128)(2,1)S(1)}, u32[]{:S(2)}, u32[]{:S(2)}) collective-permute-start(bf16[224,768]{1,0:T(8,128)(2,1)S(1)} %pair_grads.1.refs_0_), channel_id=1, source_target_pairs={{0,4},{2,6},{4,8},{6,10},{8,12},{10,14},{12,0},{14,2},{1,5},{3,7},... | collective-permute-start | bytes 1032200 | tf_op jit(solution)/shard_map/ppermute | solution.py:365
  93.8 2.0 %copy-start = (f32[896,1024]{1,0:T(8,128)S(1)}, f32[896,1024]{1,0:T(8,128)}, u32[]{:S(2)}) copy-start(f32[896,1024]{1,0:T(8,128)} %eig_ref.1) | copy-start | bytes 11010052
  111.3 1.1 copy-start.5
  112.4 0.8 copy-start.7
  115.1 2.7 %copy-start.8 = (bf16[896,256]{1,0:T(8,128)(2,1)S(1)}, bf16[896,256]{1,0:T(8,128)(2,1)}, u32[]{:S(2)}) copy-start(bf16[896,256]{1,0:T(8,128)(2,1)} %copy-done.7) | copy-start | bytes 1376260
  115.1 5.0 %copy-start.6 = (bf16[896,768]{1,0:T(8,128)(2,1)S(1)}, bf16[896,768]{1,0:T(8,128)(2,1)}, u32[]{:S(2)}) copy-start(bf16[896,768]{1,0:T(8,128)(2,1)} %copy-done.5) | copy-start | bytes 4128772
  115.2 4.9 %collective-permute-start.9 = (bf16[256,1024]{1,0:T(8,128)(2,1)S(1)}, bf16[256,1024]{1,0:T(8,128)(2,1)S(1)}, u32[]{:S(2)}, u32[]{:S(2)}) collective-permute-start(bf16[256,1024]{1,0:T(8,128)(2,1)S(1)} %query_rows.1), channel_id=1, source_target_pairs={{0,1},{1,0},{2,3},{3,2},{4,5},{5,4},{6,7},{7,6},{8,9},{9,8},{10,11... | collective-permute-start | bytes 1572872 | tf_op jit(solution)/shard_map/ppermute | solution.py:378
  117.8 2.3 %collective-permute-start.8 = (bf16[896,256]{1,0:T(8,128)(2,1)S(1)}, bf16[896,256]{1,0:T(8,128)(2,1)S(1)}, u32[]{:S(2)}, u32[]{:S(2)}) collective-permute-start(bf16[896,256]{1,0:T(8,128)(2,1)S(1)} %copy-done.8), channel_id=1, source_target_pairs={{0,1},{1,0},{2,3},{3,2},{4,5},{5,4},{6,7},{7,6},{8,9},{9,8},{10,11... | collective-permute-start | bytes 1376264 | tf_op jit(solution)/shard_map/ppermute | solution.py:377
